TPU v7x, 512 devices: a whole 4x8x8 slice. The times are simulated.
512 devices in a mesh: section: 64 (over x, y, z_lo), tp: 8 (over z_hi, core).
Axes of the slice: x: 4, y: 8, z: 8 (z_hi: 4, z_lo: 2; z = z_hi * 2 + z_lo), core: 2. Of those that a mesh axis runs over, the one named last changes fastest.
Arguments:
- queries: bfloat16 [8192, 128, 128], P('section', 'tp'), may hold values from -64 to 64
- key_heads: bfloat16 [8192, 8, 128], P('section', 'tp'), may hold values from -8 to 8
- values: bfloat16 [8192, 8, 128], P('section', 'tp'), may hold values from -6 to 6
- target: bfloat16 [8192, 128, 128], P('section', 'tp'), may hold values from -3 to 3
- map_q: float32 [128, 128, 64], P('tp'), may hold values from -1 to 1
- map_k: float32 [8, 128, 64], P('tp'), may hold values from -1 to 1
Outputs:
- grad_q: float32 [128, 128, 64], P('tp')
- grad_k: float32 [8, 128, 64], P('tp')
- distill_loss: float32 [], replicated
All inputs are finite; a program needn't handle non-finite values.
Results may differ from a plain program's by a relative error of at most 0.00048.
Values may be sent and summed in bfloat16 or wider, within the bound.
No kernel may reach another device: no remote copies, remote signals or barrier semaphores. Data moves between devices by JAX's collectives and lax.ppermute only.
A program may use at most 64 MiB of HBM per device.

v0:
```python
import math

import jax
import jax.numpy as jnp
from jax import lax
from jax.sharding import PartitionSpec as P

WIN = 128


HIGH = lax.Precision.HIGHEST


def from_behind(block, axis, distance):
    devices = range(lax.axis_size(axis))
    route = [(i - distance, i) for i in devices if i - distance in devices]
    return lax.ppermute(block, axis, route)


def carried_in(value, axis, join, neutral, backward):
    count, mine = (lax.axis_size(axis), lax.axis_index(axis))
    pieces = jax.tree.map(lambda part: lax.all_gather(part, axis), value)
    if backward:
        pieces = jax.tree.map(lambda part: part[::-1], pieces)
        mine = count - 1 - mine
    so_far = jax.tree.map(
        lambda part, zero: jnp.full_like(part, 0) + jnp.asarray(zero, part.dtype), value, neutral
    )

    def step(position, so_far):
        longer = join(so_far, jax.tree.map(lambda part: part[position], pieces))
        return jax.tree.map(lambda new, old: jnp.where(position < mine, new, old), longer, so_far)

    return lax.fori_loop(0, count - 1, step, so_far)


def features(projected):
    both = jnp.concatenate([projected, -projected], axis=-1)
    return jax.nn.softmax(both, axis=-1)


def add_pair(earlier, later):
    return (earlier[0] + later[0], earlier[1] + later[1])


def on_device(queries, key_heads, values, target, map_q, map_k):
    tokens, head_count, head_width = queries.shape
    blocks = tokens // WIN
    position = lax.axis_index("section")
    has_prev = (position > 0).astype(jnp.float32)
    count_all = float(
        tokens * head_count * head_width * lax.axis_size("section") * lax.axis_size("tp")
    )
    key_rows = key_heads[:, 0, :]
    value_rows = values[:, 0, :]
    halo_keys, halo_values = from_behind((key_rows, value_rows), "section", 1)
    value_float = value_rows.astype(jnp.float32)

    def block_states(weight_k):
        features_k = features(
            jnp.dot(key_rows.astype(jnp.float32), weight_k[0], precision=HIGH)
        ).reshape(blocks, WIN, -1)
        block_s = jnp.einsum(
            "blf,bld->bfd", features_k, value_float.reshape(blocks, WIN, head_width), precision=HIGH
        )
        return (block_s, features_k.sum(1))

    (sub_states, sub_totals), states_back = jax.vjp(block_states, map_k)
    own_state = (sub_states.sum(0), sub_totals.sum(0))
    zero_pair = (jnp.zeros_like(own_state[0]), jnp.zeros_like(own_state[1]))
    carried = carried_in(own_state, "section", add_pair, zero_pair, False)

    def student_error(weight_q, weight_k, carry_s, carry_z, block_s, block_z):
        query_feats = features(
            jnp.einsum("thd,hdf->thf", queries.astype(jnp.float32), weight_q, precision=HIGH)
        )
        halo_feats = features(jnp.dot(halo_keys.astype(jnp.float32), weight_k[0], precision=HIGH))
        halo_s = has_prev * jnp.dot(halo_feats.T, halo_values.astype(jnp.float32), precision=HIGH)
        halo_z = has_prev * halo_feats.sum(0)
        states = [carry_s - halo_s]
        totals = [carry_z - halo_z]
        far_state = jnp.stack(states)
        far_total = jnp.stack(totals)
        query_blk = queries.reshape(blocks, WIN, head_count, head_width)
        key_blk = key_rows.reshape(blocks, WIN, head_width)
        value_blk = value_rows.reshape(blocks, WIN, head_width)
        key_window = jnp.concatenate(
            [jnp.concatenate([halo_keys[None], key_blk[:-1]], axis=0), key_blk], axis=1
        )
        value_window = jnp.concatenate(
            [jnp.concatenate([halo_values[None], value_blk[:-1]], axis=0), value_blk], axis=1
        )
        scores = jnp.einsum(
            "bihd,bjd->bhij", query_blk, key_window, preferred_element_type=jnp.float32
        ) / math.sqrt(head_width)
        row_index = jnp.arange(WIN)[:, None]
        col_index = jnp.arange(2 * WIN)[None, :]
        block_index = jnp.arange(blocks)[:, None, None]
        previous_ok = (block_index > 0) | (position > 0)
        allowed = jnp.where(col_index < WIN, previous_ok, col_index - WIN <= row_index)
        scores = jnp.where(allowed[:, None], scores, -1e30)
        row_max = scores.max(-1)
        weights = jnp.exp(scores - row_max[..., None])
        window_total = weights.sum(-1)
        window_sum = jnp.einsum(
            "bhij,bjd->bihd",
            weights.astype(jnp.bfloat16),
            value_window,
            preferred_element_type=jnp.float32,
        )
        feats_blk = query_feats.reshape(blocks, WIN, head_count, -1)
        linear_sum = jnp.einsum("bihf,bfd->bihd", feats_blk, far_state, precision=HIGH)
        linear_total = jnp.einsum("bihf,bf->bih", feats_blk, far_total, precision=HIGH)
        far_scale = jnp.exp(-row_max).transpose(0, 2, 1)
        student = (window_sum + far_scale[..., None] * linear_sum) / (
            window_total.transpose(0, 2, 1) + far_scale * linear_total
        )[..., None]
        error = student - target.astype(jnp.float32).reshape(blocks, WIN, head_count, head_width)
        return jnp.sum(error * error) / count_all

    loss_local, student_back = jax.vjp(
        student_error, map_q, map_k, carried[0], carried[1], sub_states, sub_totals
    )
    grad_q, grad_k_local, grad_carry_s, grad_carry_z, grad_sub_s, grad_sub_z = student_back(
        jnp.ones((), jnp.float32)
    )
    later = carried_in((grad_carry_s, grad_carry_z), "section", add_pair, zero_pair, True)
    (grad_k_states,) = states_back((grad_sub_s + later[0][None], grad_sub_z + later[1][None]))
    grad_k = grad_k_local + grad_k_states
    grad_q, grad_k = lax.psum((grad_q, grad_k), "section")
    distill_loss = lax.psum(loss_local, ("section", "tp"))
    return (grad_q, grad_k, distill_loss)


def solution(mesh):
    in_specs = (
        P("section", "tp", None),
        P("section", "tp", None),
        P("section", "tp", None),
        P("section", "tp", None),
        P("tp", None, None),
        P("tp", None, None),
    )
    out_specs = (P("tp", None, None), P("tp", None, None), P())
    return jax.shard_map(
        on_device, mesh=mesh, in_specs=in_specs, out_specs=out_specs, check_vma=False
    )
```

profile of v0, /device:TPU:8, one launch (start us, length us, event | category | flops | bytes accessed | tf_op | source)
XLA Modules:
  0.0 1304.5 jit_solution(13688765366113609744)
XLA Ops:
  7.2 1.0 fusion.55
  8.4 1.6 fusion.31
  10.0 1.5 copy.22
  11.5 4.3 collective-permute-start.1
  15.8 2.6 collective-permute-start
  18.4 2.2 negate_reduce_fusion.2
  21.8 1.2 copy.28
  23.1 147.9 %all-gather.3 = f32[64,1,128]{2,1,0:T(1,128)S(1)} all-gather(f32[1,1,128]{2,1,0:T(1,128)S(1)} %bitcast.204), channel_id=3, replica_groups=mesh['section'=64,'tp'=8] {'section'}, dimensions={0}, use_global_device_ids=true | all-gather | bytes 33280 | tf_op jit(solution)/shard_map/all_gather | solution.py:22
  172.7 147.8 %all-gather.10.cloned.1.call-done = f32[8192,128]{1,0:T(8,128)} async-done(((f32[128,128]{1,0:T(8,128)}), f32[8192,128]{1,0:T(8,128)}) %all-gather.10.cloned.1.call-update) | async-done | bytes 4194320 | tf_op jit(solution)/shard_map/all_gather | solution.py:22
  320.5 57.2 %while.32 = (s32[]{:T(128)}, f32[128,128]{1,0:T(8,128)S(1)}, f32[128]{0:T(128)S(1)}, s32[]{:T(128)}, f32[64,128,128]{2,1,0:T(8,128)}, /*index=5*/f32[64,128]{1,0:T(8,128)S(1)}, s32[]{:T(128)}, s32[]{:T(128)}) while((s32[]{:T(128)}, f32[128,128]{1,0:T(8,128)S(1)}, f32[128]{0:T(128)S(1)}, s32[]{:T(128)}, f32[64,128,128]{2,1,0:T(8,128)}, ...), condition=%wide.region_9.10_spmd.clone, body=%wide.region_8.9_spmd.clone.sunk | while | flops 49540 | bytes 198267 | solution.py:34
  321.4 0.9 add_select_fusion.4
  322.3 0.9 add_select_fusion.4
  323.2 0.9 add_select_fusion.4
  324.2 0.9 add_select_fusion.4
  325.1 0.9 add_select_fusion.4
  326.0 0.9 add_select_fusion.4
  328.7 0.9 add_select_fusion.4
  329.6 0.9 add_select_fusion.4
  330.5 0.9 add_select_fusion.4
  331.4 0.9 add_select_fusion.4
  332.3 0.9 add_select_fusion.4
  333.2 0.9 add_select_fusion.4
  334.2 0.9 add_select_fusion.4
  335.1 0.9 add_select_fusion.4
  336.0 0.9 add_select_fusion.4
  336.9 0.9 add_select_fusion.4
  377.8 1.9 fusion.65
  380.0 1.2 fusion.2
  381.2 2.0 multiply_reduce_fusion
  383.2 1.0 copy-done.17
  384.2 1.4 convolution_bitcast_fusion.4
  387.1 99.1 %psum.23 = f32[]{:T(128)} all-reduce(f32[]{:T(128)S(6)} %div.166), channel_id=1, replica_groups=mesh['section'=64,'tp'=8] {'section','tp'}, use_global_device_ids=true, to_apply=%region_24.25 | all-reduce | flops 1 | bytes 8 | tf_op jit(solution)/shard_map/psum | solution.py:131
  486.2 0.9 fusion.64
  487.1 147.6 %all-gather.4 = f32[64,1,128]{2,1,0:T(1,128)S(1)} all-gather(f32[1,1,128]{2,1,0:T(1,128)S(1)} %bitcast.205), channel_id=4, replica_groups=mesh['section'=64,'tp'=8] {'section'}, dimensions={0}, use_global_device_ids=true | all-gather | bytes 33280 | tf_op jit(solution)/shard_map/all_gather | solution.py:22
  634.7 2.8 multiply_reduce_fusion.1
  638.0 1.4 convolution_bitcast_fusion.1
  639.5 51.2 %all-gather.8.cloned.1.call-done = f32[64,128,128]{2,1,0:T(8,128)} async-done(((f32[1,128,128]{2,1,0:T(8,128)}), f32[64,128,128]{2,1,0:T(8,128)}) %all-gather.8.cloned.1.call-update) | async-done | bytes 4194320 | tf_op jit(solution)/shard_map/all_gather | solution.py:22
  690.7 4.7 rev.6
  695.3 57.1 %while.33 = (s32[]{:T(128)}, f32[128,128]{1,0:T(8,128)S(1)}, f32[128]{0:T(128)S(1)}, s32[]{:T(128)}, f32[64,128,128]{2,1,0:T(8,128)}, /*index=5*/f32[64,128]{1,0:T(8,128)S(1)}, s32[]{:T(128)}, s32[]{:T(128)}) while((s32[]{:T(128)}, f32[128,128]{1,0:T(8,128)S(1)}, f32[128]{0:T(128)S(1)}, s32[]{:T(128)}, ...), condition=%wide.region_20.21_spmd.clone, body=%wide.region_19.20_spmd.clone.sunk | while | flops 49540 | bytes 198267 | solution.py:34
  705.3 0.9 add_select_fusion.5
  708.0 0.9 add_select_fusion.5
  708.9 0.9 add_select_fusion.5
  709.9 0.9 add_select_fusion.5
  711.7 0.9 add_select_fusion.5
  712.6 0.9 add_select_fusion.5
  718.0 0.9 add_select_fusion.5
  718.9 0.9 add_select_fusion.5
  720.7 0.9 add_select_fusion.5
  721.6 0.9 add_select_fusion.5
  728.0 0.9 add_select_fusion.5
  728.9 0.9 add_select_fusion.5
  730.7 0.9 add_select_fusion.5
  731.6 0.9 add_select_fusion.5
  737.1 0.9 add_select_fusion.5
  738.0 0.9 add_select_fusion.5
  739.8 0.9 add_select_fusion.5
  740.7 0.9 add_select_fusion.5
  747.0 0.9 add_select_fusion.5
  748.0 0.9 add_select_fusion.5
  749.8 0.9 add_select_fusion.5
  750.7 0.9 add_select_fusion.5
  753.1 303.5 %psum.22 = f32[1,128,64]{1,2,0:T(8,128)} all-reduce(f32[1,128,64]{1,2,0:T(8,128)S(1)} %fusion.8), channel_id=1, replica_groups=mesh['section'=64,'tp'=8] {'section'}, use_global_device_ids=true, to_apply=%region_22.23 | all-reduce | flops 8192 | bytes 65536 | tf_op jit(solution)/shard_map/psum | solution.py:130
  1056.5 239.6 %all-reduce.2.cloned.1.call-done = f32[16,128,64]{1,2,0:T(8,128)} async-done(((f32[16,128,64]{1,2,0:T(8,128)}), f32[16,128,64]{1,2,0:T(8,128)}) %all-reduce.2.cloned.1.call-update) | async-done | bytes 524304 | tf_op jit(solution)/shard_map/psum | solution.py:130
  1296.1 1.9 copy.70
  (296 shorter events, 83.6 us)
Async XLA Ops:
  7.2 11.2 copy-start
  7.2 14.7 %copy-start.4 = (bf16[128,16,128]{2,1,0:T(8,128)(2,1)S(1)}, bf16[128,16,128]{2,1,0:T(8,128)(2,1)}, u32[]{:S(2)}) copy-start(bf16[128,16,128]{2,1,0:T(8,128)(2,1)} %param.13) | copy-start | bytes 1572868
  7.2 313.3 %all-gather.10.cloned.1.call-start = ((), (), s32[]{:S(2)}) async-start(), calls=%async_computation.2 | async-start | bytes 4259840 | tf_op jit(solution)/shard_map/all_gather | solution.py:22
  10.0 680.7 %all-gather.8.cloned.1.call-start = ((), (), s32[]{:S(2)}) async-start(), calls=%async_computation.1 | async-start | bytes 4259840 | tf_op jit(solution)/shard_map/all_gather | solution.py:22
  11.5 368.2 %collective-permute-start.1 = (bf16[128,128]{0,1:T(8,128)(2,1)}, bf16[128,128]{0,1:T(8,128)(2,1)S(1)}, u32[]{:S(2)}, u32[]{:S(2)}) collective-permute-start(bf16[128,128]{0,1:T(8,128)(2,1)} %bitcast.9), channel_id=1, source_target_pairs={{0,8},{8,16},{16,24},{24,32},{32,40},{40,48},{48,56},{56,64},{64,7... | collective-permute-start | bytes 98312 | tf_op jit(solution)/shard_map/ppermute | solution.py:17
  15.8 155.3 %collective-permute-start = (bf16[128,128]{1,0:T(8,128)(2,1)}, bf16[128,128]{1,0:T(8,128)(2,1)S(1)}, u32[]{:S(2)}, u32[]{:S(2)}) collective-permute-start(bf16[128,128]{1,0:T(8,128)(2,1)} %bitcast.194), channel_id=1, source_target_pairs={{0,8},{8,16},{16,24},{24,32},{32,40},{40,48},{48,56},{56,64},{64,7... | collective-permute-start | bytes 98312 | tf_op jit(solution)/shard_map/ppermute | solution.py:17
  18.4 152.7 %copy-start.9 = (f32[1,128,64]{1,2,0:T(8,128)S(1)}, f32[1,128,64]{1,2,0:T(8,128)}, u32[]{:S(2)}) copy-start(f32[1,128,64]{1,2,0:T(8,128)} %param.15) | copy-start | bytes 98308
  18.4 153.6 %copy-start.7 = (bf16[128,1,128]{2,0,1:T(8,128)(2,1)S(1)}, bf16[128,1,128]{2,0,1:T(8,128)(2,1)}, u32[]{:S(2)}) copy-start(bf16[128,1,128]{2,0,1:T(8,128)(2,1)} %param.11) | copy-start | bytes 98308
  20.6 0.8 copy-start.1
  171.3 0.6 copy-start.10
  172.4 205.3 %copy-start.12 = (f32[128]{0:T(128)S(1)}, f32[128]{0:T(128)}, u32[]{:S(2)}) copy-start(f32[128]{0:T(128)} %fusion.60) | copy-start | bytes 1540
  377.7 1.9 copy-start.13
  377.8 2.0 copy-start.11
  377.8 2.2 copy-start.2
  379.9 1.3 copy-start.15
  380.0 1.3 copy-start.5
  383.2 1.0 copy-start.17
  384.2 101.9 %copy-start.3 = (f32[128,16,64]{0,2,1:T(8,128)S(1)}, f32[128,16,64]{0,2,1:T(8,128)}, u32[]{:S(2)}) copy-start(f32[128,16,64]{0,2,1:T(8,128)} %copy-done.1) | copy-start | bytes 1572868
  386.3 909.8 %all-reduce.2.cloned.1.call-start = ((), (), s32[]{:S(2)}) async-start(), calls=%async_computation | async-start | bytes 1048576 | tf_op jit(solution)/shard_map/psum | solution.py:130
  486.1 148.5 %copy-start.6 = (bf16[128,16,128]{0,2,1:T(8,128)(2,1)S(1)}, bf16[128,16,128]{0,2,1:T(8,128)(2,1)}, u32[]{:S(2)}) copy-start(bf16[128,16,128]{0,2,1:T(8,128)(2,1)} %copy.28) | copy-start | bytes 1572868
  486.2 148.5 %copy-start.14 = (f32[128]{0:T(128)S(1)}, f32[128]{0:T(128)}, u32[]{:S(2)}) copy-start(f32[128]{0:T(128)} %copy-done.13) | copy-start | bytes 1540
  486.2 148.5 %copy-start.16 = (f32[128,128,1]{1,0,2:T(8,128)S(1)}, f32[128,128,1]{1,0,2:T(8,128)}, u32[]{:S(2)}) copy-start(f32[128,128,1]{1,0,2:T(8,128)} %copy-done.15) | copy-start | bytes 196612
  639.5 113.0 %copy-start.8 = (bf16[128,1,128]{2,0,1:T(8,128)(2,1)S(1)}, bf16[128,1,128]{2,0,1:T(8,128)(2,1)}, u32[]{:S(2)}) copy-start(bf16[128,1,128]{2,0,1:T(8,128)(2,1)} %param.12) | copy-start | bytes 98308
Sparse Core Ops, SparseCore 0:
  10.1 310.3 all-gather.9
  386.4 304.1 all-gather.7
  694.2 601.8 all-reduce.1
where the time goes:
time: 1310 us; the launch traced here: 1300 us
  blocking collectives  698 us (53%)
  waiting for transfers between devices  439 us (34%)
  other arithmetic  113 us (9%)
  matrix products  18.1 us (1%)
  between operations  14.9 us (1%)
    psum x1, blocking collectives, on_device(): grad_q, grad_k = lax.psum((grad_q, grad_k), 'section')  303 us
    all_gather x2, blocking collectives, carried_in(): pieces = jax.tree.map(lambda part: lax.all_gather(part, axis), value)  296 us
    psum x1, waiting for transfers between devices, on_device(): grad_q, grad_k = lax.psum((grad_q, grad_k), 'section')  240 us
    all_gather x2, waiting for transfers between devices, carried_in(): pieces = jax.tree.map(lambda part: lax.all_gather(part, axis), value)  199 us
    select_n x252, other arithmetic, step(): jnp.where(position < mine, new, old)  111 us
    psum x1, blocking collectives, on_device(): distill_loss = lax.psum(loss_local, ('section', 'tp'))  99.1 us
  transfers between devices with their start and end apart: 5, of which 3 were waited for; matrix products, arithmetic and copies ran while one was open for 10% of the time, Pallas kernels for 0%

commit v1 on v0

v1 whole, which is shorter than its diff:
```python
import math

import jax
import jax.numpy as jnp
from jax import lax
from jax.sharding import PartitionSpec as P

WIN = 128

HIGH = lax.Precision.HIGHEST


def exchange(parts):
    return lax.all_to_all(parts, "section", 0, 0, tiled=True)


def features(projected):
    both = jnp.concatenate([projected, -projected], axis=-1)
    return jax.nn.softmax(both, axis=-1)


def pack_state(state, total, count):
    width = state.shape[-1]
    rows = state.reshape(count, -1, width)
    totals = total.reshape(count, 1, -1)
    totals = jnp.pad(totals, ((0, 0), (0, 0), (0, width - totals.shape[-1])))
    return jnp.concatenate([rows, totals], axis=1)


def unpack_state(parts, feats, width):
    count = parts.shape[0]
    per = feats // count
    state = parts[:, :per].reshape(feats, width)
    total = parts[:, per, :per].reshape(feats)
    return state, total


def on_device(queries, key_heads, values, target, map_q, map_k):
    tokens, head_count, width = queries.shape
    count = lax.axis_size("section")
    position = lax.axis_index("section")
    has_prev = position > 0
    tp_count = lax.axis_size("tp")
    count_all = float(tokens * head_count * width * count * tp_count)
    key_rows = key_heads[:, 0, :]
    value_rows = values[:, 0, :]
    halo = lax.ppermute(
        jnp.concatenate([key_rows, value_rows], axis=0),
        "section",
        [(i, i + 1) for i in range(count - 1)],
    )
    halo_keys, halo_values = halo[:tokens], halo[tokens:]
    value_float = value_rows.astype(jnp.float32)
    feats = 2 * map_q.shape[-1]

    def block_state(weight_k):
        feats_k = features(jnp.dot(key_rows.astype(jnp.float32), weight_k[0], precision=HIGH))
        return jnp.dot(feats_k.T, value_float, precision=HIGH), feats_k.sum(0)

    (own_s, own_z), state_back = jax.vjp(block_state, map_k)
    index = jnp.arange(count)
    before = (index[None, :] + 2 <= index[:, None]).astype(jnp.float32)

    gathered = exchange(pack_state(own_s, own_z, count))
    prefix = jnp.dot(before, gathered.reshape(count, -1), precision=HIGH)
    far_s, far_z = unpack_state(exchange(prefix.reshape(gathered.shape)), feats, width)

    def student_error(weight_q, far_state, far_total):
        query_feats = features(
            jnp.einsum("thd,hdf->htf", queries.astype(jnp.float32), weight_q, precision=HIGH)
        )
        key_window = jnp.concatenate([halo_keys, key_rows], axis=0)
        value_window = jnp.concatenate([halo_values, value_rows], axis=0)
        scores = jnp.einsum(
            "ihd,jd->hij", queries, key_window, preferred_element_type=jnp.float32
        ) / math.sqrt(width)
        row_index = jnp.arange(WIN)[:, None]
        col_index = jnp.arange(2 * WIN)[None, :]
        allowed = jnp.where(col_index < WIN, has_prev, col_index - WIN <= row_index)
        scores = jnp.where(allowed[None], scores, -1e30)
        row_max = scores.max(-1)
        weights = jnp.exp(scores - row_max[..., None])
        window_total = weights.sum(-1)
        window_sum = jnp.einsum(
            "hij,jd->hid",
            weights.astype(jnp.bfloat16),
            value_window,
            preferred_element_type=jnp.float32,
        )
        linear_sum = jnp.einsum("hif,fd->hid", query_feats, far_state, precision=HIGH)
        linear_total = jnp.einsum("hif,f->hi", query_feats, far_total, precision=HIGH)
        far_scale = jnp.exp(-row_max)
        student = (window_sum + far_scale[..., None] * linear_sum) / (
            window_total + far_scale * linear_total
        )[..., None]
        error = student - target.astype(jnp.float32).transpose(1, 0, 2)
        return jnp.sum(error * error) / count_all

    loss_local, (grad_q, grad_s, grad_z) = jax.value_and_grad(student_error, argnums=(0, 1, 2))(
        map_q, far_s, far_z
    )

    packed = pack_state(grad_s, grad_z, count)
    state_rows = packed.shape[1]
    packed = packed.at[:, -1, -1].set(loss_local)
    query_parts = grad_q.reshape(count, -1, width)
    parts = exchange(jnp.concatenate([packed, query_parts], axis=1))
    state_parts = parts[:, :state_rows]
    loss = state_parts[:, -1, -1].sum()
    suffix = jnp.dot(before.T, state_parts.reshape(count, -1), precision=HIGH)
    query_sum = parts[:, state_rows:].sum(0)
    back = exchange(
        jnp.concatenate(
            [
                suffix.reshape(state_parts.shape),
                jnp.broadcast_to(query_sum[None], (count,) + query_sum.shape),
            ],
            axis=1,
        )
    )
    later_s, later_z = unpack_state(back[:, :state_rows], feats, width)
    (grad_k,) = state_back((later_s, later_z))
    key_sum = exchange(grad_k.reshape(count, 1, -1)).sum(0)
    grad_k = exchange(jnp.broadcast_to(key_sum[None], (count,) + key_sum.shape))
    for bit in (1, 2, 4):
        loss = loss + lax.ppermute(loss, "tp", [(i, i ^ bit) for i in range(tp_count)])
    return back[:, state_rows:].reshape(map_q.shape), grad_k.reshape(map_k.shape), loss


def solution(mesh):
    in_specs = (
        P("section", "tp", None),
        P("section", "tp", None),
        P("section", "tp", None),
        P("section", "tp", None),
        P("tp", None, None),
        P("tp", None, None),
    )
    out_specs = (P("tp", None, None), P("tp", None, None), P())
    return jax.shard_map(
        on_device, mesh=mesh, in_specs=in_specs, out_specs=out_specs, check_vma=False
    )
```

time: 1310 us -> 177 us (0.14)
  the two profiles are of different devices: /device:TPU:8 before, /device:TPU:6 now
where the time goes in v1:
time: 177 us
  starting transfers between devices  59.7 us (34%)
  blocking collectives  41.8 us (24%)
  waiting for transfers between devices  28 us (16%)
  matrix products  17.1 us (10%)
  local copies, waits for them, and re-layouts  15.1 us (9%)
  other arithmetic  9.21 us (5%)
  between operations  5.68 us (3%)
    all_to_all x2, blocking collectives, exchange(): return lax.all_to_all(parts, 'section', 0, 0, tiled=True)  41.8 us
    all_to_all x4, starting transfers between devices, exchange(): return lax.all_to_all(parts, 'section', 0, 0, tiled=True)  37 us
    all_to_all x4, waiting for transfers between devices, exchange(): return lax.all_to_all(parts, 'section', 0, 0, tiled=True)  26.5 us
    ppermute x3, starting transfers between devices, on_device(): lax.ppermute(loss, 'tp', [(i, i ^ bit) for i in range(tp_count)])  19.3 us
    dot_general x3, matrix products, student_error(): jnp.einsum('hif,fd->hid', query_feats, far_state, precision=HIGH)  5.34 us
    scatter x1, local copies, waits for them, and re-layouts, on_device(): packed = packed.at[:, -1, -1].set(loss_local)  4.85 us
    unnamed x38, local copies, waits for them, and re-layouts  4.52 us
  transfers between devices with their start and end apart: 8, of which 5 were waited for; matrix products, arithmetic and copies ran while one was open for 8% of the time, Pallas kernels for 0%

profile of v1, /device:TPU:6, one launch (start us, length us, event | category | flops | bytes accessed | tf_op | source)
XLA Modules:
  0.0 176.6 jit_solution(17823766144822972323)
XLA Ops:
  0.6 1.0 negate_reduce_fusion
  1.8 0.1 fusion.51
  1.9 0.1 reshape.176
  2.0 0.3 copy-done.8
  2.3 0.9 fusion.30
  3.3 0.7 copy.49
  4.0 12.6 %all-to-all-start = ((f32[64,3,128]{2,1,0:T(4,128)}), f32[64,3,128]{2,1,0:T(4,128)S(1)}, u32[]{:S(2)}, u32[]{:S(2)}) async-start(f32[64,3,128]{2,1,0:T(4,128)} %copy.49), calls=%async_computation | async-start | bytes 262144 | tf_op jit(solution)/shard_map/all_to_all | solution.py:14
  16.6 0.8 pad_maximum_fusion.3
  17.4 3.4 %collective-permute-start = (bf16[256,128]{1,0:T(8,128)(2,1)S(1)}, bf16[256,128]{1,0:T(8,128)(2,1)S(1)}, u32[]{:S(2)}, u32[]{:S(2)}) collective-permute-start(bf16[256,128]{1,0:T(8,128)(2,1)S(1)} %pad_maximum_fusion.3), channel_id=1, source_target_pairs={{0,8},{8,16},{16,24},{24,32},{32,40},{40,48},{48,56},{56,64},{64,7... | collective-permute-start | bytes 196616 | tf_op jit(solution)/shard_map/ppermute | solution.py:47
  20.8 0.5 iota_compare_fusion.4
  21.3 0.6 iota_add_fusion
  21.9 2.2 %negate_reduce_fusion.1 = (f32[16,128]{1,0:T(8,128)S(1)}, f32[16,128]{1,0:T(8,128)S(1)}, f32[16,128,64]{1,2,0:T(8,128)S(1)}, f32[16,128,64]{1,2,0:T(8,128)S(1)}) fusion(f32[16,128,64]{1,2,0:T(8,128)S(1)} %copy-done, bf16[128,16,128]{2,1,0:T(8,128)(2,1)} %param.8), kind=kOutput, calls=%fused_computation.94 | convolution fusion | flops 201715712 | bytes 2113536 | tf_op jit(solution)/shard_map/jvp(thd,hdf->htf)/dot_general | solution.py:70
  24.1 0.2 fusion.16
  24.3 0.6 multiply_divide_fusion
  24.9 0.2 broadcast_divide_fusion
  25.0 2.2 %copy.55 = bf16[128,16,128]{0,2,1:T(8,128)(2,1)} copy(bf16[128,16,128]{2,1,0:T(8,128)(2,1)} %param.11) | data formatting | bytes 1048576 | tf_op args[3]
  27.2 0.8 fusion.15
  28.1 0.5 iota_add_fusion.1
  28.6 0.6 fusion.52
  29.2 1.8 %fusion.53 = (f32[16,128]{1,0:T(8,128)S(1)}, f32[16,128,256]{1,2,0:T(8,128)}) fusion(bf16[128,16,128]{2,1,0:T(8,128)(2,1)S(1)} %copy-done.2, bf16[128,128]{1,0:T(8,128)(2,1)S(1)} %bitcast.124, bf16[128,128]{1,0:T(8,128)(2,1)S(1)} %get-tuple-element.35, pred[128,256]{0,1:T(8,128)(4,1)S(1)} %fusion.15), kind=kOutput, calls=%fused_computation.97 | convolution fusion | flops 135919616 | bytes 2727936 | tf_op jit(solution)/shard_map/jvp(ihd,jd->hij)/dot_general | solution.py:74
  31.0 0.3 fusion.20
  31.3 0.7 copy.52
  32.1 10.3 %all-to-all-start.1 = ((f32[64,3,128]{2,1,0:T(4,128)}), f32[64,3,128]{2,1,0:T(4,128)S(1)}, u32[]{:S(2)}, u32[]{:S(2)}) async-start(f32[64,3,128]{2,1,0:T(4,128)} %copy.52), calls=%async_computation.1 | async-start | bytes 262144 | tf_op jit(solution)/shard_map/all_to_all | solution.py:14
  42.4 1.9 %fusion = f32[16,128]{1,0:T(8,128)S(1)} fusion(f32[16,128,256]{1,2,0:T(8,128)} %get-tuple-element.41, f32[16,128]{1,0:T(8,128)S(1)} %get-tuple-element.40), kind=kLoop, calls=%fused_computation.2 | loop fusion | flops 1046528 | bytes 2113536 | tf_op jit(solution)/shard_map/jvp()/reduce_sum | solution.py:83
  44.3 6.9 %all-to-all-done.1 = f32[64,3,128]{2,1,0:T(4,128)S(1)} async-done(((f32[64,3,128]{2,1,0:T(4,128)}), f32[64,3,128]{2,1,0:T(4,128)S(1)}, u32[]{:S(2)}, u32[]{:S(2)}) %all-to-all-start.1) | async-done | bytes 98336 | tf_op jit(solution)/shard_map/all_to_all | solution.py:14
  51.3 0.1 slice_reduce_fusion.3
  51.4 0.1 reshape.191
  51.5 0.7 reshape_squeeze.6
  52.2 0.6 fusion.54
  52.9 1.1 convolution_multiply_fusion
  54.0 2.3 %multiply_reduce_fusion.1 = (f32[]{:T(128)}, f32[16,128]{1,0:T(8,128)S(1)}, f32[16,128,128]{1,2,0:T(8,128)}) fusion(bf16[128,16,128]{0,2,1:T(8,128)(2,1)S(1)} %copy-done.4, f32[16,128]{1,0:T(8,128)S(1)} %get-tuple-element.28, f32[16,128]{1,0:T(8,128)S(1)} %get-tuple-element.27, f32[16,128,128]{1,2,0:T(8,128)S(1)} %convolution_multiply_fusion, ...), kind=kOutput, calls=%fused_computation.17 | convolution fusion | flops 138016768 | bytes 4816900 | tf_op jit(solution)/shard_map/jvp(hij,jd->hid)/dot_general | solution.py:84
  56.3 1.3 fusion.4
  57.6 0.1 copy.81
  57.8 2.7 %fusion.14 = f32[128,128,1]{1,0,2:T(8,128)S(1)} fusion(f32[16,128,128]{1,2,0:T(8,128)S(1)} %broadcast_divide_fusion, f32[16,128]{1,0:T(8,128)S(1)} %get-tuple-element.28, f32[16,128]{1,0:T(8,128)S(1)} %get-tuple-element.37, bf16[128,16,128]{0,2,1:T(8,128)(2,1)} %copy.55, f32[16,128,128]{1,2,0:T(8,128)} %get-tuple-element.42), kind=kOutput, calls=%fused_computation.32 | convolution fusion | flops 404488192 | bytes 2703360 | tf_op jit(solution)/shard_map/transpose(jvp(hif,fd->hid))/dot_general | solution.py:90
  60.5 1.6 multiply_reduce_fusion
  62.1 0.2 add_multiply_fusion
  62.3 0.6 convolution_bitcast_fusion
  62.9 0.3 copy.60
  63.3 0.2 reshape.181
  64.3 4.9 %scatter.4 = f32[64,3,128]{2,1,0:T(4,128)S(1)} dynamic-update-slice(f32[64,3,128]{2,1,0:T(4,128)S(1)} %select_maximum_fusion, f32[64,1,1]{2,1,0:T(1,128)S(1)} %broadcast.107, s32[]{:T(128)} %constant.58.clone.1, s32[]{:T(128)} %constant.52.clone.1, s32[]{:T(128)} %constant.64.clone.1) | dynamic-update-slice | bytes 516 | tf_op jit(solution)/shard_map/scatter | solution.py:105
  69.2 25.9 %all_to_all.30 = f32[64,19,128]{2,1,0:T(8,128)S(1)} all-to-all(f32[64,19,128]{2,1,0:T(8,128)S(1)} %pad_maximum_fusion), channel_id=1, replica_groups=mesh['section'=64,'tp'=8] {'section'}, dimensions={0} | all-to-all | bytes 1245184 | tf_op jit(solution)/shard_map/all_to_all | solution.py:14
  95.2 0.2 fusion.17
  95.7 1.0 pad_maximum_fusion.1
  96.6 7.6 %all-to-all-start.3 = ((f32[64,19,128]{2,1,0:T(8,128)}), f32[64,19,128]{2,1,0:T(8,128)S(1)}, u32[]{:S(2)}, u32[]{:S(2)}) async-start(f32[64,19,128]{2,1,0:T(8,128)} %pad_maximum_fusion.1), calls=%async_computation.3 | async-start | bytes 1572864 | tf_op jit(solution)/shard_map/all_to_all | solution.py:14
  104.3 19.5 %all-to-all-done.3 = f32[64,19,128]{2,1,0:T(8,128)S(1)} async-done(((f32[64,19,128]{2,1,0:T(8,128)}), f32[64,19,128]{2,1,0:T(8,128)S(1)}, u32[]{:S(2)}, u32[]{:S(2)}) %all-to-all-start.3) | async-done | bytes 622624 | tf_op jit(solution)/shard_map/all_to_all | solution.py:14
  123.8 0.1 slice_reduce_fusion.2
  123.9 0.1 reshape_squeeze.7
  124.1 0.2 fusion.29
  124.3 0.2 convolution_bitcast_fusion.1
  124.7 15.8 %all_to_all.31 = f32[64,1,128]{2,1,0:T(1,128)S(1)} all-to-all(f32[64,1,128]{2,1,0:T(1,128)S(1)} %bitcast.134), channel_id=1, replica_groups=mesh['section'=64,'tp'=8] {'section'}, dimensions={0} | all-to-all | bytes 65536 | tf_op jit(solution)/shard_map/all_to_all | solution.py:14
  140.6 0.6 broadcast_in_dim.79
  141.2 6.5 %all-to-all-start.5 = ((f32[64,1,128]{2,1,0:T(1,128)}), f32[64,1,128]{2,1,0:T(1,128)S(1)}, u32[]{:S(2)}, u32[]{:S(2)}) async-start(f32[64,1,128]{2,1,0:T(1,128)} %broadcast_in_dim.79), calls=%async_computation.5 | async-start | bytes 65536 | tf_op jit(solution)/shard_map/all_to_all | solution.py:14
  147.7 0.7 slice_reduce_fusion.1
  148.5 1.9 %collective-permute-start.1 = (f32[]{:T(128)}, f32[]{:T(128)}, u32[]{:S(2)}, u32[]{:S(2)}) collective-permute-start(f32[]{:T(128)} %slice_reduce_fusion.1), channel_id=1, source_target_pairs={{0,1},{1,0},{2,3},{3,2},{4,5},{5,4},{6,7},{7,6},{8,9},{9,8},{10,11... | collective-permute-start | bytes 20 | tf_op jit(solution)/shard_map/ppermute | solution.py:126
  150.4 1.2 collective-permute-done.1
  152.9 7.4 %collective-permute-start.2 = (f32[]{:T(128)}, f32[]{:T(128)}, u32[]{:S(2)}, u32[]{:S(2)}) collective-permute-start(f32[]{:T(128)} %add.45), channel_id=1, source_target_pairs={{0,2},{1,3},{2,0},{3,1},{4,6},{5,7},{6,4},{7,5},{8,10},{9,11},{10,... | collective-permute-start | bytes 20 | tf_op jit(solution)/shard_map/ppermute | solution.py:126
  160.3 0.2 collective-permute-done.2
  161.2 10.0 %collective-permute-start.3 = (f32[]{:T(128)}, f32[]{:T(128)}, u32[]{:S(2)}, u32[]{:S(2)}) collective-permute-start(f32[]{:T(128)} %add.46), channel_id=1, source_target_pairs={{0,4},{1,5},{2,6},{3,7},{4,0},{5,1},{6,2},{7,3},{8,12},{9,13},{10,... | collective-permute-start | bytes 20 | tf_op jit(solution)/shard_map/ppermute | solution.py:126
  171.2 0.2 collective-permute-done.3
  172.1 0.2 reshape.183
  172.3 1.1 copy.65
  173.5 0.5 broadcast.131
  174.0 0.7 reduce.21
  174.8 0.7 copy.66
  (60 shorter events, 1.1 us)
Async XLA Ops:
  0.6 21.2 %copy-start = (f32[16,128,64]{1,2,0:T(8,128)S(1)}, f32[16,128,64]{1,2,0:T(8,128)}, u32[]{:S(2)}) copy-start(f32[16,128,64]{1,2,0:T(8,128)} %param.12) | copy-start | bytes 1572868
  1.7 0.6 copy-start.8
  1.8 0.6 copy-start.11
  4.0 27.0 %all-to-all-start = ((f32[64,3,128]{2,1,0:T(4,128)}), f32[64,3,128]{2,1,0:T(4,128)S(1)}, u32[]{:S(2)}, u32[]{:S(2)}) async-start(f32[64,3,128]{2,1,0:T(4,128)} %copy.49), calls=%async_computation | async-start | bytes 262144 | tf_op jit(solution)/shard_map/all_to_all | solution.py:14
  17.4 11.2 %collective-permute-start = (bf16[256,128]{1,0:T(8,128)(2,1)S(1)}, bf16[256,128]{1,0:T(8,128)(2,1)S(1)}, u32[]{:S(2)}, u32[]{:S(2)}) collective-permute-start(bf16[256,128]{1,0:T(8,128)(2,1)S(1)} %pad_maximum_fusion.3), channel_id=1, source_target_pairs={{0,8},{8,16},{16,24},{24,32},{32,40},{40,48},{48,56},{56,64},{64,7... | collective-permute-start | bytes 196616 | tf_op jit(solution)/shard_map/ppermute | solution.py:47
  24.1 5.1 %copy-start.2 = (bf16[128,16,128]{2,1,0:T(8,128)(2,1)S(1)}, bf16[128,16,128]{2,1,0:T(8,128)(2,1)}, u32[]{:S(2)}) copy-start(bf16[128,16,128]{2,1,0:T(8,128)(2,1)} %param.8) | copy-start | bytes 1572868
  24.1 5.1 %copy-start.3 = (bf16[128,1,128]{2,0,1:T(8,128)(2,1)S(1)}, bf16[128,1,128]{2,0,1:T(8,128)(2,1)}, u32[]{:S(2)}) copy-start(bf16[128,1,128]{2,0,1:T(8,128)(2,1)} %param.9) | copy-start | bytes 98308
  28.6 2.5 %copy-start.13 = (s32[64]{0:T(128)S(1)}, s32[64]{0:T(128)}, u32[]{:S(2)}) copy-start(s32[64]{0:T(128)} %iota_add_fusion.1) | copy-start | bytes 772
  32.1 19.2 %all-to-all-start.1 = ((f32[64,3,128]{2,1,0:T(4,128)}), f32[64,3,128]{2,1,0:T(4,128)S(1)}, u32[]{:S(2)}, u32[]{:S(2)}) async-start(f32[64,3,128]{2,1,0:T(4,128)} %copy.52), calls=%async_computation.1 | async-start | bytes 262144 | tf_op jit(solution)/shard_map/all_to_all | solution.py:14
  44.3 9.7 %copy-start.6 = (bf16[128,1,128]{2,0,1:T(8,128)(2,1)S(1)}, bf16[128,1,128]{2,0,1:T(8,128)(2,1)}, u32[]{:S(2)}) copy-start(bf16[128,1,128]{2,0,1:T(8,128)(2,1)} %param.10) | copy-start | bytes 98308
  44.3 9.7 %copy-start.7 = (bf16[128,128]{1,0:T(8,128)(2,1)S(1)}, bf16[128,128]{1,0:T(8,128)(2,1)}, u32[]{:S(2)}) copy-start(bf16[128,128]{1,0:T(8,128)(2,1)} %get-tuple-element.34) | copy-start | bytes 98308
  52.2 1.8 %copy-start.1 = (f32[16,128,256]{1,2,0:T(8,128)S(1)}, f32[16,128,256]{1,2,0:T(8,128)}, u32[]{:S(2)}) copy-start(f32[16,128,256]{1,2,0:T(8,128)} %get-tuple-element.41) | copy-start | bytes 6291460
  52.2 1.8 %copy-start.4 = (bf16[128,16,128]{0,2,1:T(8,128)(2,1)S(1)}, bf16[128,16,128]{0,2,1:T(8,128)(2,1)}, u32[]{:S(2)}) copy-start(bf16[128,16,128]{0,2,1:T(8,128)(2,1)} %copy.55) | copy-start | bytes 1572868
  57.7 2.8 %copy-start.5 = (bf16[128,16,128]{0,2,1:T(8,128)(2,1)S(1)}, bf16[128,16,128]{0,2,1:T(8,128)(2,1)}, u32[]{:S(2)}) copy-start(bf16[128,16,128]{0,2,1:T(8,128)(2,1)} %copy.55) | copy-start | bytes 1572868
  57.7 2.8 %copy-start.10 = (f32[16,128]{1,0:T(8,128)S(1)}, f32[16,128]{1,0:T(8,128)}, u32[]{:S(2)}) copy-start(f32[16,128]{1,0:T(8,128)} %multiply_divide_fusion) | copy-start | bytes 24580
  57.7 2.8 %copy-start.15 = (f32[128]{0:T(128)S(1)}, f32[128]{0:T(128)}, u32[]{:S(2)}) copy-start(f32[128]{0:T(128)} %reshape_squeeze.6) | copy-start | bytes 1540
  57.8 2.8 %copy-start.16 = (f32[16,128,128]{1,2,0:T(8,128)S(1)}, f32[16,128,128]{1,2,0:T(8,128)}, u32[]{:S(2)}) copy-start(f32[16,128,128]{1,2,0:T(8,128)} %get-tuple-element.42) | copy-start | bytes 3145732
  63.5 31.7 %copy-start.14 = (s32[64]{0:T(128)S(1)}, s32[64]{0:T(128)}, u32[]{:S(2)}) copy-start(s32[64]{0:T(128)} %iota_add_fusion.1) | copy-start | bytes 772
  95.5 8.7 %copy-start.12 = (f32[128]{0:T(128)S(1)}, f32[128]{0:T(128)}, u32[]{:S(2)}) copy-start(f32[128]{0:T(128)} %copy-done.11) | copy-start | bytes 1540
  95.5 28.5 %copy-start.9 = (f32[128]{0:T(128)S(1)}, f32[128]{0:T(128)}, u32[]{:S(2)}) copy-start(f32[128]{0:T(128)} %copy-done.8) | copy-start | bytes 1540
  96.6 27.1 %all-to-all-start.3 = ((f32[64,19,128]{2,1,0:T(8,128)}), f32[64,19,128]{2,1,0:T(8,128)S(1)}, u32[]{:S(2)}, u32[]{:S(2)}) async-start(f32[64,19,128]{2,1,0:T(8,128)} %pad_maximum_fusion.1), calls=%async_computation.3 | async-start | bytes 1572864 | tf_op jit(solution)/shard_map/all_to_all | solution.py:14
  141.2 32.3 %all-to-all-start.5 = ((f32[64,1,128]{2,1,0:T(1,128)}), f32[64,1,128]{2,1,0:T(1,128)S(1)}, u32[]{:S(2)}, u32[]{:S(2)}) async-start(f32[64,1,128]{2,1,0:T(1,128)} %broadcast_in_dim.79), calls=%async_computation.5 | async-start | bytes 65536 | tf_op jit(solution)/shard_map/all_to_all | solution.py:14
  148.5 3.1 %collective-permute-start.1 = (f32[]{:T(128)}, f32[]{:T(128)}, u32[]{:S(2)}, u32[]{:S(2)}) collective-permute-start(f32[]{:T(128)} %slice_reduce_fusion.1), channel_id=1, source_target_pairs={{0,1},{1,0},{2,3},{3,2},{4,5},{5,4},{6,7},{7,6},{8,9},{9,8},{10,11... | collective-permute-start | bytes 20 | tf_op jit(solution)/shard_map/ppermute | solution.py:126
  152.9 7.6 %collective-permute-start.2 = (f32[]{:T(128)}, f32[]{:T(128)}, u32[]{:S(2)}, u32[]{:S(2)}) collective-permute-start(f32[]{:T(128)} %add.45), channel_id=1, source_target_pairs={{0,2},{1,3},{2,0},{3,1},{4,6},{5,7},{6,4},{7,5},{8,10},{9,11},{10,... | collective-permute-start | bytes 20 | tf_op jit(solution)/shard_map/ppermute | solution.py:126
  161.2 10.2 %collective-permute-start.3 = (f32[]{:T(128)}, f32[]{:T(128)}, u32[]{:S(2)}, u32[]{:S(2)}) collective-permute-start(f32[]{:T(128)} %add.46), channel_id=1, source_target_pairs={{0,4},{1,5},{2,6},{3,7},{4,0},{5,1},{6,2},{7,3},{8,12},{9,13},{10,... | collective-permute-start | bytes 20 | tf_op jit(solution)/shard_map/ppermute | solution.py:126

commit v2 on v1

v2 whole, which is shorter than its diff:
```python
import math

import jax
import jax.numpy as jnp
from jax import lax
from jax.sharding import PartitionSpec as P

WIN = 128

HIGH = lax.Precision.HIGHEST


def exchange(parts, axis="section"):
    return lax.all_to_all(parts, axis, 0, 0, tiled=True)


def spread(part, count):
    return jnp.broadcast_to(part[None], (count,) + part.shape)


def features(projected):
    both = jnp.concatenate([projected, -projected], axis=-1)
    return jax.nn.softmax(both, axis=-1)


def features_back(feats, grad):
    half = feats.shape[-1] // 2
    inner = feats * (grad - (feats * grad).sum(-1, keepdims=True))
    return inner[..., :half] - inner[..., half:]


def pack_state(state, total, count):
    width = state.shape[-1]
    rows = state.reshape(count, -1, width)
    totals = total.reshape(count, 1, -1)
    totals = jnp.pad(totals, ((0, 0), (0, 0), (0, width - totals.shape[-1])))
    return jnp.concatenate([rows, totals], axis=1)


def unpack_state(parts, feats, width):
    per = feats // parts.shape[0]
    state = parts[:, :per].reshape(feats, width)
    total = parts[:, per, :per].reshape(feats)
    return state, total


def on_device(queries, key_heads, values, target, map_q, map_k):
    tokens, head_count, width = queries.shape
    count = lax.axis_size("section")
    position = lax.axis_index("section")
    tp_count = lax.axis_size("tp")
    count_all = float(tokens * head_count * width * count * tp_count)
    key_rows = key_heads[:, 0, :]
    value_rows = values[:, 0, :]
    key_float = key_rows.astype(jnp.float32)
    value_float = value_rows.astype(jnp.float32)
    feats = 2 * map_q.shape[-1]
    index = jnp.arange(count)
    before = (index[None, :] + 2 <= index[:, None]).astype(jnp.float32)

    with jax.named_scope("own_state"):
        key_feats = features(jnp.dot(key_float, map_k[0], precision=HIGH))
        own_s = jnp.dot(key_feats.T, value_float, precision=HIGH)
        packed = pack_state(own_s, key_feats.sum(0), count)
    with jax.named_scope("states_out"):
        gathered = exchange(packed)
    halo = lax.ppermute(
        jnp.concatenate([key_rows, value_rows], axis=0),
        "section",
        [(i, i + 1) for i in range(count - 1)],
    )
    with jax.named_scope("query_feats"):
        query_heads = queries.transpose(1, 0, 2)
        query_feats = features(
            jnp.einsum("htd,hdf->htf", query_heads.astype(jnp.float32), map_q, precision=HIGH)
        )
        target_float = target.transpose(1, 0, 2).astype(jnp.float32)
    with jax.named_scope("prefix"):
        prefix = jnp.dot(before, gathered.reshape(count, -1), precision=HIGH)
        prefix, halo, query_feats, target_float = lax.optimization_barrier(
            (prefix, halo, query_feats, target_float)
        )
    with jax.named_scope("states_back"):
        returned = exchange(prefix.reshape(packed.shape))

    with jax.named_scope("window"):
        key_window = jnp.concatenate([halo[:tokens], key_rows], axis=0)
        value_window = jnp.concatenate([halo[tokens:], value_rows], axis=0)
        scores = jnp.einsum(
            "hid,jd->hij", query_heads, key_window, preferred_element_type=jnp.float32
        ) / math.sqrt(width)
        row_index = jnp.arange(WIN)[:, None]
        col_index = jnp.arange(2 * WIN)[None, :]
        allowed = jnp.where(col_index < WIN, position > 0, col_index - WIN <= row_index)
        scores = jnp.where(allowed[None], scores, -1e30)
        row_max = scores.max(-1)
        weights = jnp.exp(scores - row_max[..., None])
        window_total = weights.sum(-1)
        window_sum = jnp.einsum(
            "hij,jd->hid",
            weights.astype(jnp.bfloat16),
            value_window,
            preferred_element_type=jnp.float32,
        )
        far_scale = jnp.exp(-row_max)
        returned, window_sum, window_total, far_scale = lax.optimization_barrier(
            (returned, window_sum, window_total, far_scale)
        )

    with jax.named_scope("student"):
        far_state, far_total = unpack_state(returned, feats, width)
        linear_sum = jnp.einsum("hif,fd->hid", query_feats, far_state, precision=HIGH)
        linear_total = jnp.einsum("hif,f->hi", query_feats, far_total, precision=HIGH)
        divisor = window_total + far_scale * linear_total
        student = (window_sum + far_scale[..., None] * linear_sum) / divisor[..., None]
        error = student - target_float
        loss_local = jnp.sum(error * error) / count_all
        scale = far_scale * (2.0 / count_all) / divisor
        grad_sum = error * scale[..., None]
        grad_total = -(grad_sum * student).sum(-1)
        grad_s = jnp.einsum("hif,hid->fd", query_feats, grad_sum, precision=HIGH)
        grad_z = jnp.einsum("hif,hi->f", query_feats, grad_total, precision=HIGH)
        packed = pack_state(grad_s, grad_z, count)
    with jax.named_scope("grads_out"):
        gathered = exchange(packed)
    with jax.named_scope("loss_tp"):
        loss_tp = loss_local
        for bit in (1, 2, 4):
            other = lax.ppermute(loss_tp, "tp", [(i, i ^ bit) for i in range(tp_count)])
            loss_tp = loss_tp + other
        loss_rows = jnp.broadcast_to(loss_tp, (count, 1, width))

    with jax.named_scope("grad_q"):
        grad_feats = (
            jnp.einsum("hid,fd->hif", grad_sum, far_state, precision=HIGH)
            + grad_total[..., None] * far_total
        )
        grad_proj = features_back(query_feats, grad_feats)
        grad_q = jnp.einsum(
            "htd,htf->hfd", query_heads.astype(jnp.float32), grad_proj, precision=HIGH
        )
    with jax.named_scope("suffix"):
        suffix = jnp.dot(before.T, gathered.reshape(count, -1), precision=HIGH)
    with jax.named_scope("grads_back"):
        later_s, later_z = unpack_state(exchange(suffix.reshape(packed.shape)), feats, width)
    with jax.named_scope("grad_k"):
        grad_feats = jnp.dot(value_float, later_s.T, precision=HIGH) + later_z
        grad_k = jnp.dot(features_back(key_feats, grad_feats).T, key_float, precision=HIGH)
    with jax.named_scope("maps_out"):
        parts = jnp.concatenate(
            [grad_q.reshape(count, -1, width), grad_k.reshape(count, 1, -1), loss_rows], axis=1
        )
        sums = exchange(parts).sum(0)
        loss = sums[-1, 0]
    with jax.named_scope("maps_back"):
        maps = exchange(spread(sums[:-1], count))
        grad_q = maps[:, :-1].reshape(head_count, -1, width).transpose(0, 2, 1)
        grad_k = maps[:, -1].reshape(-1, width).T
    return grad_q, grad_k[None], loss


def solution(mesh):
    in_specs = (
        P("section", "tp", None),
        P("section", "tp", None),
        P("section", "tp", None),
        P("section", "tp", None),
        P("tp", None, None),
        P("tp", None, None),
    )
    out_specs = (P("tp", None, None), P("tp", None, None), P())
    return jax.shard_map(
        on_device, mesh=mesh, in_specs=in_specs, out_specs=out_specs, check_vma=False
    )
```

time: 177 us -> 174 us (0.983)
  blocking collectives: 41.8 us -> 30.5 us
  local copies, waits for them, and re-layouts: 15.1 us -> 7.52 us
  matrix products: 17.1 us -> 23.8 us
  starting transfers between devices: 59.7 us -> 66.3 us
  waiting for transfers between devices: 28 us -> 33.7 us
  other arithmetic: 9.21 us -> 6.68 us
  between operations: 5.68 us -> 3.72 us
    all_to_all x2 -> x1, blocking collectives: 41.8 us -> 30.5 us  [exchange(): return lax.all_to_all(parts, axis, 0, 0, tiled=True)]
    dot_general x14, matrix products: 16.8 us -> 23.5 us  [the longest x1 5.32 us: on_device(): jnp.einsum('hif,fd->hid', query_feats, far_state, precision=HIGH)]
    all_to_all x4 -> x5, waiting for transfers between devices: 26.5 us -> 32.5 us  [exchange(): return lax.all_to_all(parts, axis, 0, 0, tiled=True)]
    all_to_all x4 -> x5, starting transfers between devices: 37 us -> 42.8 us  [exchange(): return lax.all_to_all(parts, axis, 0, 0, tiled=True)]
    scatter x1 -> x0, local copies, waits for them, and re-layouts: 4.85 us -> none  [on_device(): packed = packed.at[:, -1, -1].set(loss_local)]
    unnamed x38 -> x18, local copies, waits for them, and re-layouts: 4.52 us -> 0.05 us
    slice x3 -> x4, local copies, waits for them, and re-layouts: 0.69 us -> 3.37 us  [the longest x1 1.39 us: on_device(): value_window = jnp.concatenate([halo[tokens:], value_rows], axis=0)]
    reduce_sum x5 -> x3, other arithmetic: 2.91 us -> 0.51 us  [the longest x1 0.31 us: on_device(): window_total = weights.sum(-1)]
  transfers between devices with their start and end apart: 8 -> 9, of which waited for: 5 -> 6; matrix products, arithmetic and copies ran while one was open for 8% -> 12% of each run, Pallas kernels for 0% -> 0%
where the time goes in v2:
time: 174 us; the launch traced here: 172 us
  starting transfers between devices  66.3 us (38%)
  waiting for transfers between devices  33.7 us (19%)
  blocking collectives  30.5 us (18%)
  matrix products  23.8 us (14%)
  local copies, waits for them, and re-layouts  7.52 us (4%)
  other arithmetic  6.68 us (4%)
  between operations  3.72 us (2%)
    all_to_all x5, starting transfers between devices, exchange(): return lax.all_to_all(parts, axis, 0, 0, tiled=True)  42.8 us
    all_to_all x5, waiting for transfers between devices, exchange(): return lax.all_to_all(parts, axis, 0, 0, tiled=True)  32.5 us
    all_to_all x1, blocking collectives, exchange(): return lax.all_to_all(parts, axis, 0, 0, tiled=True)  30.5 us
    ppermute x3, starting transfers between devices, on_device(): other = lax.ppermute(loss_tp, 'tp', [(i, i ^ bit) for i in range(tp_count)])  20.1 us
    dot_general x1, matrix products, on_device(): jnp.einsum('hif,fd->hid', query_feats, far_state, precision=HIGH)  5.32 us
  transfers between devices with their start and end apart: 9, of which 6 were waited for; matrix products, arithmetic and copies ran while one was open for 12% of the time, Pallas kernels for 0%

profile of v2, /device:TPU:6, one launch (start us, length us, event | category | flops | bytes accessed | tf_op | source)
XLA Modules:
  0.0 172.3 jit_solution(618952149614120213)
XLA Ops:
  0.6 0.0 copy-start
  0.7 1.1 negate_reduce_fusion
  1.8 0.1 fusion.59
  1.9 0.1 reshape.117
  2.0 0.9 fusion.38
  3.0 0.7 copy.37
  3.7 12.6 %all-to-all-start = ((f32[64,3,128]{2,1,0:T(4,128)}), f32[64,3,128]{2,1,0:T(4,128)S(1)}, u32[]{:S(2)}, u32[]{:S(2)}) async-start(f32[64,3,128]{2,1,0:T(4,128)} %copy.37), calls=%async_computation | async-start | bytes 262144 | tf_op jit(solution)/shard_map/states_out/all_to_all | solution.py:14
  16.3 1.4 pad_maximum_fusion.2
  17.7 3.4 %collective-permute-start = (bf16[256,128]{1,0:T(8,128)(2,1)}, bf16[256,128]{1,0:T(8,128)(2,1)}, u32[]{:S(2)}, u32[]{:S(2)}) collective-permute-start(bf16[256,128]{1,0:T(8,128)(2,1)} %pad_maximum_fusion.2), channel_id=1, source_target_pairs={{0,8},{8,16},{16,24},{24,32},{32,40},{40,48},{48,56},{56,64},{64,7... | collective-permute-start | bytes 196616 | tf_op jit(solution)/shard_map/ppermute | solution.py:67
  21.1 0.0 copy-start.7
  21.2 1.2 convert_bitcast_fusion
  22.4 2.1 %negate_reduce_fusion.1 = (f32[16,128]{1,0:T(8,128)S(1)}, f32[16,128]{1,0:T(8,128)S(1)}, f32[16,128,64]{1,2,0:T(8,128)}, f32[16,128,64]{1,2,0:T(8,128)}) fusion(f32[16,128,64]{1,2,0:T(8,128)S(1)} %copy-done, bf16[16,128,128]{2,0,1:T(8,128)(2,1)S(1)} %bitcast.100), kind=kOutput, calls=%fused_computation.89 | convolution fusion | flops 201715712 | bytes 2113536 | tf_op jit(solution)/shard_map/query_feats/htd,hdf->htf/dot_general | solution.py:75
  24.5 1.4 fusion.3
  25.9 0.0 copy-start.5
  25.9 0.1 fusion.25
  26.0 0.0 all-to-all-done
  26.0 0.0 copy-done.7
  26.1 0.3 fusion.26
  26.4 0.9 collective-permute-done
  27.2 1.4 fusion.62
  28.6 0.0 copy-done.6
  28.6 1.8 %fusion.63 = (f32[16,128]{1,0:T(8,128)S(1)}, f32[16,128,256]{1,2,0:T(8,128)}) fusion(bf16[16,128,128]{2,0,1:T(8,128)(2,1)S(1)} %bitcast.101, bf16[128,128]{1,0:T(8,128)(2,1)S(1)} %bitcast.108, bf16[128,128]{1,0:T(8,128)(2,1)S(1)} %get-tuple-element.33, pred[128,256]{0,1:T(8,128)(4,1)S(1)} %fusion.25), kind=kOutput, calls=%fused_computation.95 | convolution fusion | flops 135919616 | bytes 2727936 | tf_op jit(solution)/shard_map/window/hid,jd->hij/dot_general | solution.py:89
  30.4 0.7 reshape.119
  31.1 9.5 %all-to-all-start.1 = ((f32[64,3,128]{2,1,0:T(4,128)}), f32[64,3,128]{2,1,0:T(4,128)S(1)}, u32[]{:S(2)}, u32[]{:S(2)}) async-start(f32[64,3,128]{2,1,0:T(4,128)} %reshape.119), calls=%async_computation.1 | async-start | bytes 262144 | tf_op jit(solution)/shard_map/states_back/all_to_all | solution.py:14
  40.7 3.3 %fusion.7 = f32[16,128,128]{2,1,0:T(8,128)} fusion(f32[16,128,256]{1,2,0:T(8,128)} %get-tuple-element.38, f32[16,128]{1,0:T(8,128)S(1)} %get-tuple-element.37, bf16[128,128]{1,0:T(8,128)(2,1)S(1)} %bitcast.106, bf16[128,128]{1,0:T(8,128)(2,1)} %get-tuple-element.32), kind=kOutput, calls=%fused_computation.13 | convolution fusion | flops 135397376 | bytes 3219456 | tf_op jit(solution)/shard_map/window/hij,jd->hid/dot_general | solution.py:99
  43.9 0.3 fusion.1
  44.2 5.3 %all-to-all-done.1 = f32[64,3,128]{2,1,0:T(4,128)S(1)} async-done(((f32[64,3,128]{2,1,0:T(4,128)}), f32[64,3,128]{2,1,0:T(4,128)S(1)}, u32[]{:S(2)}, u32[]{:S(2)}) %all-to-all-start.1) | async-done | bytes 98336 | tf_op jit(solution)/shard_map/states_back/all_to_all | solution.py:14
  49.5 0.1 fusion.61
  49.6 0.1 reshape.132
  49.8 0.7 fusion.64
  50.4 5.3 %multiply_reduce_fusion = (f32[]{:T(128)}, f32[16,128]{1,0:T(8,128)S(1)}, f32[16,128,128]{2,1,0:T(8,128)}) fusion(f32[16,128,128]{2,1,0:T(8,128)S(1)} %convert_bitcast_fusion, f32[16,128]{1,0:T(8,128)S(1)} %get-tuple-element.25, f32[16,128]{1,0:T(8,128)S(1)} %get-tuple-element.26, f32[16,128,128]{2,1,0:T(8,128)} %fusion.7, f32[16,128,128]{1,2,0:T(8,128)S(1)} %fusion.3, ...), kind=kOutput, calls=%fused_computation.17 | convolution fusion | flops 405010432 | bytes 4292612 | tf_op jit(solution)/shard_map/student/hif,fd->hid/dot_general | solution.py:112
  56.4 2.7 %collective-permute-start.1 = (f32[]{:T(128)}, f32[]{:T(128)}, u32[]{:S(2)}, u32[]{:S(2)}) collective-permute-start(f32[]{:T(128)} %div.48), channel_id=1, source_target_pairs={{0,1},{1,0},{2,3},{3,2},{4,5},{5,4},{6,7},{7,6},{8,9},{9,8},{10,11... | collective-permute-start | bytes 20 | tf_op jit(solution)/shard_map/loss_tp/ppermute | solution.py:129
  59.1 0.1 squeeze.23
  59.3 2.7 %fusion.11 = f32[128,128,1]{1,0,2:T(8,128)S(1)} fusion(f32[16,128,128]{1,2,0:T(8,128)S(1)} %fusion.3, f32[16,128]{1,0:T(8,128)S(1)} %get-tuple-element.25, f32[16,128,128]{2,1,0:T(8,128)} %get-tuple-element.39, f32[16,128,128]{2,1,0:T(8,128)S(1)} %convert_bitcast_fusion), kind=kOutput, calls=%fused_computation.22 | convolution fusion | flops 403177472 | bytes 3219456 | tf_op jit(solution)/shard_map/student/hif,hid->fd/dot_general | solution.py:121
  62.0 2.4 %multiply_reduce_fusion.1 = (f32[16,128]{1,0:T(8,128)S(1)}, f32[16,128,128]{1,2,0:T(8,128)}) fusion(f32[16,128,128]{1,2,0:T(8,128)S(1)} %fusion.3, f32[128]{0:T(128)S(1)} %squeeze.23, f32[16,128]{1,0:T(8,128)S(1)} %neg.19, f32[128,128,1]{1,0,2:T(8,128)S(1)} %bitcast.113, f32[16,128]{1,0:T(8,128)S(1)} %get-tuple-element.25, ...), kind=kOutput, calls=%fused_computation.19 | convolution fusion | flops 404224000 | bytes 4284928 | tf_op jit(solution)/shard_map/grad_q/hid,fd->hif/dot_general | solution.py:135
  64.3 0.9 convolution_bitcast_fusion
  65.3 0.1 reshape.123
  65.4 0.7 pad_maximum_fusion
  66.2 6.7 %all-to-all-start.2 = ((f32[64,3,128]{2,1,0:T(4,128)}), f32[64,3,128]{2,1,0:T(4,128)S(1)}, u32[]{:S(2)}, u32[]{:S(2)}) async-start(f32[64,3,128]{2,1,0:T(4,128)} %pad_maximum_fusion), calls=%async_computation.2 | async-start | bytes 262144 | tf_op jit(solution)/shard_map/grads_out/all_to_all | solution.py:14
  72.8 1.1 subtract_multiply_fusion
  74.0 8.6 %all-to-all-done.2 = f32[64,3,128]{2,1,0:T(4,128)S(1)} async-done(((f32[64,3,128]{2,1,0:T(4,128)}), f32[64,3,128]{2,1,0:T(4,128)S(1)}, u32[]{:S(2)}, u32[]{:S(2)}) %all-to-all-start.2) | async-done | bytes 98336 | tf_op jit(solution)/shard_map/grads_out/all_to_all | solution.py:14
  82.5 0.2 fusion.29
  82.8 0.7 copy.48
  83.5 6.5 %all-to-all-start.3 = ((f32[64,3,128]{2,1,0:T(4,128)}), f32[64,3,128]{2,1,0:T(4,128)S(1)}, u32[]{:S(2)}, u32[]{:S(2)}) async-start(f32[64,3,128]{2,1,0:T(4,128)} %copy.48), calls=%async_computation.3 | async-start | bytes 262144 | tf_op jit(solution)/shard_map/grads_back/all_to_all | solution.py:14
  90.0 1.8 %fusion.16 = f32[16,64,128]{2,1,0:T(8,128)S(1)} fusion(f32[16,128,128]{1,2,0:T(8,128)} %subtract_multiply_fusion, bf16[16,128,128]{2,0,1:T(8,128)(2,1)S(1)} %bitcast.102), kind=kOutput, calls=%fused_computation.28 | convolution fusion | flops 201457664 | bytes 2097152 | tf_op jit(solution)/shard_map/grad_q/htd,htf->hfd/dot_general | solution.py:139
  92.5 7.4 %collective-permute-start.2 = (f32[]{:T(128)}, f32[]{:T(128)}, u32[]{:S(2)}, u32[]{:S(2)}) collective-permute-start(f32[]{:T(128)} %add.63), channel_id=1, source_target_pairs={{0,2},{1,3},{2,0},{3,1},{4,6},{5,7},{6,4},{7,5},{8,10},{9,11},{10,... | collective-permute-start | bytes 20 | tf_op jit(solution)/shard_map/loss_tp/ppermute | solution.py:129
  99.9 0.2 collective-permute-done.2
  100.8 10.0 %collective-permute-start.3 = (f32[]{:T(128)}, f32[]{:T(128)}, u32[]{:S(2)}, u32[]{:S(2)}) collective-permute-start(f32[]{:T(128)} %add.64), channel_id=1, source_target_pairs={{0,4},{1,5},{2,6},{3,7},{4,0},{5,1},{6,2},{7,3},{8,12},{9,13},{10,... | collective-permute-start | bytes 20 | tf_op jit(solution)/shard_map/loss_tp/ppermute | solution.py:129
  110.8 0.2 collective-permute-done.3
  111.7 0.1 pad.11.clone
  111.8 0.0 all-to-all-done.3
  111.8 0.1 slice_reduce_fusion
  111.9 0.1 add.59
  112.0 0.2 multiply_reduce_fusion.3
  112.3 0.2 fusion.42
  112.4 0.1 maximum_maximum_fusion
  112.6 30.5 %all_to_all.30 = f32[64,18,128]{2,1,0:T(8,128)S(1)} all-to-all(f32[64,18,128]{2,1,0:T(8,128)S(1)} %maximum_maximum_fusion), channel_id=1, replica_groups=mesh['section'=64,'tp'=8] {'section'}, dimensions={0} | all-to-all | bytes 1179648 | tf_op jit(solution)/shard_map/maps_out/all_to_all | solution.py:14
  143.0 0.1 reduce_sum.89
  143.1 0.9 broadcast_in_dim.35
  144.0 7.6 %all-to-all-start.5 = ((f32[64,17,128]{2,1,0:T(8,128)}), f32[64,17,128]{2,1,0:T(8,128)S(1)}, u32[]{:S(2)}, u32[]{:S(2)}) async-start(f32[64,17,128]{2,1,0:T(8,128)} %broadcast_in_dim.35), calls=%async_computation.5 | async-start | bytes 1572864 | tf_op jit(solution)/shard_map/maps_back/all_to_all | solution.py:14
  151.6 0.5 slice.65
  152.1 18.7 %all-to-all-done.5 = f32[64,17,128]{2,1,0:T(8,128)S(1)} async-done(((f32[64,17,128]{2,1,0:T(8,128)}), f32[64,17,128]{2,1,0:T(8,128)S(1)}, u32[]{:S(2)}, u32[]{:S(2)}) %all-to-all-start.5) | async-done | bytes 557088 | tf_op jit(solution)/shard_map/maps_back/all_to_all | solution.py:14
  170.8 0.8 slice.63
  171.6 0.6 slice.64
  (28 shorter events, 0.2 us)
Async XLA Ops:
  0.6 21.7 %copy-start = (f32[16,128,64]{1,2,0:T(8,128)S(1)}, f32[16,128,64]{1,2,0:T(8,128)}, u32[]{:S(2)}) copy-start(f32[16,128,64]{1,2,0:T(8,128)} %param.10) | copy-start | bytes 1572868
  0.6 21.7 %copy-start.2 = (bf16[128,16,128]{2,1,0:T(8,128)(2,1)S(1)}, bf16[128,16,128]{2,1,0:T(8,128)(2,1)}, u32[]{:S(2)}) copy-start(bf16[128,16,128]{2,1,0:T(8,128)(2,1)} %param.6) | copy-start | bytes 1572868
  3.7 22.3 %all-to-all-start = ((f32[64,3,128]{2,1,0:T(4,128)}), f32[64,3,128]{2,1,0:T(4,128)S(1)}, u32[]{:S(2)}, u32[]{:S(2)}) async-start(f32[64,3,128]{2,1,0:T(4,128)} %copy.37), calls=%async_computation | async-start | bytes 262144 | tf_op jit(solution)/shard_map/states_out/all_to_all | solution.py:14
  17.7 9.5 %collective-permute-start = (bf16[256,128]{1,0:T(8,128)(2,1)}, bf16[256,128]{1,0:T(8,128)(2,1)}, u32[]{:S(2)}, u32[]{:S(2)}) collective-permute-start(bf16[256,128]{1,0:T(8,128)(2,1)} %pad_maximum_fusion.2), channel_id=1, source_target_pairs={{0,8},{8,16},{16,24},{24,32},{32,40},{40,48},{48,56},{56,64},{64,7... | collective-permute-start | bytes 196616 | tf_op jit(solution)/shard_map/ppermute | solution.py:67
  21.1 4.9 %copy-start.7 = (s32[64]{0:T(128)}, s32[64]{0:T(128)S(1)}, u32[]{:S(2)}) copy-start(s32[64]{0:T(128)S(1)} %iota_add_fusion.1) | copy-start | bytes 772
  24.5 4.2 %copy-start.6 = (bf16[128,1,128]{2,0,1:T(8,128)(2,1)S(1)}, bf16[128,1,128]{2,0,1:T(8,128)(2,1)}, u32[]{:S(2)}) copy-start(bf16[128,1,128]{2,0,1:T(8,128)(2,1)} %param.7) | copy-start | bytes 98308
  25.9 14.8 %copy-start.5 = (bf16[128,1,128]{2,0,1:T(8,128)(2,1)S(1)}, bf16[128,1,128]{2,0,1:T(8,128)(2,1)}, u32[]{:S(2)}) copy-start(bf16[128,1,128]{2,0,1:T(8,128)(2,1)} %param.8) | copy-start | bytes 98308
  31.1 18.4 %all-to-all-start.1 = ((f32[64,3,128]{2,1,0:T(4,128)}), f32[64,3,128]{2,1,0:T(4,128)S(1)}, u32[]{:S(2)}, u32[]{:S(2)}) async-start(f32[64,3,128]{2,1,0:T(4,128)} %reshape.119), calls=%async_computation.1 | async-start | bytes 262144 | tf_op jit(solution)/shard_map/states_back/all_to_all | solution.py:14
  40.6 3.3 %copy-start.1 = (f32[16,128,256]{1,2,0:T(8,128)S(1)}, f32[16,128,256]{1,2,0:T(8,128)}, u32[]{:S(2)}) copy-start(f32[16,128,256]{1,2,0:T(8,128)} %get-tuple-element.38) | copy-start | bytes 6291460
  56.4 35.4 %collective-permute-start.1 = (f32[]{:T(128)}, f32[]{:T(128)}, u32[]{:S(2)}, u32[]{:S(2)}) collective-permute-start(f32[]{:T(128)} %div.48), channel_id=1, source_target_pairs={{0,1},{1,0},{2,3},{3,2},{4,5},{5,4},{6,7},{7,6},{8,9},{9,8},{10,11... | collective-permute-start | bytes 20 | tf_op jit(solution)/shard_map/loss_tp/ppermute | solution.py:129
  59.3 2.7 %copy-start.3 = (f32[16,128,128]{2,1,0:T(8,128)S(1)}, f32[16,128,128]{2,1,0:T(8,128)}, u32[]{:S(2)}) copy-start(f32[16,128,128]{2,1,0:T(8,128)} %get-tuple-element.39) | copy-start | bytes 3145732
  64.3 8.5 %copy-start.4 = (f32[16,128,128]{1,2,0:T(8,128)S(1)}, f32[16,128,128]{1,2,0:T(8,128)}, u32[]{:S(2)}) copy-start(f32[16,128,128]{1,2,0:T(8,128)} %get-tuple-element.43) | copy-start | bytes 3145732
  65.3 17.3 %copy-start.8 = (s32[64]{0:T(128)S(1)}, s32[64]{0:T(128)}, u32[]{:S(2)}) copy-start(s32[64]{0:T(128)} %copy-done.7) | copy-start | bytes 772
  66.2 16.4 %all-to-all-start.2 = ((f32[64,3,128]{2,1,0:T(4,128)}), f32[64,3,128]{2,1,0:T(4,128)S(1)}, u32[]{:S(2)}, u32[]{:S(2)}) async-start(f32[64,3,128]{2,1,0:T(4,128)} %pad_maximum_fusion), calls=%async_computation.2 | async-start | bytes 262144 | tf_op jit(solution)/shard_map/grads_out/all_to_all | solution.py:14
  83.5 28.3 %all-to-all-start.3 = ((f32[64,3,128]{2,1,0:T(4,128)}), f32[64,3,128]{2,1,0:T(4,128)S(1)}, u32[]{:S(2)}, u32[]{:S(2)}) async-start(f32[64,3,128]{2,1,0:T(4,128)} %copy.48), calls=%async_computation.3 | async-start | bytes 262144 | tf_op jit(solution)/shard_map/grads_back/all_to_all | solution.py:14
  92.5 7.5 %collective-permute-start.2 = (f32[]{:T(128)}, f32[]{:T(128)}, u32[]{:S(2)}, u32[]{:S(2)}) collective-permute-start(f32[]{:T(128)} %add.63), channel_id=1, source_target_pairs={{0,2},{1,3},{2,0},{3,1},{4,6},{5,7},{6,4},{7,5},{8,10},{9,11},{10,... | collective-permute-start | bytes 20 | tf_op jit(solution)/shard_map/loss_tp/ppermute | solution.py:129
  100.8 10.2 %collective-permute-start.3 = (f32[]{:T(128)}, f32[]{:T(128)}, u32[]{:S(2)}, u32[]{:S(2)}) collective-permute-start(f32[]{:T(128)} %add.64), channel_id=1, source_target_pairs={{0,4},{1,5},{2,6},{3,7},{4,0},{5,1},{6,2},{7,3},{8,12},{9,13},{10,... | collective-permute-start | bytes 20 | tf_op jit(solution)/shard_map/loss_tp/ppermute | solution.py:129
  144.0 26.8 %all-to-all-start.5 = ((f32[64,17,128]{2,1,0:T(8,128)}), f32[64,17,128]{2,1,0:T(8,128)S(1)}, u32[]{:S(2)}, u32[]{:S(2)}) async-start(f32[64,17,128]{2,1,0:T(8,128)} %broadcast_in_dim.35), calls=%async_computation.5 | async-start | bytes 1572864 | tf_op jit(solution)/shard_map/maps_back/all_to_all | solution.py:14

commit v3 on v2

v3 whole, which is shorter than its diff:
```python
import math

import jax
import jax.numpy as jnp
from jax import lax
from jax.experimental import pallas as pl
from jax.experimental.pallas import tpu as pltpu
from jax.sharding import PartitionSpec as P

NN = (((1,), (0,)), ((), ()))
NT = (((1,), (1,)), ((), ()))
LIMIT = 40 * 1024 * 1024
STEPS = 4
PAIR = 256


def exchange(parts, axis="section"):
    return lax.all_to_all(parts, axis, 0, 0, tiled=True)


def mxu(a, b, dims=NN):
    return lax.dot_general(a, b, dims, preferred_element_type=jnp.float32)


def split(x, terms=2):
    out = []
    for _ in range(terms - 1):
        high = x.astype(jnp.bfloat16)
        out.append(high)
        x = x - high.astype(jnp.float32)
    out.append(x.astype(jnp.bfloat16))
    return out


def mxu3(a, b, dims=NN):
    return mxu(a[0], b[0], dims) + (mxu(a[0], b[1], dims) + mxu(a[1], b[0], dims))


def features_t(weight, rows):
    both = jnp.concatenate([weight, -weight], axis=0)
    proj = sum(mxu(term, rows, NT) for term in reversed(split(both, 3)))
    half = proj.shape[0] // 2
    top = jnp.max(jnp.abs(proj[:half]), axis=0, keepdims=True)
    raised = jnp.exp(proj - top)
    return raised * (1.0 / jnp.sum(raised, axis=0, keepdims=True))


def features_back_t(feats, grad):
    return feats * (grad - jnp.sum(feats * grad, axis=0, keepdims=True))


def put_state(ref, state, total):
    half = state.shape[0] // 2
    lane = lax.broadcasted_iota(jnp.int32, (half, state.shape[1]), 1)
    ref[:, 0, :] = state[:half]
    ref[:, 1, :] = state[half:]
    ref[:, 2, :] = jnp.where(lane < half, total[:half], total[half:])


def get_state(ref):
    state = jnp.concatenate([ref[:, 0, :], ref[:, 1, :]], axis=0)
    totals = ref[:, 2, :]
    half, width = totals.shape
    total = jnp.concatenate(
        [
            jnp.broadcast_to(totals[:, :1], (half, width)),
            jnp.broadcast_to(totals[:, half : half + 1], (half, width)),
        ],
        axis=0,
    )
    return state, total


def key_kernel(key_ref, value_ref, map_ref, parts_ref, feats_ref):
    feats = features_t(map_ref[0], key_ref[...])
    feats_ref[...] = feats
    state = sum(mxu(term, value_ref[...]) for term in reversed(split(feats)))
    total = jnp.broadcast_to(jnp.sum(feats, axis=1, keepdims=True), state.shape)
    put_state(parts_ref, state, total)


def running_kernel(backward, parts_ref, out_ref):
    count = parts_ref.shape[0]
    row = lax.broadcasted_iota(jnp.int32, (count, count), 0)
    col = lax.broadcasted_iota(jnp.int32, (count, count), 1)
    wanted = (row + 2 <= col) if backward else (col + 2 <= row)
    chosen = jnp.where(wanted, 1.0, 0.0).astype(jnp.bfloat16)
    for k in range(parts_ref.shape[1]):
        terms = split(parts_ref[:, k, :], 3)
        out_ref[:, k, :] = sum(mxu(chosen, term) for term in reversed(terms))


def query_kernel(query_ref, map_ref, high_ref, low_ref):
    tokens = query_ref.shape[0] // map_ref.shape[0]
    for h in range(map_ref.shape[0]):
        here = slice(h * tokens, (h + 1) * tokens)
        high_ref[:, here], low_ref[:, here] = split(features_t(map_ref[h], query_ref[here, :]))


def window_kernel(
    query_ref, key_ref, value_ref, halo_ref, target_ref, sum_ref, scale_ref, target_t_ref
):
    tokens, width = key_ref.shape
    has_prev = lax.axis_index("section") > 0
    row = lax.broadcasted_iota(jnp.int32, (tokens, PAIR), 0)
    col = lax.broadcasted_iota(jnp.int32, (tokens, PAIR), 1)
    earlier = row <= lax.rem(col, tokens)
    root = 1.0 / math.sqrt(width)
    halo_keys = halo_ref[:tokens]
    halo_values_t = halo_ref[tokens:].astype(jnp.float32).T.astype(jnp.bfloat16)
    values_t = value_ref[...].astype(jnp.float32).T.astype(jnp.bfloat16)
    for k in range(query_ref.shape[0] // PAIR):
        here = slice(k * PAIR, (k + 1) * PAIR)
        query = query_ref[here, :]
        before = jnp.where(has_prev, mxu(halo_keys, query, NT) * root, -1e30)
        own = jnp.where(earlier, mxu(key_ref[...], query, NT) * root, -1e30)
        top = jnp.max(jnp.maximum(before, own), axis=0, keepdims=True)
        before = jnp.exp(before - top)
        own = jnp.exp(own - top)
        inverse = 1.0 / jnp.sum(before + own, axis=0, keepdims=True)
        total = mxu(halo_values_t, before.astype(jnp.bfloat16)) + mxu(
            values_t, own.astype(jnp.bfloat16)
        )
        sum_ref[:, here] = total * inverse
        scale_ref[:, here] = jnp.exp(-top) * inverse
        target_t_ref[:, here] = target_ref[here, :].astype(jnp.float32).T.astype(jnp.bfloat16)


def student_kernel(
    factor,
    high_ref,
    low_ref,
    sum_ref,
    scale_ref,
    target_ref,
    state_ref,
    parts_ref,
    loss_ref,
    grad_high_ref,
    grad_low_ref,
    grad_total_ref,
    state_high,
    state_low,
    total_acc,
    grad_acc,
    grad_total_acc,
    loss_acc,
):
    step = pl.program_id(0)

    @pl.when(step == 0)
    def _():
        state, total = get_state(state_ref)
        state_high[...], state_low[...] = split(state.T)
        total_acc[...] = total
        grad_acc[...] = jnp.zeros_like(grad_acc)
        grad_total_acc[...] = jnp.zeros_like(grad_total_acc)
        loss_acc[...] = jnp.zeros_like(loss_acc)

    state = (state_high[...], state_low[...])
    total = jnp.concatenate([total_acc[...]] * (PAIR // total_acc.shape[1]), axis=1)
    for k in range(sum_ref.shape[1] // PAIR):
        here = slice(k * PAIR, (k + 1) * PAIR)
        pair = (high_ref[:, here], low_ref[:, here])
        feats = pair[0].astype(jnp.float32) + pair[1].astype(jnp.float32)
        scale = scale_ref[:, here]
        linear_total = jnp.sum(feats * total, axis=0, keepdims=True)
        inverse = 1.0 / (1.0 + scale * linear_total)
        student = (sum_ref[:, here] + scale * mxu3(state, pair)) * inverse
        error = student - target_ref[:, here].astype(jnp.float32)
        loss_acc[...] += error * error
        grad_sum = error * (scale * inverse * factor)
        grad_total = -jnp.sum(grad_sum * student, axis=0, keepdims=True)
        grads = split(grad_sum)
        grad_high_ref[:, here], grad_low_ref[:, here] = grads
        grad_total_ref[:, here] = grad_total
        grad_acc[...] += mxu3(pair, grads, NT)
        grad_total_acc[...] += feats * grad_total

    @pl.when(step == pl.num_programs(0) - 1)
    def _():
        grad = grad_acc[...]
        grad_total = jnp.sum(grad_total_acc[...], axis=1, keepdims=True)
        put_state(parts_ref, grad, jnp.broadcast_to(grad_total, grad.shape))
        loss_ref[...] = jnp.full(loss_ref.shape, jnp.sum(loss_acc[...]) * (0.5 * factor))


def grad_q_kernel(
    high_ref, low_ref, grad_high_ref, grad_low_ref, grad_total_ref, query_ref, state_ref, out_ref
):
    state, total = get_state(state_ref)
    total = jnp.concatenate([total] * (PAIR // total.shape[1]), axis=1)
    state = split(state)
    heads, half, _ = out_ref.shape
    tokens = query_ref.shape[0] // heads
    for k in range(query_ref.shape[0] // PAIR):
        here = slice(k * PAIR, (k + 1) * PAIR)
        grad = mxu3(state, (grad_high_ref[:, here], grad_low_ref[:, here]))
        grad = grad + total * grad_total_ref[:, here]
        feats = high_ref[:, here].astype(jnp.float32) + low_ref[:, here].astype(jnp.float32)
        inner = split(features_back_t(feats, grad))
        for n in range(PAIR // tokens):
            cut = slice(n * tokens, (n + 1) * tokens)
            query = query_ref[k * PAIR + n * tokens : k * PAIR + (n + 1) * tokens, :]
            out = mxu(inner[1][:, cut], query) + mxu(inner[0][:, cut], query)
            out_ref[k * (PAIR // tokens) + n] = out[:half] - out[half:]


def grad_k_kernel(state_ref, feats_ref, key_ref, value_ref, query_ref, out_ref):
    state, total = get_state(state_ref)
    grad = sum(mxu(term, value_ref[...], NT) for term in reversed(split(state))) + total
    inner = split(features_back_t(feats_ref[...], grad))
    out = mxu(inner[1], key_ref[...]) + mxu(inner[0], key_ref[...])
    half = out.shape[0] // 2
    heads = query_ref.shape[0]
    for h in range(heads):
        out_ref[:, h // 2, h % 2, :] = query_ref[h]
    out_ref[:, heads // 2, 0, :] = out[:half] - out[half:]
    out_ref[:, heads // 2, 1, :] = jnp.zeros((half, out.shape[1]), jnp.float32)


def total_kernel(parts_ref, loss_ref, out_ref):
    total = jnp.sum(parts_ref[...], axis=0)
    out_ref[...] = jnp.broadcast_to(total[None], out_ref.shape)
    count, last, _, width = out_ref.shape
    out_ref[:, last - 1, 1, :] = jnp.broadcast_to(loss_ref[:1], (count, width))


def finish_kernel(parts_ref, query_ref, key_ref, loss_ref):
    heads = query_ref.shape[0]
    for h in range(heads):
        query_ref[h] = parts_ref[:, h // 2, h % 2, :]
    key_ref[...] = parts_ref[:, heads // 2, 0, :]
    loss_ref[...] = jnp.sum(parts_ref[:, heads // 2, 1, :], axis=0, keepdims=True)


def call(kernel, out_shape, cost, grid=None, in_specs=None, out_specs=None, scratch=()):
    extra = {} if grid is None else dict(grid=grid, in_specs=in_specs, out_specs=out_specs)
    flops, nbytes = cost
    return pl.pallas_call(
        kernel,
        out_shape=out_shape,
        scratch_shapes=scratch,
        compiler_params=pltpu.CompilerParams(vmem_limit_bytes=LIMIT),
        cost_estimate=pl.CostEstimate(flops=flops, bytes_accessed=nbytes, transcendentals=0),
        **extra,
    )


def shape(*dims, dtype=jnp.float32):
    return jax.ShapeDtypeStruct(dims, dtype)


def far(*dims, dtype=jnp.float32):
    return pltpu.HBM(dims, dtype)


def keep_far(*arrays):
    return [pltpu.with_memory_space_constraint(array, pltpu.HBM) for array in arrays]


def whole(*dims):
    return pl.BlockSpec(dims, lambda i: (0,) * len(dims))


def on_device(queries, key_heads, values, target, map_q, map_k):
    tokens, heads, width = queries.shape
    count = lax.axis_size("section")
    tp_count = lax.axis_size("tp")
    count_all = float(tokens * heads * width * count * tp_count)
    key_rows = key_heads[:, 0, :]
    value_rows = values[:, 0, :]
    map_q = map_q.transpose(0, 2, 1)
    map_k = map_k.transpose(0, 2, 1)
    half = map_q.shape[1]
    feats = 2 * half
    per = heads // STEPS
    positions = heads * tokens
    low = jnp.bfloat16
    mega = 1 << 20
    by_row = pl.BlockSpec((positions // STEPS, width), lambda i: (i, 0))
    by_head = pl.BlockSpec((per, half, width), lambda i: (i, 0, 0))

    def by_lane(rows):
        return pl.BlockSpec((rows, positions // STEPS), lambda i: (0, i))

    parts_shape = shape(count, 3, width)
    with jax.named_scope("own_state"):
        packed, key_feats = call(
            key_kernel, (parts_shape, shape(feats, tokens)), (30 * mega, mega // 2)
        )(*keep_far(key_rows, value_rows, map_k))
    with jax.named_scope("states_out"):
        gathered = exchange(packed)
    halo_keys, halo_values, key_feats = lax.optimization_barrier((key_rows, value_rows, key_feats))
    halo = lax.ppermute(
        jnp.concatenate([halo_keys, halo_values], axis=0),
        "section",
        [(i, i + 1) for i in range(count - 1)],
    )
    with jax.named_scope("query_feats"):
        query_rows = queries.transpose(1, 0, 2).reshape(positions, width)
        target_rows = target.transpose(1, 0, 2).reshape(positions, width)
        pair_shape = far(feats, positions, dtype=low)
        pair = call(
            query_kernel,
            (pair_shape, pair_shape),
            (600 * mega, 3 * mega),
            (STEPS,),
            [by_row, by_head],
            [by_lane(feats)] * 2,
        )(query_rows, map_q)
    with jax.named_scope("prefix"):
        prefix = call(lambda *refs: running_kernel(False, *refs), parts_shape, (mega, mega // 4))(
            gathered
        )
        prefix, halo, query_rows, target_rows, pair = lax.optimization_barrier(
            (prefix, halo, query_rows, target_rows, pair)
        )
    with jax.named_scope("states_back"):
        returned = exchange(prefix)
    with jax.named_scope("window"):
        window = call(
            window_kernel,
            (far(width, positions), far(1, positions), far(width, positions, dtype=low)),
            (2000 * mega, 8 * mega),
            (STEPS,),
            [by_row, whole(tokens, width), whole(tokens, width), whole(2 * tokens, width), by_row],
            [by_lane(width), by_lane(1), by_lane(width)],
        )(query_rows, key_rows, value_rows, halo, target_rows)
    with jax.named_scope("student"):
        grad_shape = far(width, positions, dtype=low)
        packed, loss_local, *grads = call(
            lambda *refs: student_kernel(2.0 / count_all, *refs),
            (parts_shape, shape(8, width), grad_shape, grad_shape, far(1, positions)),
            (400 * mega, 4 * mega),
            (STEPS,),
            [by_lane(feats), by_lane(feats), by_lane(width), by_lane(1), by_lane(width)]
            + [whole(count, 3, width)],
            [whole(count, 3, width), whole(8, width)]
            + [by_lane(width), by_lane(width), by_lane(1)],
            [
                pltpu.VMEM((width, feats), low),
                pltpu.VMEM((width, feats), low),
                pltpu.VMEM((feats, width), jnp.float32),
                pltpu.VMEM((feats, width), jnp.float32),
                pltpu.VMEM((feats, PAIR), jnp.float32),
                pltpu.VMEM((width, PAIR), jnp.float32),
            ],
        )(*keep_far(*pair, *window), returned)
    with jax.named_scope("grads_out"):
        gathered = exchange(packed)
    with jax.named_scope("grad_q"):
        grad_q = call(
            grad_q_kernel,
            shape(heads, half, width),
            (1000 * mega, 4 * mega),
            (STEPS,),
            [by_lane(feats), by_lane(feats), by_lane(width), by_lane(width), by_lane(1)]
            + [by_row, whole(count, 3, width)],
            by_head,
        )(*keep_far(*pair, *grads, query_rows), returned)
    with jax.named_scope("suffix"):
        suffix = call(lambda *refs: running_kernel(True, *refs), parts_shape, (mega, mega // 4))(
            gathered
        )
    with jax.named_scope("grads_back"):
        later = exchange(suffix)

    def over_tp(loss, bit):
        return loss + lax.ppermute(loss, "tp", [(i, i ^ bit) for i in range(tp_count)])

    with jax.named_scope("loss_near"):
        loss = over_tp(loss_local, 1)
    maps_shape = shape(count, heads // 2 + 1, 2, width)

    def exchange_maps(parts):
        return exchange(parts.reshape(-1, 2, width)).reshape(parts.shape)

    with jax.named_scope("grad_k"):
        parts = call(grad_k_kernel, maps_shape, (20 * mega, mega))(
            later, key_feats, key_rows, value_rows, grad_q
        )
        parts, loss = lax.optimization_barrier((parts, loss))
    with jax.named_scope("loss_far"):
        loss = over_tp(over_tp(loss, 2), 4)
    with jax.named_scope("maps_out"):
        sums = call(total_kernel, maps_shape, (mega, mega))(exchange_maps(parts), loss)
    with jax.named_scope("maps_back"):
        grad_q, grad_k, loss = call(
            finish_kernel,
            (shape(heads, half, width), shape(half, width), shape(1, width)),
            (mega, mega),
        )(exchange_maps(sums))
        grad_q = grad_q.transpose(0, 2, 1)
        grad_k = grad_k.T
        loss = loss[0, 0]
    return grad_q, grad_k[None], loss


def solution(mesh):
    in_specs = (
        P("section", "tp", None),
        P("section", "tp", None),
        P("section", "tp", None),
        P("section", "tp", None),
        P("tp", None, None),
        P("tp", None, None),
    )
    out_specs = (P("tp", None, None), P("tp", None, None), P())
    return jax.shard_map(
        on_device, mesh=mesh, in_specs=in_specs, out_specs=out_specs, check_vma=False
    )
```

time: 174 us -> 140 us (0.80)
  matrix products: 23.8 us -> 0 us
  Pallas kernels: 0 us -> 22.9 us
  waiting for transfers between devices: 33.7 us -> 11.7 us
  blocking collectives: 30.5 us -> 42.1 us
  starting transfers between devices: 66.3 us -> 58.5 us
  other arithmetic: 6.68 us -> 0.02 us
  local copies, waits for them, and re-layouts: 7.52 us -> 2.47 us
  between operations: 3.72 us -> 0.8 us
    all_to_all x5 -> x4, waiting for transfers between devices: 32.5 us -> 8.45 us  [exchange(): return lax.all_to_all(parts, axis, 0, 0, tiled=True)]
    dot_general x15 -> x0, matrix products: 23.8 us -> none  [the longest x1 5.32 us: on_device(): jnp.einsum('hif,fd->hid', query_feats, far_state, precision=HIGH)]
    pallas_call x0 -> x10, Pallas kernels: none -> 22.9 us  [the longest x1 5.31 us: on_device(): call(lambda *refs: student_kernel(2.0 / count_all, *refs), (parts_shape,...]
    all_to_all x1 -> x2, blocking collectives: 30.5 us -> 42.1 us  [exchange(): return lax.all_to_all(parts, axis, 0, 0, tiled=True)]
    all_to_all x5 -> x4, starting transfers between devices: 42.8 us -> 38.3 us  [exchange(): return lax.all_to_all(parts, axis, 0, 0, tiled=True)]
    slice x8 -> x0, local copies, waits for them, and re-layouts: 3.63 us -> none  [the longest x1 1.39 us: on_device(): value_window = jnp.concatenate([halo[tokens:], value_rows], axis=0)]
    ppermute x4, starting transfers between devices: 23.5 us -> 20.1 us  [the longest x3 16.8 us: over_tp(): lax.ppermute(loss, 'tp', [(i, i ^ bit) for i in range(tp_count)])]
    concatenate x4 -> x1, other arithmetic: 2.25 us -> 0.01 us  [on_device(): jnp.concatenate([halo_keys, halo_values], axis=0)]
  transfers between devices with their start and end apart: 9 -> 8, of which waited for: 6 -> 6; matrix products, arithmetic and copies ran while one was open for 12% -> 1% of each run, Pallas kernels for 0% -> 8%
where the time goes in v3:
time: 140 us; the launch traced here: 138 us
  starting transfers between devices  58.5 us (42%)
  blocking collectives  42.1 us (30%)
  Pallas kernels  22.9 us (16%)
  waiting for transfers between devices  11.7 us (8%)
  local copies, waits for them, and re-layouts  2.47 us (2%)
    all_to_all x2, blocking collectives, exchange(): return lax.all_to_all(parts, axis, 0, 0, tiled=True)  42.1 us
    all_to_all x4, starting transfers between devices, exchange(): return lax.all_to_all(parts, axis, 0, 0, tiled=True)  38.3 us
    ppermute x3, starting transfers between devices, over_tp(): lax.ppermute(loss, 'tp', [(i, i ^ bit) for i in range(tp_count)])  16.8 us
    all_to_all x4, waiting for transfers between devices, exchange(): return lax.all_to_all(parts, axis, 0, 0, tiled=True)  8.45 us
    pallas_call x1, Pallas kernels, on_device(): call(lambda *refs: student_kernel(2.0 / count_all, *refs), (parts_shape,...  5.31 us
    pallas_call x1, Pallas kernels, on_device(): call(grad_q_kernel, shape(heads, half, width), (1000 * mega, 4 * mega), (...  4.62 us
    ppermute x1, starting transfers between devices, on_device(): lax.ppermute(jnp.concatenate([halo_keys, halo_values], axis=0), 'section'...  3.38 us
    ppermute x3, waiting for transfers between devices, over_tp(): lax.ppermute(loss, 'tp', [(i, i ^ bit) for i in range(tp_count)])  3.22 us
  transfers between devices with their start and end apart: 8, of which 6 were waited for; matrix products, arithmetic and copies ran while one was open for 1% of the time, Pallas kernels for 8%

profile of v3, /device:TPU:6, one launch (start us, length us, event | category | flops | bytes accessed | tf_op | source)
XLA Modules:
  0.0 138.4 jit_solution(4480045416892489193)
XLA Ops:
  0.6 1.9 %own_state.1 = (f32[64,3,128]{2,1,0:T(4,128)}, f32[128,128]{1,0:T(8,128)S(1)}) custom-call(bf16[128,128]{1,0:T(8,128)(2,1)} %bitcast.25, bf16[128,128]{1,0:T(8,128)(2,1)} %bitcast.29, f32[1,64,128]{2,1,0:T(8,128)} %bitcast.37), custom_call_target="tpu_custom_call" | custom-call | flops 31457280 | bytes 524288 | tf_op jit(solution)/shard_map/own_state/pallas_call | solution.py:289
  2.5 0.0 copy-start.1
  2.5 0.0 copy-start.2
  2.5 12.7 %all-to-all-start = ((f32[64,3,128]{2,1,0:T(4,128)}), f32[64,3,128]{2,1,0:T(4,128)S(1)}, u32[]{:S(2)}, u32[]{:S(2)}) async-start(f32[64,3,128]{2,1,0:T(4,128)} %get-tuple-element.29), calls=%async_computation | async-start | bytes 262144 | tf_op jit(solution)/shard_map/states_out/all_to_all | solution.py:18
  15.2 0.0 copy-done.1
  15.2 0.0 copy-done.2
  15.3 3.4 %collective-permute-start = (bf16[256,128]{1,0:T(8,128)(2,1)S(1)}, bf16[256,128]{1,0:T(8,128)(2,1)S(1)}, u32[]{:S(2)}, u32[]{:S(2)}) collective-permute-start(bf16[256,128]{1,0:T(8,128)(2,1)S(1)} %pad_maximum_fusion), channel_id=1, source_target_pairs={{0,8},{8,16},{16,24},{24,32},{32,40},{40,48},{48,56},{56,64},{64,7... | collective-permute-start | bytes 196616 | tf_op jit(solution)/shard_map/ppermute | solution.py:295
  18.7 0.0 copy-start.4
  18.7 1.2 copy.9
  19.9 0.0 copy-start
  19.9 0.0 copy-done.4
  19.9 0.0 copy-start.3
  19.9 0.1 copy.10
  20.1 1.1 copy-done.3
  21.2 2.8 %query_feats.1 = (bf16[128,2048]{1,0:T(8,128)(2,1)}, bf16[128,2048]{1,0:T(8,128)(2,1)}) custom-call(bf16[2048,128]{1,0:T(8,128)(2,1)S(1)} %bitcast.21, f32[16,64,128]{2,1,0:T(8,128)S(1)} %bitcast.33), custom_call_target="tpu_custom_call" | custom-call | flops 629145600 | bytes 3145728 | tf_op jit(solution)/shard_map/query_feats/pallas_call | solution.py:304
  24.0 0.3 all-to-all-done.refs_0_
  24.3 1.2 prefix.1
  25.5 0.0 collective-permute-done.halo_ref
  25.5 10.0 %all-to-all-start.1 = ((f32[64,3,128]{2,1,0:T(4,128)}), f32[64,3,128]{2,1,0:T(4,128)S(1)}, u32[]{:S(2)}, u32[]{:S(2)}) async-start(f32[64,3,128]{2,1,0:T(4,128)} %prefix.1), calls=%async_computation.1 | async-start | bytes 262144 | tf_op jit(solution)/shard_map/states_back/all_to_all | solution.py:18
  35.5 0.0 copy-done
  35.5 3.1 %window.1 = (f32[128,2048]{1,0:T(8,128)}, f32[1,2048]{1,0:T(1,128)}, bf16[128,2048]{1,0:T(8,128)(2,1)}) custom-call(bf16[2048,128]{1,0:T(8,128)(2,1)S(1)} %bitcast.22, bf16[128,128]{1,0:T(8,128)(2,1)S(1)} %bitcast.27, bf16[128,128]{1,0:T(8,128)(2,1)S(1)} %bitcast.31, bf16[256,128]{1,0:T(8,128)(2,1)S(1)} %collective-permute-done.halo_ref, ...), custom_call_target="tpu_custom_call" | custom-call | flops 2097152000 | bytes 8388608 | tf_op jit(solution)/shard_map/window/pallas_call | solution.py:322
  38.6 5.8 %all-to-all-done.1.refs_5_.state_ref = f32[64,3,128]{2,1,0:T(4,128)S(1)} async-done(((f32[64,3,128]{2,1,0:T(4,128)}), f32[64,3,128]{2,1,0:T(4,128)S(1)}, u32[]{:S(2)}, u32[]{:S(2)}) %all-to-all-start.1) | async-done | bytes 98336 | tf_op jit(solution)/shard_map/states_back/all_to_all | solution.py:18
  44.4 5.3 %student.1 = (f32[64,3,128]{2,1,0:T(4,128)S(1)}, f32[8,128]{1,0:T(8,128)S(1)}, bf16[128,2048]{1,0:T(8,128)(2,1)}, bf16[128,2048]{1,0:T(8,128)(2,1)}, f32[1,2048]{1,0:T(1,128)}) custom-call(bf16[128,2048]{1,0:T(8,128)(2,1)} %get-tuple-element.35.refs_0_.high_ref, bf16[128,2048]{1,0:T(8,128)(2,1)} %get-tuple-element.36.refs_1_.low_ref, ...), custom_call_target="tpu_custom_call" | custom-call | flops 419430400 | bytes 4194304 | tf_op jit(solution)/shard_map/student/pallas_call | solution.py:332
  49.7 15.0 %all_to_all.30.refs_0_ = f32[64,3,128]{2,1,0:T(4,128)S(1)} all-to-all(f32[64,3,128]{2,1,0:T(4,128)S(1)} %get-tuple-element.44), channel_id=1, replica_groups=mesh['section'=64,'tp'=8] {'section'}, dimensions={0} | all-to-all | bytes 196608 | tf_op jit(solution)/shard_map/grads_out/all_to_all | solution.py:18
  64.7 1.2 suffix.1
  65.9 6.5 %all-to-all-start.3 = ((f32[64,3,128]{2,1,0:T(4,128)}), f32[64,3,128]{2,1,0:T(4,128)S(1)}, u32[]{:S(2)}, u32[]{:S(2)}) async-start(f32[64,3,128]{2,1,0:T(4,128)} %suffix.1), calls=%async_computation.3 | async-start | bytes 262144 | tf_op jit(solution)/shard_map/grads_back/all_to_all | solution.py:18
  72.4 1.9 %collective-permute-start.1 = (f32[8,128]{1,0:T(8,128)S(1)}, f32[8,128]{1,0:T(8,128)S(1)}, u32[]{:S(2)}, u32[]{:S(2)}) collective-permute-start(f32[8,128]{1,0:T(8,128)S(1)} %get-tuple-element.49), channel_id=1, source_target_pairs={{0,1},{1,0},{2,3},{3,2},{4,5},{5,4},{6,7},{7,6},{8,9},{9,8},{10,11... | collective-permute-start | bytes 12296 | tf_op jit(solution)/shard_map/loss_near/ppermute | solution.py:370
  74.3 4.6 %grad_q.1.query_ref = f32[16,64,128]{2,1,0:T(8,128)S(1)} custom-call(bf16[128,2048]{1,0:T(8,128)(2,1)} %get-tuple-element.35.refs_0_.high_ref, bf16[128,2048]{1,0:T(8,128)(2,1)} %get-tuple-element.36.refs_1_.low_ref, bf16[128,2048]{1,0:T(8,128)(2,1)} %get-tuple-element.46.grad_high_ref, bf16[128,2048]{1,0:T(8,128)(2,1)} %get-tuple-element.47.grad_low_ref, ...), custom_call_target="tpu_custom_call" | custom-call | flops 1048576000 | bytes 4194304 | tf_op jit(solution)/shard_map/grad_q/pallas_call | solution.py:353
  78.9 0.0 collective-permute-done.1
  79.0 2.2 %all-to-all-done.3.state_ref = f32[64,3,128]{2,1,0:T(4,128)S(1)} async-done(((f32[64,3,128]{2,1,0:T(4,128)}), f32[64,3,128]{2,1,0:T(4,128)S(1)}, u32[]{:S(2)}, u32[]{:S(2)}) %all-to-all-start.3) | async-done | bytes 98336 | tf_op jit(solution)/shard_map/grads_back/all_to_all | solution.py:18
  81.2 1.4 %grad_k.1 = f32[64,9,2,128]{3,2,1,0:T(2,128)} custom-call(f32[64,3,128]{2,1,0:T(4,128)S(1)} %all-to-all-done.3.state_ref, f32[128,128]{1,0:T(8,128)S(1)} %get-tuple-element.45.feats_ref, bf16[128,128]{1,0:T(8,128)(2,1)S(1)} %bitcast.28, bf16[128,128]{1,0:T(8,128)(2,1)S(1)} %bitcast.32, f32[16,64,128]{2,1,0:T(8,128)S(1)} %grad_q.1.query_ref), custom_call_target="tpu_custom_call" | custom-call | flops 20971520 | bytes 1048576 | tf_op jit(solution)/shard_map/grad_k/pallas_call | solution.py:380
  82.6 9.0 %all-to-all-start.4 = ((f32[576,2,128]{2,1,0:T(2,128)}), f32[576,2,128]{2,1,0:T(2,128)S(1)}, u32[]{:S(2)}, u32[]{:S(2)}) async-start(f32[576,2,128]{2,1,0:T(2,128)} %bitcast.8), calls=%async_computation.4 | async-start | bytes 1179648 | tf_op jit(solution)/shard_map/maps_out/all_to_all | solution.py:18
  91.6 6.1 %collective-permute-start.2 = (f32[8,128]{1,0:T(8,128)S(1)}, f32[8,128]{1,0:T(8,128)S(1)}, u32[]{:S(2)}, u32[]{:S(2)}) collective-permute-start(f32[8,128]{1,0:T(8,128)S(1)} %add.9), channel_id=1, source_target_pairs={{0,2},{1,3},{2,0},{3,1},{4,6},{5,7},{6,4},{7,5},{8,10},{9,11},{10,... | collective-permute-start | bytes 12296 | tf_op jit(solution)/shard_map/loss_far/ppermute | solution.py:370
  97.8 1.6 %collective-permute-done.2 = f32[8,128]{1,0:T(8,128)S(1)} collective-permute-done((f32[8,128]{1,0:T(8,128)S(1)}, f32[8,128]{1,0:T(8,128)S(1)}, u32[]{:S(2)}, u32[]{:S(2)}) %collective-permute-start.2) | collective-permute-done | bytes 4128 | tf_op jit(solution)/shard_map/loss_far/ppermute | solution.py:370
  99.4 8.7 %collective-permute-start.3 = (f32[8,128]{1,0:T(8,128)S(1)}, f32[8,128]{1,0:T(8,128)S(1)}, u32[]{:S(2)}, u32[]{:S(2)}) collective-permute-start(f32[8,128]{1,0:T(8,128)S(1)} %add.10), channel_id=1, source_target_pairs={{0,4},{1,5},{2,6},{3,7},{4,0},{5,1},{6,2},{7,3},{8,12},{9,13},{10,... | collective-permute-start | bytes 12296 | tf_op jit(solution)/shard_map/loss_far/ppermute | solution.py:370
  108.1 1.6 %collective-permute-done.3 = f32[8,128]{1,0:T(8,128)S(1)} collective-permute-done((f32[8,128]{1,0:T(8,128)S(1)}, f32[8,128]{1,0:T(8,128)S(1)}, u32[]{:S(2)}, u32[]{:S(2)}) %collective-permute-start.3) | collective-permute-done | bytes 4128 | tf_op jit(solution)/shard_map/loss_far/ppermute | solution.py:370
  109.7 0.2 all-to-all-done.4
  109.9 0.3 maps_out.1
  110.2 27.1 %all_to_all.31 = f32[576,2,128]{2,1,0:T(2,128)S(1)} all-to-all(f32[576,2,128]{2,1,0:T(2,128)S(1)} %bitcast.20), channel_id=1, replica_groups=mesh['section'=64,'tp'=8] {'section'}, dimensions={0} | all-to-all | bytes 1179648 | tf_op jit(solution)/shard_map/maps_back/all_to_all | solution.py:18
  137.3 1.1 maps_back.1
  (4 shorter events, 0.0 us)
Async XLA Ops:
  2.5 12.8 %copy-start.1 = (bf16[128,1,128]{2,0,1:T(8,128)(2,1)S(1)}, bf16[128,1,128]{2,0,1:T(8,128)(2,1)}, u32[]{:S(2)}) copy-start(bf16[128,1,128]{2,0,1:T(8,128)(2,1)} %param.7) | copy-start | bytes 98308
  2.5 12.8 %copy-start.2 = (bf16[128,1,128]{2,0,1:T(8,128)(2,1)S(1)}, bf16[128,1,128]{2,0,1:T(8,128)(2,1)}, u32[]{:S(2)}) copy-start(bf16[128,1,128]{2,0,1:T(8,128)(2,1)} %param.8) | copy-start | bytes 98308
  2.5 21.8 %all-to-all-start = ((f32[64,3,128]{2,1,0:T(4,128)}), f32[64,3,128]{2,1,0:T(4,128)S(1)}, u32[]{:S(2)}, u32[]{:S(2)}) async-start(f32[64,3,128]{2,1,0:T(4,128)} %get-tuple-element.29), calls=%async_computation | async-start | bytes 262144 | tf_op jit(solution)/shard_map/states_out/all_to_all | solution.py:18
  15.3 10.2 %collective-permute-start = (bf16[256,128]{1,0:T(8,128)(2,1)S(1)}, bf16[256,128]{1,0:T(8,128)(2,1)S(1)}, u32[]{:S(2)}, u32[]{:S(2)}) collective-permute-start(bf16[256,128]{1,0:T(8,128)(2,1)S(1)} %pad_maximum_fusion), channel_id=1, source_target_pairs={{0,8},{8,16},{16,24},{24,32},{32,40},{40,48},{48,56},{56,64},{64,7... | collective-permute-start | bytes 196616 | tf_op jit(solution)/shard_map/ppermute | solution.py:295
  18.7 1.3 copy-start.4
  19.9 15.6 %copy-start = (bf16[16,128,128]{2,1,0:T(8,128)(2,1)}, bf16[16,128,128]{2,1,0:T(8,128)(2,1)S(1)}, u32[]{:S(2)}) copy-start(bf16[16,128,128]{2,1,0:T(8,128)(2,1)S(1)} %copy.9) | copy-start | bytes 1572868
  19.9 1.2 copy-start.3
  25.5 18.9 %all-to-all-start.1 = ((f32[64,3,128]{2,1,0:T(4,128)}), f32[64,3,128]{2,1,0:T(4,128)S(1)}, u32[]{:S(2)}, u32[]{:S(2)}) async-start(f32[64,3,128]{2,1,0:T(4,128)} %prefix.1), calls=%async_computation.1 | async-start | bytes 262144 | tf_op jit(solution)/shard_map/states_back/all_to_all | solution.py:18
  65.9 15.3 %all-to-all-start.3 = ((f32[64,3,128]{2,1,0:T(4,128)}), f32[64,3,128]{2,1,0:T(4,128)S(1)}, u32[]{:S(2)}, u32[]{:S(2)}) async-start(f32[64,3,128]{2,1,0:T(4,128)} %suffix.1), calls=%async_computation.3 | async-start | bytes 262144 | tf_op jit(solution)/shard_map/grads_back/all_to_all | solution.py:18
  72.4 6.6 %collective-permute-start.1 = (f32[8,128]{1,0:T(8,128)S(1)}, f32[8,128]{1,0:T(8,128)S(1)}, u32[]{:S(2)}, u32[]{:S(2)}) collective-permute-start(f32[8,128]{1,0:T(8,128)S(1)} %get-tuple-element.49), channel_id=1, source_target_pairs={{0,1},{1,0},{2,3},{3,2},{4,5},{5,4},{6,7},{7,6},{8,9},{9,8},{10,11... | collective-permute-start | bytes 12296 | tf_op jit(solution)/shard_map/loss_near/ppermute | solution.py:370
  82.6 27.3 %all-to-all-start.4 = ((f32[576,2,128]{2,1,0:T(2,128)}), f32[576,2,128]{2,1,0:T(2,128)S(1)}, u32[]{:S(2)}, u32[]{:S(2)}) async-start(f32[576,2,128]{2,1,0:T(2,128)} %bitcast.8), calls=%async_computation.4 | async-start | bytes 1179648 | tf_op jit(solution)/shard_map/maps_out/all_to_all | solution.py:18
  91.6 7.7 %collective-permute-start.2 = (f32[8,128]{1,0:T(8,128)S(1)}, f32[8,128]{1,0:T(8,128)S(1)}, u32[]{:S(2)}, u32[]{:S(2)}) collective-permute-start(f32[8,128]{1,0:T(8,128)S(1)} %add.9), channel_id=1, source_target_pairs={{0,2},{1,3},{2,0},{3,1},{4,6},{5,7},{6,4},{7,5},{8,10},{9,11},{10,... | collective-permute-start | bytes 12296 | tf_op jit(solution)/shard_map/loss_far/ppermute | solution.py:370
  99.4 10.4 %collective-permute-start.3 = (f32[8,128]{1,0:T(8,128)S(1)}, f32[8,128]{1,0:T(8,128)S(1)}, u32[]{:S(2)}, u32[]{:S(2)}) collective-permute-start(f32[8,128]{1,0:T(8,128)S(1)} %add.10), channel_id=1, source_target_pairs={{0,4},{1,5},{2,6},{3,7},{4,0},{5,1},{6,2},{7,3},{8,12},{9,13},{10,... | collective-permute-start | bytes 12296 | tf_op jit(solution)/shard_map/loss_far/ppermute | solution.py:370

commit v4 on v3

--- a/solution.py
+++ b/solution.py
@@ -12,6 +12,7 @@
 LIMIT = 40 * 1024 * 1024
 STEPS = 4
 PAIR = 256
+SUBLANES = 8
 
 
 def exchange(parts, axis="section"):
@@ -79,7 +80,7 @@
     put_state(parts_ref, state, total)
 
 
-def running_kernel(backward, parts_ref, out_ref):
+def running_kernel(backward, parts_ref, out_ref, *loss_ref):
     count = parts_ref.shape[0]
     row = lax.broadcasted_iota(jnp.int32, (count, count), 0)
     col = lax.broadcasted_iota(jnp.int32, (count, count), 1)
@@ -88,6 +89,10 @@
     for k in range(parts_ref.shape[1]):
         terms = split(parts_ref[:, k, :], 3)
         out_ref[:, k, :] = sum(mxu(chosen, term) for term in reversed(terms))
+    if loss_ref:
+        width = parts_ref.shape[2]
+        loss = jnp.sum(parts_ref[:, 2, width - 1 :], axis=0, keepdims=True)
+        loss_ref[0][...] = jnp.broadcast_to(loss, loss_ref[0].shape)
 
 
 def query_kernel(query_ref, map_ref, high_ref, low_ref):
@@ -135,54 +140,38 @@
     target_ref,
     state_ref,
     parts_ref,
-    loss_ref,
     grad_high_ref,
     grad_low_ref,
     grad_total_ref,
-    state_high,
-    state_low,
-    total_acc,
-    grad_acc,
-    grad_total_acc,
-    loss_acc,
 ):
-    step = pl.program_id(0)
-
-    @pl.when(step == 0)
-    def _():
-        state, total = get_state(state_ref)
-        state_high[...], state_low[...] = split(state.T)
-        total_acc[...] = total
-        grad_acc[...] = jnp.zeros_like(grad_acc)
-        grad_total_acc[...] = jnp.zeros_like(grad_total_acc)
-        loss_acc[...] = jnp.zeros_like(loss_acc)
-
-    state = (state_high[...], state_low[...])
-    total = jnp.concatenate([total_acc[...]] * (PAIR // total_acc.shape[1]), axis=1)
+    state, total = get_state(state_ref)
+    width = state.shape[1]
+    extra = 2 * SUBLANES
+    state = split(jnp.concatenate([state.T, total.T[:extra]], axis=0))
+    grad_both = 0.0
+    loss = 0.0
     for k in range(sum_ref.shape[1] // PAIR):
         here = slice(k * PAIR, (k + 1) * PAIR)
         pair = (high_ref[:, here], low_ref[:, here])
-        feats = pair[0].astype(jnp.float32) + pair[1].astype(jnp.float32)
         scale = scale_ref[:, here]
-        linear_total = jnp.sum(feats * total, axis=0, keepdims=True)
-        inverse = 1.0 / (1.0 + scale * linear_total)
-        student = (sum_ref[:, here] + scale * mxu3(state, pair)) * inverse
+        linear = mxu3(state, pair)
+        inverse = 1.0 / (1.0 + scale * linear[width : width + 1])
+        student = (sum_ref[:, here] + scale * linear[:width]) * inverse
         error = student - target_ref[:, here].astype(jnp.float32)
-        loss_acc[...] += error * error
+        loss = loss + jnp.sum((error * error).reshape(-1, SUBLANES, PAIR), axis=0)
         grad_sum = error * (scale * inverse * factor)
         grad_total = -jnp.sum(grad_sum * student, axis=0, keepdims=True)
         grads = split(grad_sum)
         grad_high_ref[:, here], grad_low_ref[:, here] = grads
         grad_total_ref[:, here] = grad_total
-        grad_acc[...] += mxu3(pair, grads, NT)
-        grad_total_acc[...] += feats * grad_total
-
-    @pl.when(step == pl.num_programs(0) - 1)
-    def _():
-        grad = grad_acc[...]
-        grad_total = jnp.sum(grad_total_acc[...], axis=1, keepdims=True)
-        put_state(parts_ref, grad, jnp.broadcast_to(grad_total, grad.shape))
-        loss_ref[...] = jnp.full(loss_ref.shape, jnp.sum(loss_acc[...]) * (0.5 * factor))
+        totals = split(jnp.broadcast_to(grad_total, (extra, PAIR)))
+        grads = [jnp.concatenate(both, axis=0) for both in zip(grads, totals)]
+        grad_both = grad_both + mxu3(pair, grads, NT)
+    grad = grad_both[:, :width]
+    total = jnp.broadcast_to(grad_both[:, width : width + 1], grad.shape)
+    lane = lax.broadcasted_iota(jnp.int32, total.shape, 1)
+    total = jnp.where(lane == width - 1, jnp.sum(loss) * (0.5 * factor), total)
+    put_state(parts_ref, grad, total)
 
 
 def grad_q_kernel(
@@ -231,7 +220,13 @@
     for h in range(heads):
         query_ref[h] = parts_ref[:, h // 2, h % 2, :]
     key_ref[...] = parts_ref[:, heads // 2, 0, :]
-    loss_ref[...] = jnp.sum(parts_ref[:, heads // 2, 1, :], axis=0, keepdims=True)
+    group = lax.axis_index("tp")
+    count = lax.axis_size("tp")
+    losses = parts_ref[:count, heads // 2, 1, :]
+    owner = lax.rem(lax.broadcasted_iota(jnp.int32, losses.shape, 0) + group, count)
+    loss_ref[...] = sum(
+        jnp.sum(jnp.where(owner == k, losses, 0.0), axis=0, keepdims=True) for k in range(count)
+    )
 
 
 def call(kernel, out_shape, cost, grid=None, in_specs=None, out_specs=None, scratch=()):
@@ -329,23 +324,10 @@
         )(query_rows, key_rows, value_rows, halo, target_rows)
     with jax.named_scope("student"):
         grad_shape = far(width, positions, dtype=low)
-        packed, loss_local, *grads = call(
+        packed, *grads = call(
             lambda *refs: student_kernel(2.0 / count_all, *refs),
-            (parts_shape, shape(8, width), grad_shape, grad_shape, far(1, positions)),
+            (parts_shape, grad_shape, grad_shape, far(1, positions)),
             (400 * mega, 4 * mega),
-            (STEPS,),
-            [by_lane(feats), by_lane(feats), by_lane(width), by_lane(1), by_lane(width)]
-            + [whole(count, 3, width)],
-            [whole(count, 3, width), whole(8, width)]
-            + [by_lane(width), by_lane(width), by_lane(1)],
-            [
-                pltpu.VMEM((width, feats), low),
-                pltpu.VMEM((width, feats), low),
-                pltpu.VMEM((feats, width), jnp.float32),
-                pltpu.VMEM((feats, width), jnp.float32),
-                pltpu.VMEM((feats, PAIR), jnp.float32),
-                pltpu.VMEM((width, PAIR), jnp.float32),
-            ],
         )(*keep_far(*pair, *window), returned)
     with jax.named_scope("grads_out"):
         gathered = exchange(packed)
@@ -360,17 +342,13 @@
             by_head,
         )(*keep_far(*pair, *grads, query_rows), returned)
     with jax.named_scope("suffix"):
-        suffix = call(lambda *refs: running_kernel(True, *refs), parts_shape, (mega, mega // 4))(
-            gathered
-        )
+        suffix, loss = call(
+            lambda *refs: running_kernel(True, *refs),
+            (parts_shape, shape(SUBLANES, width)),
+            (mega, mega // 4),
+        )(gathered)
     with jax.named_scope("grads_back"):
         later = exchange(suffix)
-
-    def over_tp(loss, bit):
-        return loss + lax.ppermute(loss, "tp", [(i, i ^ bit) for i in range(tp_count)])
-
-    with jax.named_scope("loss_near"):
-        loss = over_tp(loss_local, 1)
     maps_shape = shape(count, heads // 2 + 1, 2, width)
 
     def exchange_maps(parts):
@@ -381,8 +359,16 @@
             later, key_feats, key_rows, value_rows, grad_q
         )
         parts, loss = lax.optimization_barrier((parts, loss))
-    with jax.named_scope("loss_far"):
-        loss = over_tp(over_tp(loss, 2), 4)
+    with jax.named_scope("loss_turn"):
+        loss = lax.ppermute(
+            loss,
+            ("section", "tp"),
+            [
+                (s * tp_count + (t + s) % tp_count, s * tp_count + t)
+                for s in range(count)
+                for t in range(tp_count)
+            ],
+        )
     with jax.named_scope("maps_out"):
         sums = call(total_kernel, maps_shape, (mega, mega))(exchange_maps(parts), loss)
     with jax.named_scope("maps_back"):

time: 140 us -> 131 us (0.936)
  starting transfers between devices: 58.5 us -> 40.4 us
  waiting for transfers between devices: 11.7 us -> 23.7 us
  blocking collectives: 42.1 us -> 40.3 us
    ppermute x3 -> x1, starting transfers between devices: 16.8 us -> 0.66 us  [on_device(): lax.ppermute(loss, ('section', 'tp'), [(s * tp_count + (t + s) % tp_count...]
    all_to_all x4, waiting for transfers between devices: 8.45 us -> 23.7 us  [exchange(): return lax.all_to_all(parts, axis, 0, 0, tiled=True)]
    ppermute x3 -> x1, waiting for transfers between devices: 3.22 us -> 0.01 us  [on_device(): lax.ppermute(loss, ('section', 'tp'), [(s * tp_count + (t + s) % tp_count...]
    all_to_all x4, starting transfers between devices: 38.3 us -> 36.4 us  [exchange(): return lax.all_to_all(parts, axis, 0, 0, tiled=True)]
    all_to_all x2, blocking collectives: 42.1 us -> 40.3 us  [exchange(): return lax.all_to_all(parts, axis, 0, 0, tiled=True)]
  transfers between devices with their start and end apart: 8 -> 6, of which waited for: 6 -> 4; matrix products, arithmetic and copies ran while one was open for 1% -> 1% of each run, Pallas kernels for 8% -> 9%
where the time goes in v4:
time: 131 us; the launch traced here: 129 us
  starting transfers between devices  40.4 us (31%)
  blocking collectives  40.3 us (31%)
  waiting for transfers between devices  23.7 us (18%)
  Pallas kernels  21.6 us (16%)
  local copies, waits for them, and re-layouts  2.47 us (2%)
    all_to_all x2, blocking collectives, exchange(): return lax.all_to_all(parts, axis, 0, 0, tiled=True)  40.3 us
    all_to_all x4, starting transfers between devices, exchange(): return lax.all_to_all(parts, axis, 0, 0, tiled=True)  36.4 us
    all_to_all x4, waiting for transfers between devices, exchange(): return lax.all_to_all(parts, axis, 0, 0, tiled=True)  23.7 us
    pallas_call x1, Pallas kernels, on_device(): call(grad_q_kernel, shape(heads, half, width), (1000 * mega, 4 * mega), (...  4.62 us
    pallas_call x1, Pallas kernels, on_device(): call(lambda *refs: student_kernel(2.0 / count_all, *refs), (parts_shape,...  4.03 us
    ppermute x1, starting transfers between devices, on_device(): lax.ppermute(jnp.concatenate([halo_keys, halo_values], axis=0), 'section'...  3.38 us
    pallas_call x1, Pallas kernels, on_device(): call(window_kernel, (far(width, positions), far(1, positions), far(width,...  3.07 us
    pallas_call x1, Pallas kernels, on_device(): call(query_kernel, (pair_shape, pair_shape), (600 * mega, 3 * mega), (STE...  2.83 us
  transfers between devices with their start and end apart: 6, of which 4 were waited for; matrix products, arithmetic and copies ran while one was open for 1% of the time, Pallas kernels for 9%

profile of v4, /device:TPU:6, one launch (start us, length us, event | category | flops | bytes accessed | tf_op | source)
XLA Modules:
  0.0 129.3 jit_solution(9445214659351988692)
XLA Ops:
  0.6 1.9 %own_state.1 = (f32[64,3,128]{2,1,0:T(4,128)}, f32[128,128]{1,0:T(8,128)S(1)}) custom-call(bf16[128,128]{1,0:T(8,128)(2,1)} %bitcast.25, bf16[128,128]{1,0:T(8,128)(2,1)} %bitcast.29, f32[1,64,128]{2,1,0:T(8,128)} %bitcast.37), custom_call_target="tpu_custom_call" | custom-call | flops 31457280 | bytes 524288 | tf_op jit(solution)/shard_map/own_state/pallas_call | solution.py:284
  2.5 0.0 copy-start.1
  2.5 0.0 copy-start.2
  2.5 12.7 %all-to-all-start = ((f32[64,3,128]{2,1,0:T(4,128)}), f32[64,3,128]{2,1,0:T(4,128)S(1)}, u32[]{:S(2)}, u32[]{:S(2)}) async-start(f32[64,3,128]{2,1,0:T(4,128)} %get-tuple-element.30), calls=%async_computation | async-start | bytes 262144 | tf_op jit(solution)/shard_map/states_out/all_to_all | solution.py:19
  15.2 0.0 copy-done.1
  15.2 0.0 copy-done.2
  15.3 3.4 %collective-permute-start = (bf16[256,128]{1,0:T(8,128)(2,1)S(1)}, bf16[256,128]{1,0:T(8,128)(2,1)S(1)}, u32[]{:S(2)}, u32[]{:S(2)}) collective-permute-start(bf16[256,128]{1,0:T(8,128)(2,1)S(1)} %pad_maximum_fusion), channel_id=1, source_target_pairs={{0,8},{8,16},{16,24},{24,32},{32,40},{40,48},{48,56},{56,64},{64,7... | collective-permute-start | bytes 196616 | tf_op jit(solution)/shard_map/ppermute | solution.py:290
  18.7 0.0 copy-start.4
  18.7 1.2 copy.9
  19.9 0.0 copy-start
  19.9 0.0 copy-done.4
  19.9 0.0 copy-start.3
  19.9 0.1 copy.10
  20.1 1.1 copy-done.3
  21.2 2.8 %query_feats.1 = (bf16[128,2048]{1,0:T(8,128)(2,1)}, bf16[128,2048]{1,0:T(8,128)(2,1)}) custom-call(bf16[2048,128]{1,0:T(8,128)(2,1)S(1)} %bitcast.21, f32[16,64,128]{2,1,0:T(8,128)S(1)} %bitcast.33), custom_call_target="tpu_custom_call" | custom-call | flops 629145600 | bytes 3145728 | tf_op jit(solution)/shard_map/query_feats/pallas_call | solution.py:299
  24.0 0.3 all-to-all-done.refs_0_
  24.3 1.2 prefix.1
  25.5 0.0 collective-permute-done.halo_ref
  25.5 10.0 %all-to-all-start.1 = ((f32[64,3,128]{2,1,0:T(4,128)}), f32[64,3,128]{2,1,0:T(4,128)S(1)}, u32[]{:S(2)}, u32[]{:S(2)}) async-start(f32[64,3,128]{2,1,0:T(4,128)} %prefix.1), calls=%async_computation.1 | async-start | bytes 262144 | tf_op jit(solution)/shard_map/states_back/all_to_all | solution.py:19
  35.5 0.0 copy-done
  35.5 3.1 %window.1 = (f32[128,2048]{1,0:T(8,128)}, f32[1,2048]{1,0:T(1,128)}, bf16[128,2048]{1,0:T(8,128)(2,1)}) custom-call(bf16[2048,128]{1,0:T(8,128)(2,1)S(1)} %bitcast.22, bf16[128,128]{1,0:T(8,128)(2,1)S(1)} %bitcast.27, bf16[128,128]{1,0:T(8,128)(2,1)S(1)} %bitcast.31, bf16[256,128]{1,0:T(8,128)(2,1)S(1)} %collective-permute-done.halo_ref, ...), custom_call_target="tpu_custom_call" | custom-call | flops 2097152000 | bytes 8388608 | tf_op jit(solution)/shard_map/window/pallas_call | solution.py:317
  38.6 5.8 %all-to-all-done.1.refs_5_.state_ref = f32[64,3,128]{2,1,0:T(4,128)S(1)} async-done(((f32[64,3,128]{2,1,0:T(4,128)}), f32[64,3,128]{2,1,0:T(4,128)S(1)}, u32[]{:S(2)}, u32[]{:S(2)}) %all-to-all-start.1) | async-done | bytes 98336 | tf_op jit(solution)/shard_map/states_back/all_to_all | solution.py:19
  44.4 4.0 %student.1 = (f32[64,3,128]{2,1,0:T(4,128)S(1)}, bf16[128,2048]{1,0:T(8,128)(2,1)}, bf16[128,2048]{1,0:T(8,128)(2,1)}, f32[1,2048]{1,0:T(1,128)}) custom-call(bf16[128,2048]{1,0:T(8,128)(2,1)} %get-tuple-element.36.refs_0_.high_ref, bf16[128,2048]{1,0:T(8,128)(2,1)} %get-tuple-element.37.refs_1_.low_ref, f32[128,2048]{1,0:T(8,128)} %get-tuple-element.41.refs_2_, ...), custom_call_target="tpu_custom_call" | custom-call | flops 419430400 | bytes 4194304 | tf_op jit(solution)/shard_map/student/pallas_call | solution.py:327
  48.4 15.0 %all_to_all.30.refs_0_ = f32[64,3,128]{2,1,0:T(4,128)S(1)} all-to-all(f32[64,3,128]{2,1,0:T(4,128)S(1)} %get-tuple-element.45), channel_id=1, replica_groups=mesh['section'=64,'tp'=8] {'section'}, dimensions={0} | all-to-all | bytes 196608 | tf_op jit(solution)/shard_map/grads_out/all_to_all | solution.py:19
  63.4 1.2 suffix.1
  64.6 6.5 %all-to-all-start.3 = ((f32[64,3,128]{2,1,0:T(4,128)}), f32[64,3,128]{2,1,0:T(4,128)S(1)}, u32[]{:S(2)}, u32[]{:S(2)}) async-start(f32[64,3,128]{2,1,0:T(4,128)} %get-tuple-element.46), calls=%async_computation.3 | async-start | bytes 262144 | tf_op jit(solution)/shard_map/grads_back/all_to_all | solution.py:19
  71.1 4.6 %grad_q.1.query_ref = f32[16,64,128]{2,1,0:T(8,128)S(1)} custom-call(bf16[128,2048]{1,0:T(8,128)(2,1)} %get-tuple-element.36.refs_0_.high_ref, bf16[128,2048]{1,0:T(8,128)(2,1)} %get-tuple-element.37.refs_1_.low_ref, bf16[128,2048]{1,0:T(8,128)(2,1)} %get-tuple-element.48.grad_high_ref, bf16[128,2048]{1,0:T(8,128)(2,1)} %get-tuple-element.49.grad_low_ref, ...), custom_call_target="tpu_custom_call" | custom-call | flops 1048576000 | bytes 4194304 | tf_op jit(solution)/shard_map/grad_q/pallas_call | solution.py:335
  75.8 4.2 %all-to-all-done.3.state_ref = f32[64,3,128]{2,1,0:T(4,128)S(1)} async-done(((f32[64,3,128]{2,1,0:T(4,128)}), f32[64,3,128]{2,1,0:T(4,128)S(1)}, u32[]{:S(2)}, u32[]{:S(2)}) %all-to-all-start.3) | async-done | bytes 98336 | tf_op jit(solution)/shard_map/grads_back/all_to_all | solution.py:19
  79.9 1.4 %grad_k.1 = f32[64,9,2,128]{3,2,1,0:T(2,128)} custom-call(f32[64,3,128]{2,1,0:T(4,128)S(1)} %all-to-all-done.3.state_ref, f32[128,128]{1,0:T(8,128)S(1)} %get-tuple-element.47.feats_ref, bf16[128,128]{1,0:T(8,128)(2,1)S(1)} %bitcast.28, bf16[128,128]{1,0:T(8,128)(2,1)S(1)} %bitcast.32, f32[16,64,128]{2,1,0:T(8,128)S(1)} %grad_q.1.query_ref), custom_call_target="tpu_custom_call" | custom-call | flops 20971520 | bytes 1048576 | tf_op jit(solution)/shard_map/grad_k/pallas_call | solution.py:358
  81.4 7.1 %all-to-all-start.4 = ((f32[576,2,128]{2,1,0:T(2,128)}), f32[576,2,128]{2,1,0:T(2,128)S(1)}, u32[]{:S(2)}, u32[]{:S(2)}) async-start(f32[576,2,128]{2,1,0:T(2,128)} %bitcast.8), calls=%async_computation.4 | async-start | bytes 1179648 | tf_op jit(solution)/shard_map/maps_out/all_to_all | solution.py:19
  88.5 0.7 collective-permute-start.1
  89.1 0.0 collective-permute-done.1.loss_ref
  89.1 13.5 %all-to-all-done.4 = f32[576,2,128]{2,1,0:T(2,128)S(1)} async-done(((f32[576,2,128]{2,1,0:T(2,128)}), f32[576,2,128]{2,1,0:T(2,128)S(1)}, u32[]{:S(2)}, u32[]{:S(2)}) %all-to-all-start.4) | async-done | bytes 589856 | tf_op jit(solution)/shard_map/maps_out/all_to_all | solution.py:19
  102.6 0.3 maps_out.1
  102.9 25.3 %all_to_all.31 = f32[576,2,128]{2,1,0:T(2,128)S(1)} all-to-all(f32[576,2,128]{2,1,0:T(2,128)S(1)} %bitcast.20), channel_id=1, replica_groups=mesh['section'=64,'tp'=8] {'section'}, dimensions={0} | all-to-all | bytes 1179648 | tf_op jit(solution)/shard_map/maps_back/all_to_all | solution.py:19
  128.2 1.1 maps_back.1
  (1 shorter events, 0.0 us)
Async XLA Ops:
  2.5 12.8 %copy-start.1 = (bf16[128,1,128]{2,0,1:T(8,128)(2,1)S(1)}, bf16[128,1,128]{2,0,1:T(8,128)(2,1)}, u32[]{:S(2)}) copy-start(bf16[128,1,128]{2,0,1:T(8,128)(2,1)} %param.7) | copy-start | bytes 98308
  2.5 12.8 %copy-start.2 = (bf16[128,1,128]{2,0,1:T(8,128)(2,1)S(1)}, bf16[128,1,128]{2,0,1:T(8,128)(2,1)}, u32[]{:S(2)}) copy-start(bf16[128,1,128]{2,0,1:T(8,128)(2,1)} %param.8) | copy-start | bytes 98308
  2.5 21.8 %all-to-all-start = ((f32[64,3,128]{2,1,0:T(4,128)}), f32[64,3,128]{2,1,0:T(4,128)S(1)}, u32[]{:S(2)}, u32[]{:S(2)}) async-start(f32[64,3,128]{2,1,0:T(4,128)} %get-tuple-element.30), calls=%async_computation | async-start | bytes 262144 | tf_op jit(solution)/shard_map/states_out/all_to_all | solution.py:19
  15.3 10.2 %collective-permute-start = (bf16[256,128]{1,0:T(8,128)(2,1)S(1)}, bf16[256,128]{1,0:T(8,128)(2,1)S(1)}, u32[]{:S(2)}, u32[]{:S(2)}) collective-permute-start(bf16[256,128]{1,0:T(8,128)(2,1)S(1)} %pad_maximum_fusion), channel_id=1, source_target_pairs={{0,8},{8,16},{16,24},{24,32},{32,40},{40,48},{48,56},{56,64},{64,7... | collective-permute-start | bytes 196616 | tf_op jit(solution)/shard_map/ppermute | solution.py:290
  18.7 1.3 copy-start.4
  19.9 15.6 %copy-start = (bf16[16,128,128]{2,1,0:T(8,128)(2,1)}, bf16[16,128,128]{2,1,0:T(8,128)(2,1)S(1)}, u32[]{:S(2)}) copy-start(bf16[16,128,128]{2,1,0:T(8,128)(2,1)S(1)} %copy.9) | copy-start | bytes 1572868
  19.9 1.2 copy-start.3
  25.5 18.9 %all-to-all-start.1 = ((f32[64,3,128]{2,1,0:T(4,128)}), f32[64,3,128]{2,1,0:T(4,128)S(1)}, u32[]{:S(2)}, u32[]{:S(2)}) async-start(f32[64,3,128]{2,1,0:T(4,128)} %prefix.1), calls=%async_computation.1 | async-start | bytes 262144 | tf_op jit(solution)/shard_map/states_back/all_to_all | solution.py:19
  64.6 15.3 %all-to-all-start.3 = ((f32[64,3,128]{2,1,0:T(4,128)}), f32[64,3,128]{2,1,0:T(4,128)S(1)}, u32[]{:S(2)}, u32[]{:S(2)}) async-start(f32[64,3,128]{2,1,0:T(4,128)} %get-tuple-element.46), calls=%async_computation.3 | async-start | bytes 262144 | tf_op jit(solution)/shard_map/grads_back/all_to_all | solution.py:19
  81.4 21.2 %all-to-all-start.4 = ((f32[576,2,128]{2,1,0:T(2,128)}), f32[576,2,128]{2,1,0:T(2,128)S(1)}, u32[]{:S(2)}, u32[]{:S(2)}) async-start(f32[576,2,128]{2,1,0:T(2,128)} %bitcast.8), calls=%async_computation.4 | async-start | bytes 1179648 | tf_op jit(solution)/shard_map/maps_out/all_to_all | solution.py:19
  88.5 0.7 collective-permute-start.1

commit v5 on v4

--- a/solution.py
+++ b/solution.py
@@ -10,7 +10,7 @@
 NN = (((1,), (0,)), ((), ()))
 NT = (((1,), (1,)), ((), ()))
 LIMIT = 40 * 1024 * 1024
-STEPS = 4
+STEPS = 2
 PAIR = 256
 SUBLANES = 8
 
@@ -180,8 +180,9 @@
     state, total = get_state(state_ref)
     total = jnp.concatenate([total] * (PAIR // total.shape[1]), axis=1)
     state = split(state)
-    heads, half, _ = out_ref.shape
-    tokens = query_ref.shape[0] // heads
+    _, kept, half, _ = out_ref.shape
+    tokens = query_ref.shape[0] // kept
+    slot = (pl.program_id(0) + lax.axis_index("section")) % 2
     for k in range(query_ref.shape[0] // PAIR):
         here = slice(k * PAIR, (k + 1) * PAIR)
         grad = mxu3(state, (grad_high_ref[:, here], grad_low_ref[:, here]))
@@ -192,41 +193,40 @@
             cut = slice(n * tokens, (n + 1) * tokens)
             query = query_ref[k * PAIR + n * tokens : k * PAIR + (n + 1) * tokens, :]
             out = mxu(inner[1][:, cut], query) + mxu(inner[0][:, cut], query)
-            out_ref[k * (PAIR // tokens) + n] = out[:half] - out[half:]
-
-
-def grad_k_kernel(state_ref, feats_ref, key_ref, value_ref, query_ref, out_ref):
+            out_ref[slot, k * (PAIR // tokens) + n] = out[:half] - out[half:]
+
+
+def grad_k_kernel(state_ref, feats_ref, key_ref, value_ref, query_ref, other_ref, out_ref):
     state, total = get_state(state_ref)
     grad = sum(mxu(term, value_ref[...], NT) for term in reversed(split(state))) + total
     inner = split(features_back_t(feats_ref[...], grad))
     out = mxu(inner[1], key_ref[...]) + mxu(inner[0], key_ref[...])
     half = out.shape[0] // 2
-    heads = query_ref.shape[0]
-    for h in range(heads):
-        out_ref[:, h // 2, h % 2, :] = query_ref[h]
-    out_ref[:, heads // 2, 0, :] = out[:half] - out[half:]
-    out_ref[:, heads // 2, 1, :] = jnp.zeros((half, out.shape[1]), jnp.float32)
-
-
-def total_kernel(parts_ref, loss_ref, out_ref):
-    total = jnp.sum(parts_ref[...], axis=0)
-    out_ref[...] = jnp.broadcast_to(total[None], out_ref.shape)
-    count, last, _, width = out_ref.shape
-    out_ref[:, last - 1, 1, :] = jnp.broadcast_to(loss_ref[:1], (count, width))
-
-
-def finish_kernel(parts_ref, query_ref, key_ref, loss_ref):
+    kept = query_ref.shape[1]
+    for h in range(kept):
+        out_ref[:, h // 2, h % 2, :] = query_ref[0, h] + other_ref[h]
+    out_ref[:, kept // 2, 0, :] = out[:half] - out[half:]
+    out_ref[:, kept // 2, 1, :] = jnp.zeros((half, out.shape[1]), jnp.float32)
+
+
+def total_kernel(parts_ref, out_ref):
+    count, last, _, width = parts_ref.shape
+    parts = parts_ref[...].reshape(count // 2, 2, last, 2, width)
+    total = jnp.sum(parts, axis=0)
+    last = last - 1
+    for n in range(2):
+        out_ref[:, n * last : (n + 1) * last] = jnp.broadcast_to(
+            total[n, None, :last], (count, last, 2, width)
+        )
+    out_ref[:, 2 * last, 0, :] = jnp.broadcast_to(total[0, last, :1] + total[1, last, :1], (count, width))
+    out_ref[:, 2 * last, 1, :] = jnp.zeros((count, width), jnp.float32)
+
+
+def finish_kernel(parts_ref, query_ref, key_ref):
     heads = query_ref.shape[0]
     for h in range(heads):
         query_ref[h] = parts_ref[:, h // 2, h % 2, :]
     key_ref[...] = parts_ref[:, heads // 2, 0, :]
-    group = lax.axis_index("tp")
-    count = lax.axis_size("tp")
-    losses = parts_ref[:count, heads // 2, 1, :]
-    owner = lax.rem(lax.broadcasted_iota(jnp.int32, losses.shape, 0) + group, count)
-    loss_ref[...] = sum(
-        jnp.sum(jnp.where(owner == k, losses, 0.0), axis=0, keepdims=True) for k in range(count)
-    )
 
 
 def call(kernel, out_shape, cost, grid=None, in_specs=None, out_specs=None, scratch=()):
@@ -294,7 +294,6 @@
     )
     with jax.named_scope("query_feats"):
         query_rows = queries.transpose(1, 0, 2).reshape(positions, width)
-        target_rows = target.transpose(1, 0, 2).reshape(positions, width)
         pair_shape = far(feats, positions, dtype=low)
         pair = call(
             query_kernel,
@@ -308,12 +307,13 @@
         prefix = call(lambda *refs: running_kernel(False, *refs), parts_shape, (mega, mega // 4))(
             gathered
         )
-        prefix, halo, query_rows, target_rows, pair = lax.optimization_barrier(
-            (prefix, halo, query_rows, target_rows, pair)
+        prefix, halo, query_rows, target, pair = lax.optimization_barrier(
+            (prefix, halo, query_rows, target, pair)
         )
     with jax.named_scope("states_back"):
         returned = exchange(prefix)
     with jax.named_scope("window"):
+        target_rows = target.transpose(1, 0, 2).reshape(positions, width)
         window = call(
             window_kernel,
             (far(width, positions), far(1, positions), far(width, positions, dtype=low)),
@@ -334,14 +334,17 @@
     with jax.named_scope("grad_q"):
         grad_q = call(
             grad_q_kernel,
-            shape(heads, half, width),
+            shape(2, heads // 2, half, width),
             (1000 * mega, 4 * mega),
             (STEPS,),
             [by_lane(feats), by_lane(feats), by_lane(width), by_lane(width), by_lane(1)]
             + [by_row, whole(count, 3, width)],
-            by_head,
+            whole(2, heads // 2, half, width),
         )(*keep_far(*pair, *grads, query_rows), returned)
+    with jax.named_scope("grad_q_swap"):
+        other = lax.ppermute(grad_q[1], "section", [(i, i ^ 1) for i in range(count)])
     with jax.named_scope("suffix"):
+        gathered, grad_q = lax.optimization_barrier((gathered, grad_q))
         suffix, loss = call(
             lambda *refs: running_kernel(True, *refs),
             (parts_shape, shape(SUBLANES, width)),
@@ -349,33 +352,34 @@
         )(gathered)
     with jax.named_scope("grads_back"):
         later = exchange(suffix)
+    def over_tp(loss, bit):
+        return loss + lax.ppermute(loss, "tp", [(i, i ^ bit) for i in range(tp_count)])
+
+    with jax.named_scope("loss_core"):
+        loss = over_tp(loss, 1)
+        later, loss = lax.optimization_barrier((later, loss))
+    sent_shape = shape(count, heads // 4 + 1, 2, width)
     maps_shape = shape(count, heads // 2 + 1, 2, width)
 
     def exchange_maps(parts):
         return exchange(parts.reshape(-1, 2, width)).reshape(parts.shape)
 
     with jax.named_scope("grad_k"):
-        parts = call(grad_k_kernel, maps_shape, (20 * mega, mega))(
-            later, key_feats, key_rows, value_rows, grad_q
+        parts = call(grad_k_kernel, sent_shape, (20 * mega, mega))(
+            later, key_feats, key_rows, value_rows, grad_q, other
         )
         parts, loss = lax.optimization_barrier((parts, loss))
-    with jax.named_scope("loss_turn"):
-        loss = lax.ppermute(
-            loss,
-            ("section", "tp"),
-            [
-                (s * tp_count + (t + s) % tp_count, s * tp_count + t)
-                for s in range(count)
-                for t in range(tp_count)
-            ],
-        )
+    with jax.named_scope("loss_near"):
+        loss = over_tp(loss, 2)
     with jax.named_scope("maps_out"):
-        sums = call(total_kernel, maps_shape, (mega, mega))(exchange_maps(parts), loss)
+        parts, loss = lax.optimization_barrier((exchange_maps(parts), loss))
+        sums = call(total_kernel, maps_shape, (mega, mega))(parts)
+        sums, loss = lax.optimization_barrier((sums, loss))
+    with jax.named_scope("loss_far"):
+        loss = over_tp(loss, 4)
     with jax.named_scope("maps_back"):
-        grad_q, grad_k, loss = call(
-            finish_kernel,
-            (shape(heads, half, width), shape(half, width), shape(1, width)),
-            (mega, mega),
+        grad_q, grad_k = call(
+            finish_kernel, (shape(heads, half, width), shape(half, width)), (mega, mega)
         )(exchange_maps(sums))
         grad_q = grad_q.transpose(0, 2, 1)
         grad_k = grad_k.T

time: 131 us -> 129 us (0.985)
  blocking collectives: 40.3 us -> 0 us
  starting transfers between devices: 40.4 us -> 74.7 us
  waiting for transfers between devices: 23.7 us -> 29 us
    all_to_all x2 -> x0, blocking collectives: 40.3 us -> none  [exchange(): return lax.all_to_all(parts, axis, 0, 0, tiled=True)]
    ppermute x1 -> x4, starting transfers between devices: 0.66 us -> 21.3 us  [the longest x3 17.9 us: over_tp(): lax.ppermute(loss, 'tp', [(i, i ^ bit) for i in range(tp_count)])]
    all_to_all x4 -> x6, starting transfers between devices: 36.4 us -> 50 us  [exchange(): return lax.all_to_all(parts, axis, 0, 0, tiled=True)]
    ppermute x1 -> x4, waiting for transfers between devices: 0.01 us -> 4.49 us  [the longest x3 4.49 us: over_tp(): lax.ppermute(loss, 'tp', [(i, i ^ bit) for i in range(tp_count)])]
    all_to_all x4 -> x6, waiting for transfers between devices: 23.7 us -> 24.6 us  [exchange(): return lax.all_to_all(parts, axis, 0, 0, tiled=True)]
  transfers between devices with their start and end apart: 6 -> 11, of which waited for: 4 -> 9; matrix products, arithmetic and copies ran while one was open for 1% -> 2% of each run, Pallas kernels for 9% -> 9%
where the time goes in v5:
time: 129 us; the launch traced here: 127 us
  starting transfers between devices  74.7 us (58%)
  waiting for transfers between devices  29 us (22%)
  Pallas kernels  20.3 us (16%)
  local copies, waits for them, and re-layouts  1.93 us (1%)
    all_to_all x6, starting transfers between devices, exchange(): return lax.all_to_all(parts, axis, 0, 0, tiled=True)  50 us
    all_to_all x6, waiting for transfers between devices, exchange(): return lax.all_to_all(parts, axis, 0, 0, tiled=True)  24.6 us
    ppermute x3, starting transfers between devices, over_tp(): lax.ppermute(loss, 'tp', [(i, i ^ bit) for i in range(tp_count)])  17.9 us
    ppermute x3, waiting for transfers between devices, over_tp(): lax.ppermute(loss, 'tp', [(i, i ^ bit) for i in range(tp_count)])  4.49 us
    pallas_call x1, Pallas kernels, on_device(): call(lambda *refs: student_kernel(2.0 / count_all, *refs), (parts_shape,...  4.08 us
    pallas_call x1, Pallas kernels, on_device(): call(grad_q_kernel, shape(2, heads // 2, half, width), (1000 * mega, 4 *...  4 us
    ppermute x1, starting transfers between devices, on_device(): lax.ppermute(jnp.concatenate([halo_keys, halo_values], axis=0), 'section'...  3.38 us
    ppermute x1, starting transfers between devices, on_device(): lax.ppermute(grad_q[1], 'section', [(i, i ^ 1) for i in range(count)])  3.38 us
  transfers between devices with their start and end apart: 11, of which 9 were waited for; matrix products, arithmetic and copies ran while one was open for 2% of the time, Pallas kernels for 9%

profile of v5, /device:TPU:6, one launch (start us, length us, event | category | flops | bytes accessed | tf_op | source)
XLA Modules:
  0.0 126.8 jit_solution(11232843005957497110)
XLA Ops:
  0.6 1.9 %own_state.1 = (f32[64,3,128]{2,1,0:T(4,128)}, f32[128,128]{1,0:T(8,128)S(1)}) custom-call(bf16[128,128]{1,0:T(8,128)(2,1)} %bitcast.25, bf16[128,128]{1,0:T(8,128)(2,1)} %bitcast.29, f32[1,64,128]{2,1,0:T(8,128)} %bitcast.37), custom_call_target="tpu_custom_call" | custom-call | flops 31457280 | bytes 524288 | tf_op jit(solution)/shard_map/own_state/pallas_call | solution.py:284
  2.5 0.0 copy-start.1
  2.5 0.0 copy-start.2
  2.5 12.7 %all-to-all-start = ((f32[64,3,128]{2,1,0:T(4,128)}), f32[64,3,128]{2,1,0:T(4,128)S(1)}, u32[]{:S(2)}, u32[]{:S(2)}) async-start(f32[64,3,128]{2,1,0:T(4,128)} %get-tuple-element.37), calls=%async_computation | async-start | bytes 262144 | tf_op jit(solution)/shard_map/states_out/all_to_all | solution.py:19
  15.2 0.0 copy-done.1
  15.2 0.0 copy-done.2
  15.3 3.4 %collective-permute-start = (bf16[256,128]{1,0:T(8,128)(2,1)S(1)}, bf16[256,128]{1,0:T(8,128)(2,1)S(1)}, u32[]{:S(2)}, u32[]{:S(2)}) collective-permute-start(bf16[256,128]{1,0:T(8,128)(2,1)S(1)} %pad_maximum_fusion), channel_id=1, source_target_pairs={{0,8},{8,16},{16,24},{24,32},{32,40},{40,48},{48,56},{56,64},{64,7... | collective-permute-start | bytes 196616 | tf_op jit(solution)/shard_map/ppermute | solution.py:290
  18.7 0.0 copy-start.3
  18.7 1.2 copy.9
  19.9 0.0 copy-start
  19.9 0.0 copy-done.3
  19.9 2.3 %query_feats.1 = (bf16[128,2048]{1,0:T(8,128)(2,1)}, bf16[128,2048]{1,0:T(8,128)(2,1)}) custom-call(bf16[2048,128]{1,0:T(8,128)(2,1)S(1)} %bitcast.21, f32[16,64,128]{2,1,0:T(8,128)S(1)} %bitcast.33), custom_call_target="tpu_custom_call" | custom-call | flops 629145600 | bytes 3145728 | tf_op jit(solution)/shard_map/query_feats/pallas_call | solution.py:298
  22.3 0.0 copy-start.4
  22.3 2.0 %all-to-all-done.refs_0_ = f32[64,3,128]{2,1,0:T(4,128)S(1)} async-done(((f32[64,3,128]{2,1,0:T(4,128)}), f32[64,3,128]{2,1,0:T(4,128)S(1)}, u32[]{:S(2)}, u32[]{:S(2)}) %all-to-all-start) | async-done | bytes 98336 | tf_op jit(solution)/shard_map/states_out/all_to_all | solution.py:19
  24.3 1.2 prefix.1
  25.5 0.0 collective-permute-done.halo_ref
  25.5 8.4 %all-to-all-start.1 = ((f32[64,3,128]{2,1,0:T(4,128)}), f32[64,3,128]{2,1,0:T(4,128)S(1)}, u32[]{:S(2)}, u32[]{:S(2)}) async-start(f32[64,3,128]{2,1,0:T(4,128)} %prefix.1), calls=%async_computation.1 | async-start | bytes 262144 | tf_op jit(solution)/shard_map/states_back/all_to_all | solution.py:19
  33.9 0.0 copy-done.4
  33.9 0.1 copy.10
  34.0 0.0 copy-done
  34.0 2.3 %window.1 = (f32[128,2048]{1,0:T(8,128)}, f32[1,2048]{1,0:T(1,128)}, bf16[128,2048]{1,0:T(8,128)(2,1)}) custom-call(bf16[2048,128]{1,0:T(8,128)(2,1)S(1)} %bitcast.22, bf16[128,128]{1,0:T(8,128)(2,1)S(1)} %bitcast.27, bf16[128,128]{1,0:T(8,128)(2,1)S(1)} %bitcast.31, bf16[256,128]{1,0:T(8,128)(2,1)S(1)} %collective-permute-done.halo_ref, ...), custom_call_target="tpu_custom_call" | custom-call | flops 2097152000 | bytes 8388608 | tf_op jit(solution)/shard_map/window/pallas_call | solution.py:317
  36.3 6.4 %all-to-all-done.1.refs_5_.state_ref = f32[64,3,128]{2,1,0:T(4,128)S(1)} async-done(((f32[64,3,128]{2,1,0:T(4,128)}), f32[64,3,128]{2,1,0:T(4,128)S(1)}, u32[]{:S(2)}, u32[]{:S(2)}) %all-to-all-start.1) | async-done | bytes 98336 | tf_op jit(solution)/shard_map/states_back/all_to_all | solution.py:19
  42.7 4.1 %student.1 = (f32[64,3,128]{2,1,0:T(4,128)}, bf16[128,2048]{1,0:T(8,128)(2,1)}, bf16[128,2048]{1,0:T(8,128)(2,1)}, f32[1,2048]{1,0:T(1,128)}) custom-call(bf16[128,2048]{1,0:T(8,128)(2,1)} %get-tuple-element.43.refs_0_.high_ref, bf16[128,2048]{1,0:T(8,128)(2,1)} %get-tuple-element.44.refs_1_.low_ref, f32[128,2048]{1,0:T(8,128)} %get-tuple-element.48.refs_2_, ...), custom_call_target="tpu_custom_call" | custom-call | flops 419430400 | bytes 4194304 | tf_op jit(solution)/shard_map/student/pallas_call | solution.py:327
  46.8 6.5 %all-to-all-start.2 = ((f32[64,3,128]{2,1,0:T(4,128)}), f32[64,3,128]{2,1,0:T(4,128)S(1)}, u32[]{:S(2)}, u32[]{:S(2)}) async-start(f32[64,3,128]{2,1,0:T(4,128)} %get-tuple-element.52), calls=%async_computation.2 | async-start | bytes 262144 | tf_op jit(solution)/shard_map/grads_out/all_to_all | solution.py:19
  53.3 4.0 %grad_q.1.query_ref = f32[2,8,64,128]{3,2,1,0:T(8,128)S(1)} custom-call(bf16[128,2048]{1,0:T(8,128)(2,1)} %get-tuple-element.43.refs_0_.high_ref, bf16[128,2048]{1,0:T(8,128)(2,1)} %get-tuple-element.44.refs_1_.low_ref, bf16[128,2048]{1,0:T(8,128)(2,1)} %get-tuple-element.53.grad_high_ref, bf16[128,2048]{1,0:T(8,128)(2,1)} %get-tuple-element.54.grad_low_ref, ...), custom_call_target="tpu_custom_call" | custom-call | flops 1048576000 | bytes 4194304 | tf_op jit(solution)/shard_map/grad_q/pallas_call | solution.py:335
  57.3 3.4 %collective-permute-start.2 = (f32[8,64,128]{2,1,0:T(8,128)S(1)}, f32[8,64,128]{2,1,0:T(8,128)S(1)}, u32[]{:S(2)}, u32[]{:S(2)}) collective-permute-start(f32[8,64,128]{2,1,0:T(8,128)S(1)} %slice_bitcast_fusion), channel_id=1, source_target_pairs={{0,8},{8,0},{16,24},{24,16},{32,40},{40,32},{48,56},{56,48},{64,72... | collective-permute-start | bytes 786440 | tf_op jit(solution)/shard_map/grad_q_swap/ppermute | solution.py:345
  60.7 1.4 %all-to-all-done.2.refs_0_ = f32[64,3,128]{2,1,0:T(4,128)S(1)} async-done(((f32[64,3,128]{2,1,0:T(4,128)}), f32[64,3,128]{2,1,0:T(4,128)S(1)}, u32[]{:S(2)}, u32[]{:S(2)}) %all-to-all-start.2) | async-done | bytes 98336 | tf_op jit(solution)/shard_map/grads_out/all_to_all | solution.py:19
  62.1 1.2 suffix.1
  63.3 9.0 %all-to-all-start.3 = ((f32[64,3,128]{2,1,0:T(4,128)}), f32[64,3,128]{2,1,0:T(4,128)S(1)}, u32[]{:S(2)}, u32[]{:S(2)}) async-start(f32[64,3,128]{2,1,0:T(4,128)} %get-tuple-element.57), calls=%async_computation.3 | async-start | bytes 262144 | tf_op jit(solution)/shard_map/grads_back/all_to_all | solution.py:19
  72.3 1.9 %collective-permute-start.1 = (f32[8,128]{1,0:T(8,128)S(1)}, f32[8,128]{1,0:T(8,128)S(1)}, u32[]{:S(2)}, u32[]{:S(2)}) collective-permute-start(f32[8,128]{1,0:T(8,128)S(1)} %get-tuple-element.58), channel_id=1, source_target_pairs={{0,1},{1,0},{2,3},{3,2},{4,5},{5,4},{6,7},{7,6},{8,9},{9,8},{10,11... | collective-permute-start | bytes 12296 | tf_op jit(solution)/shard_map/loss_core/ppermute | solution.py:356
  74.2 1.1 collective-permute-done.1
  75.3 5.7 %all-to-all-done.3.state_ref = f32[64,3,128]{2,1,0:T(4,128)S(1)} async-done(((f32[64,3,128]{2,1,0:T(4,128)}), f32[64,3,128]{2,1,0:T(4,128)S(1)}, u32[]{:S(2)}, u32[]{:S(2)}) %all-to-all-start.3) | async-done | bytes 98336 | tf_op jit(solution)/shard_map/grads_back/all_to_all | solution.py:19
  81.0 0.0 collective-permute-done.2.other_ref
  81.1 1.2 grad_k.1
  82.3 6.5 %all-to-all-start.4 = ((f32[320,2,128]{2,1,0:T(2,128)}), f32[320,2,128]{2,1,0:T(2,128)S(1)}, u32[]{:S(2)}, u32[]{:S(2)}) async-start(f32[320,2,128]{2,1,0:T(2,128)} %bitcast.9), calls=%async_computation.4 | async-start | bytes 655360 | tf_op jit(solution)/shard_map/maps_out/all_to_all | solution.py:19
  88.8 6.1 %collective-permute-start.3 = (f32[8,128]{1,0:T(8,128)S(1)}, f32[8,128]{1,0:T(8,128)S(1)}, u32[]{:S(2)}, u32[]{:S(2)}) collective-permute-start(f32[8,128]{1,0:T(8,128)S(1)} %add.9), channel_id=1, source_target_pairs={{0,2},{1,3},{2,0},{3,1},{4,6},{5,7},{6,4},{7,5},{8,10},{9,11},{10,... | collective-permute-start | bytes 12296 | tf_op jit(solution)/shard_map/loss_near/ppermute | solution.py:356
  94.9 1.6 %collective-permute-done.3 = f32[8,128]{1,0:T(8,128)S(1)} collective-permute-done((f32[8,128]{1,0:T(8,128)S(1)}, f32[8,128]{1,0:T(8,128)S(1)}, u32[]{:S(2)}, u32[]{:S(2)}) %collective-permute-start.3) | collective-permute-done | bytes 4128 | tf_op jit(solution)/shard_map/loss_near/ppermute | solution.py:356
  96.5 4.3 %all-to-all-done.4 = f32[320,2,128]{2,1,0:T(2,128)S(1)} async-done(((f32[320,2,128]{2,1,0:T(2,128)}), f32[320,2,128]{2,1,0:T(2,128)S(1)}, u32[]{:S(2)}, u32[]{:S(2)}) %all-to-all-start.4) | async-done | bytes 327712 | tf_op jit(solution)/shard_map/maps_out/all_to_all | solution.py:19
  100.8 1.1 maps_out.1
  101.9 6.9 %all-to-all-start.5 = ((f32[576,2,128]{2,1,0:T(2,128)}), f32[576,2,128]{2,1,0:T(2,128)S(1)}, u32[]{:S(2)}, u32[]{:S(2)}) async-start(f32[576,2,128]{2,1,0:T(2,128)} %bitcast.11), calls=%async_computation.5 | async-start | bytes 1179648 | tf_op jit(solution)/shard_map/maps_back/all_to_all | solution.py:19
  108.8 9.9 %collective-permute-start.4 = (f32[8,128]{1,0:T(8,128)S(1)}, f32[8,128]{1,0:T(8,128)S(1)}, u32[]{:S(2)}, u32[]{:S(2)}) collective-permute-start(f32[8,128]{1,0:T(8,128)S(1)} %add.10), channel_id=1, source_target_pairs={{0,4},{1,5},{2,6},{3,7},{4,0},{5,1},{6,2},{7,3},{8,12},{9,13},{10,... | collective-permute-start | bytes 12296 | tf_op jit(solution)/shard_map/loss_far/ppermute | solution.py:356
  118.7 1.8 %collective-permute-done.4 = f32[8,128]{1,0:T(8,128)S(1)} collective-permute-done((f32[8,128]{1,0:T(8,128)S(1)}, f32[8,128]{1,0:T(8,128)S(1)}, u32[]{:S(2)}, u32[]{:S(2)}) %collective-permute-start.4) | collective-permute-done | bytes 4128 | tf_op jit(solution)/shard_map/loss_far/ppermute | solution.py:356
  120.4 0.5 slice.7
  121.0 4.8 %all-to-all-done.5 = f32[576,2,128]{2,1,0:T(2,128)S(1)} async-done(((f32[576,2,128]{2,1,0:T(2,128)}), f32[576,2,128]{2,1,0:T(2,128)S(1)}, u32[]{:S(2)}, u32[]{:S(2)}) %all-to-all-start.5) | async-done | bytes 589856 | tf_op jit(solution)/shard_map/maps_back/all_to_all | solution.py:19
  125.7 1.1 maps_back.1
  (5 shorter events, 0.0 us)
Async XLA Ops:
  2.5 12.8 %copy-start.1 = (bf16[128,1,128]{2,0,1:T(8,128)(2,1)S(1)}, bf16[128,1,128]{2,0,1:T(8,128)(2,1)}, u32[]{:S(2)}) copy-start(bf16[128,1,128]{2,0,1:T(8,128)(2,1)} %param.7) | copy-start | bytes 98308
  2.5 12.8 %copy-start.2 = (bf16[128,1,128]{2,0,1:T(8,128)(2,1)S(1)}, bf16[128,1,128]{2,0,1:T(8,128)(2,1)}, u32[]{:S(2)}) copy-start(bf16[128,1,128]{2,0,1:T(8,128)(2,1)} %param.8) | copy-start | bytes 98308
  2.5 21.8 %all-to-all-start = ((f32[64,3,128]{2,1,0:T(4,128)}), f32[64,3,128]{2,1,0:T(4,128)S(1)}, u32[]{:S(2)}, u32[]{:S(2)}) async-start(f32[64,3,128]{2,1,0:T(4,128)} %get-tuple-element.37), calls=%async_computation | async-start | bytes 262144 | tf_op jit(solution)/shard_map/states_out/all_to_all | solution.py:19
  15.3 10.2 %collective-permute-start = (bf16[256,128]{1,0:T(8,128)(2,1)S(1)}, bf16[256,128]{1,0:T(8,128)(2,1)S(1)}, u32[]{:S(2)}, u32[]{:S(2)}) collective-permute-start(bf16[256,128]{1,0:T(8,128)(2,1)S(1)} %pad_maximum_fusion), channel_id=1, source_target_pairs={{0,8},{8,16},{16,24},{24,32},{32,40},{40,48},{48,56},{56,64},{64,7... | collective-permute-start | bytes 196616 | tf_op jit(solution)/shard_map/ppermute | solution.py:290
  18.7 1.3 copy-start.3
  19.9 14.1 %copy-start = (bf16[16,128,128]{2,1,0:T(8,128)(2,1)}, bf16[16,128,128]{2,1,0:T(8,128)(2,1)S(1)}, u32[]{:S(2)}) copy-start(bf16[16,128,128]{2,1,0:T(8,128)(2,1)S(1)} %copy.9) | copy-start | bytes 1572868
  22.3 11.6 %copy-start.4 = (bf16[128,16,128]{2,1,0:T(8,128)(2,1)S(1)}, bf16[128,16,128]{2,1,0:T(8,128)(2,1)}, u32[]{:S(2)}) copy-start(bf16[128,16,128]{2,1,0:T(8,128)(2,1)} %param.9) | copy-start | bytes 1572868
  25.5 17.2 %all-to-all-start.1 = ((f32[64,3,128]{2,1,0:T(4,128)}), f32[64,3,128]{2,1,0:T(4,128)S(1)}, u32[]{:S(2)}, u32[]{:S(2)}) async-start(f32[64,3,128]{2,1,0:T(4,128)} %prefix.1), calls=%async_computation.1 | async-start | bytes 262144 | tf_op jit(solution)/shard_map/states_back/all_to_all | solution.py:19
  46.8 15.3 %all-to-all-start.2 = ((f32[64,3,128]{2,1,0:T(4,128)}), f32[64,3,128]{2,1,0:T(4,128)S(1)}, u32[]{:S(2)}, u32[]{:S(2)}) async-start(f32[64,3,128]{2,1,0:T(4,128)} %get-tuple-element.52), calls=%async_computation.2 | async-start | bytes 262144 | tf_op jit(solution)/shard_map/grads_out/all_to_all | solution.py:19
  57.3 23.7 %collective-permute-start.2 = (f32[8,64,128]{2,1,0:T(8,128)S(1)}, f32[8,64,128]{2,1,0:T(8,128)S(1)}, u32[]{:S(2)}, u32[]{:S(2)}) collective-permute-start(f32[8,64,128]{2,1,0:T(8,128)S(1)} %slice_bitcast_fusion), channel_id=1, source_target_pairs={{0,8},{8,0},{16,24},{24,16},{32,40},{40,32},{48,56},{56,48},{64,72... | collective-permute-start | bytes 786440 | tf_op jit(solution)/shard_map/grad_q_swap/ppermute | solution.py:345
  63.3 17.8 %all-to-all-start.3 = ((f32[64,3,128]{2,1,0:T(4,128)}), f32[64,3,128]{2,1,0:T(4,128)S(1)}, u32[]{:S(2)}, u32[]{:S(2)}) async-start(f32[64,3,128]{2,1,0:T(4,128)} %get-tuple-element.57), calls=%async_computation.3 | async-start | bytes 262144 | tf_op jit(solution)/shard_map/grads_back/all_to_all | solution.py:19
  72.3 3.1 %collective-permute-start.1 = (f32[8,128]{1,0:T(8,128)S(1)}, f32[8,128]{1,0:T(8,128)S(1)}, u32[]{:S(2)}, u32[]{:S(2)}) collective-permute-start(f32[8,128]{1,0:T(8,128)S(1)} %get-tuple-element.58), channel_id=1, source_target_pairs={{0,1},{1,0},{2,3},{3,2},{4,5},{5,4},{6,7},{7,6},{8,9},{9,8},{10,11... | collective-permute-start | bytes 12296 | tf_op jit(solution)/shard_map/loss_core/ppermute | solution.py:356
  82.3 18.5 %all-to-all-start.4 = ((f32[320,2,128]{2,1,0:T(2,128)}), f32[320,2,128]{2,1,0:T(2,128)S(1)}, u32[]{:S(2)}, u32[]{:S(2)}) async-start(f32[320,2,128]{2,1,0:T(2,128)} %bitcast.9), calls=%async_computation.4 | async-start | bytes 655360 | tf_op jit(solution)/shard_map/maps_out/all_to_all | solution.py:19
  88.8 7.7 %collective-permute-start.3 = (f32[8,128]{1,0:T(8,128)S(1)}, f32[8,128]{1,0:T(8,128)S(1)}, u32[]{:S(2)}, u32[]{:S(2)}) collective-permute-start(f32[8,128]{1,0:T(8,128)S(1)} %add.9), channel_id=1, source_target_pairs={{0,2},{1,3},{2,0},{3,1},{4,6},{5,7},{6,4},{7,5},{8,10},{9,11},{10,... | collective-permute-start | bytes 12296 | tf_op jit(solution)/shard_map/loss_near/ppermute | solution.py:356
  101.9 23.9 %all-to-all-start.5 = ((f32[576,2,128]{2,1,0:T(2,128)}), f32[576,2,128]{2,1,0:T(2,128)S(1)}, u32[]{:S(2)}, u32[]{:S(2)}) async-start(f32[576,2,128]{2,1,0:T(2,128)} %bitcast.11), calls=%async_computation.5 | async-start | bytes 1179648 | tf_op jit(solution)/shard_map/maps_back/all_to_all | solution.py:19
  108.8 11.6 %collective-permute-start.4 = (f32[8,128]{1,0:T(8,128)S(1)}, f32[8,128]{1,0:T(8,128)S(1)}, u32[]{:S(2)}, u32[]{:S(2)}) collective-permute-start(f32[8,128]{1,0:T(8,128)S(1)} %add.10), channel_id=1, source_target_pairs={{0,4},{1,5},{2,6},{3,7},{4,0},{5,1},{6,2},{7,3},{8,12},{9,13},{10,... | collective-permute-start | bytes 12296 | tf_op jit(solution)/shard_map/loss_far/ppermute | solution.py:356

commit v6 on v5

--- a/solution.py
+++ b/solution.py
@@ -355,9 +355,6 @@
     def over_tp(loss, bit):
         return loss + lax.ppermute(loss, "tp", [(i, i ^ bit) for i in range(tp_count)])
 
-    with jax.named_scope("loss_core"):
-        loss = over_tp(loss, 1)
-        later, loss = lax.optimization_barrier((later, loss))
     sent_shape = shape(count, heads // 4 + 1, 2, width)
     maps_shape = shape(count, heads // 2 + 1, 2, width)
 
@@ -376,7 +373,7 @@
         sums = call(total_kernel, maps_shape, (mega, mega))(parts)
         sums, loss = lax.optimization_barrier((sums, loss))
     with jax.named_scope("loss_far"):
-        loss = over_tp(loss, 4)
+        loss = over_tp(over_tp(loss, 1), 4)
     with jax.named_scope("maps_back"):
         grad_q, grad_k = call(
             finish_kernel, (shape(heads, half, width), shape(half, width)), (mega, mega)

time: 129 us -> 125 us (0.969)
  waiting for transfers between devices: 29 us -> 25.6 us
    all_to_all x6, waiting for transfers between devices: 24.6 us -> 21.2 us  [exchange(): return lax.all_to_all(parts, axis, 0, 0, tiled=True)]
    all_to_all x6, starting transfers between devices: 50 us -> 51.6 us  [exchange(): return lax.all_to_all(parts, axis, 0, 0, tiled=True)]
  transfers between devices with their start and end apart: 11 -> 11, of which waited for: 9 -> 8; matrix products, arithmetic and copies ran while one was open for 2% -> 2% of each run, Pallas kernels for 9% -> 9%
where the time goes in v6:
time: 125 us; the launch traced here: 124 us
  starting transfers between devices  75.2 us (60%)
  waiting for transfers between devices  25.6 us (20%)
  Pallas kernels  20.3 us (16%)
  local copies, waits for them, and re-layouts  1.93 us (2%)
    all_to_all x6, starting transfers between devices, exchange(): return lax.all_to_all(parts, axis, 0, 0, tiled=True)  51.6 us
    all_to_all x6, waiting for transfers between devices, exchange(): return lax.all_to_all(parts, axis, 0, 0, tiled=True)  21.2 us
    ppermute x3, starting transfers between devices, over_tp(): lax.ppermute(loss, 'tp', [(i, i ^ bit) for i in range(tp_count)])  16.8 us
    ppermute x3, waiting for transfers between devices, over_tp(): lax.ppermute(loss, 'tp', [(i, i ^ bit) for i in range(tp_count)])  4.33 us
    pallas_call x1, Pallas kernels, on_device(): call(lambda *refs: student_kernel(2.0 / count_all, *refs), (parts_shape,...  4.08 us
    pallas_call x1, Pallas kernels, on_device(): call(grad_q_kernel, shape(2, heads // 2, half, width), (1000 * mega, 4 *...  4 us
    ppermute x1, starting transfers between devices, on_device(): lax.ppermute(jnp.concatenate([halo_keys, halo_values], axis=0), 'section'...  3.38 us
    ppermute x1, starting transfers between devices, on_device(): lax.ppermute(grad_q[1], 'section', [(i, i ^ 1) for i in range(count)])  3.38 us
  transfers between devices with their start and end apart: 11, of which 8 were waited for; matrix products, arithmetic and copies ran while one was open for 2% of the time, Pallas kernels for 9%

profile of v6, /device:TPU:6, one launch (start us, length us, event | category | flops | bytes accessed | tf_op | source)
XLA Modules:
  0.0 123.8 jit_solution(16027361919759129287)
XLA Ops:
  0.6 1.9 %own_state.1 = (f32[64,3,128]{2,1,0:T(4,128)}, f32[128,128]{1,0:T(8,128)S(1)}) custom-call(bf16[128,128]{1,0:T(8,128)(2,1)} %bitcast.25, bf16[128,128]{1,0:T(8,128)(2,1)} %bitcast.29, f32[1,64,128]{2,1,0:T(8,128)} %bitcast.37), custom_call_target="tpu_custom_call" | custom-call | flops 31457280 | bytes 524288 | tf_op jit(solution)/shard_map/own_state/pallas_call | solution.py:284
  2.5 0.0 copy-start.1
  2.5 0.0 copy-start.2
  2.5 12.7 %all-to-all-start = ((f32[64,3,128]{2,1,0:T(4,128)}), f32[64,3,128]{2,1,0:T(4,128)S(1)}, u32[]{:S(2)}, u32[]{:S(2)}) async-start(f32[64,3,128]{2,1,0:T(4,128)} %get-tuple-element.35), calls=%async_computation | async-start | bytes 262144 | tf_op jit(solution)/shard_map/states_out/all_to_all | solution.py:19
  15.2 0.0 copy-done.1
  15.2 0.0 copy-done.2
  15.3 3.4 %collective-permute-start = (bf16[256,128]{1,0:T(8,128)(2,1)S(1)}, bf16[256,128]{1,0:T(8,128)(2,1)S(1)}, u32[]{:S(2)}, u32[]{:S(2)}) collective-permute-start(bf16[256,128]{1,0:T(8,128)(2,1)S(1)} %pad_maximum_fusion), channel_id=1, source_target_pairs={{0,8},{8,16},{16,24},{24,32},{32,40},{40,48},{48,56},{56,64},{64,7... | collective-permute-start | bytes 196616 | tf_op jit(solution)/shard_map/ppermute | solution.py:290
  18.7 0.0 copy-start.3
  18.7 1.2 copy.9
  19.9 0.0 copy-start
  19.9 0.0 copy-done.3
  19.9 2.3 %query_feats.1 = (bf16[128,2048]{1,0:T(8,128)(2,1)}, bf16[128,2048]{1,0:T(8,128)(2,1)}) custom-call(bf16[2048,128]{1,0:T(8,128)(2,1)S(1)} %bitcast.21, f32[16,64,128]{2,1,0:T(8,128)S(1)} %bitcast.33), custom_call_target="tpu_custom_call" | custom-call | flops 629145600 | bytes 3145728 | tf_op jit(solution)/shard_map/query_feats/pallas_call | solution.py:298
  22.3 0.0 copy-start.4
  22.3 2.0 %all-to-all-done.refs_0_ = f32[64,3,128]{2,1,0:T(4,128)S(1)} async-done(((f32[64,3,128]{2,1,0:T(4,128)}), f32[64,3,128]{2,1,0:T(4,128)S(1)}, u32[]{:S(2)}, u32[]{:S(2)}) %all-to-all-start) | async-done | bytes 98336 | tf_op jit(solution)/shard_map/states_out/all_to_all | solution.py:19
  24.3 1.2 prefix.1
  25.5 0.0 collective-permute-done.halo_ref
  25.5 8.4 %all-to-all-start.1 = ((f32[64,3,128]{2,1,0:T(4,128)}), f32[64,3,128]{2,1,0:T(4,128)S(1)}, u32[]{:S(2)}, u32[]{:S(2)}) async-start(f32[64,3,128]{2,1,0:T(4,128)} %prefix.1), calls=%async_computation.1 | async-start | bytes 262144 | tf_op jit(solution)/shard_map/states_back/all_to_all | solution.py:19
  33.9 0.0 copy-done.4
  33.9 0.1 copy.10
  34.0 0.0 copy-done
  34.0 2.3 %window.1 = (f32[128,2048]{1,0:T(8,128)}, f32[1,2048]{1,0:T(1,128)}, bf16[128,2048]{1,0:T(8,128)(2,1)}) custom-call(bf16[2048,128]{1,0:T(8,128)(2,1)S(1)} %bitcast.22, bf16[128,128]{1,0:T(8,128)(2,1)S(1)} %bitcast.27, bf16[128,128]{1,0:T(8,128)(2,1)S(1)} %bitcast.31, bf16[256,128]{1,0:T(8,128)(2,1)S(1)} %collective-permute-done.halo_ref, ...), custom_call_target="tpu_custom_call" | custom-call | flops 2097152000 | bytes 8388608 | tf_op jit(solution)/shard_map/window/pallas_call | solution.py:317
  36.3 6.4 %all-to-all-done.1.refs_5_.state_ref = f32[64,3,128]{2,1,0:T(4,128)S(1)} async-done(((f32[64,3,128]{2,1,0:T(4,128)}), f32[64,3,128]{2,1,0:T(4,128)S(1)}, u32[]{:S(2)}, u32[]{:S(2)}) %all-to-all-start.1) | async-done | bytes 98336 | tf_op jit(solution)/shard_map/states_back/all_to_all | solution.py:19
  42.7 4.1 %student.1 = (f32[64,3,128]{2,1,0:T(4,128)}, bf16[128,2048]{1,0:T(8,128)(2,1)}, bf16[128,2048]{1,0:T(8,128)(2,1)}, f32[1,2048]{1,0:T(1,128)}) custom-call(bf16[128,2048]{1,0:T(8,128)(2,1)} %get-tuple-element.41.refs_0_.high_ref, bf16[128,2048]{1,0:T(8,128)(2,1)} %get-tuple-element.42.refs_1_.low_ref, f32[128,2048]{1,0:T(8,128)} %get-tuple-element.46.refs_2_, ...), custom_call_target="tpu_custom_call" | custom-call | flops 419430400 | bytes 4194304 | tf_op jit(solution)/shard_map/student/pallas_call | solution.py:327
  46.8 6.5 %all-to-all-start.2 = ((f32[64,3,128]{2,1,0:T(4,128)}), f32[64,3,128]{2,1,0:T(4,128)S(1)}, u32[]{:S(2)}, u32[]{:S(2)}) async-start(f32[64,3,128]{2,1,0:T(4,128)} %get-tuple-element.50), calls=%async_computation.2 | async-start | bytes 262144 | tf_op jit(solution)/shard_map/grads_out/all_to_all | solution.py:19
  53.3 4.0 %grad_q.1.query_ref = f32[2,8,64,128]{3,2,1,0:T(8,128)S(1)} custom-call(bf16[128,2048]{1,0:T(8,128)(2,1)} %get-tuple-element.41.refs_0_.high_ref, bf16[128,2048]{1,0:T(8,128)(2,1)} %get-tuple-element.42.refs_1_.low_ref, bf16[128,2048]{1,0:T(8,128)(2,1)} %get-tuple-element.51.grad_high_ref, bf16[128,2048]{1,0:T(8,128)(2,1)} %get-tuple-element.52.grad_low_ref, ...), custom_call_target="tpu_custom_call" | custom-call | flops 1048576000 | bytes 4194304 | tf_op jit(solution)/shard_map/grad_q/pallas_call | solution.py:335
  57.3 3.4 %collective-permute-start.1 = (f32[8,64,128]{2,1,0:T(8,128)S(1)}, f32[8,64,128]{2,1,0:T(8,128)S(1)}, u32[]{:S(2)}, u32[]{:S(2)}) collective-permute-start(f32[8,64,128]{2,1,0:T(8,128)S(1)} %slice_bitcast_fusion), channel_id=1, source_target_pairs={{0,8},{8,0},{16,24},{24,16},{32,40},{40,32},{48,56},{56,48},{64,72... | collective-permute-start | bytes 786440 | tf_op jit(solution)/shard_map/grad_q_swap/ppermute | solution.py:345
  60.7 1.4 %all-to-all-done.2.refs_0_ = f32[64,3,128]{2,1,0:T(4,128)S(1)} async-done(((f32[64,3,128]{2,1,0:T(4,128)}), f32[64,3,128]{2,1,0:T(4,128)S(1)}, u32[]{:S(2)}, u32[]{:S(2)}) %all-to-all-start.2) | async-done | bytes 98336 | tf_op jit(solution)/shard_map/grads_out/all_to_all | solution.py:19
  62.1 1.2 suffix.1
  63.3 9.0 %all-to-all-start.3 = ((f32[64,3,128]{2,1,0:T(4,128)}), f32[64,3,128]{2,1,0:T(4,128)S(1)}, u32[]{:S(2)}, u32[]{:S(2)}) async-start(f32[64,3,128]{2,1,0:T(4,128)} %get-tuple-element.55), calls=%async_computation.3 | async-start | bytes 262144 | tf_op jit(solution)/shard_map/grads_back/all_to_all | solution.py:19
  72.3 0.0 collective-permute-done.1.other_ref
  72.3 8.8 %all-to-all-done.3.state_ref = f32[64,3,128]{2,1,0:T(4,128)S(1)} async-done(((f32[64,3,128]{2,1,0:T(4,128)}), f32[64,3,128]{2,1,0:T(4,128)S(1)}, u32[]{:S(2)}, u32[]{:S(2)}) %all-to-all-start.3) | async-done | bytes 98336 | tf_op jit(solution)/shard_map/grads_back/all_to_all | solution.py:19
  81.0 1.2 grad_k.1
  82.3 6.5 %all-to-all-start.4 = ((f32[320,2,128]{2,1,0:T(2,128)}), f32[320,2,128]{2,1,0:T(2,128)S(1)}, u32[]{:S(2)}, u32[]{:S(2)}) async-start(f32[320,2,128]{2,1,0:T(2,128)} %bitcast.9), calls=%async_computation.4 | async-start | bytes 655360 | tf_op jit(solution)/shard_map/maps_out/all_to_all | solution.py:19
  88.8 6.1 %collective-permute-start.2 = (f32[8,128]{1,0:T(8,128)S(1)}, f32[8,128]{1,0:T(8,128)S(1)}, u32[]{:S(2)}, u32[]{:S(2)}) collective-permute-start(f32[8,128]{1,0:T(8,128)S(1)} %get-tuple-element.60), channel_id=1, source_target_pairs={{0,2},{1,3},{2,0},{3,1},{4,6},{5,7},{6,4},{7,5},{8,10},{9,11},{10,... | collective-permute-start | bytes 12296 | tf_op jit(solution)/shard_map/loss_near/ppermute | solution.py:356
  94.9 1.6 %collective-permute-done.2 = f32[8,128]{1,0:T(8,128)S(1)} collective-permute-done((f32[8,128]{1,0:T(8,128)S(1)}, f32[8,128]{1,0:T(8,128)S(1)}, u32[]{:S(2)}, u32[]{:S(2)}) %collective-permute-start.2) | collective-permute-done | bytes 4128 | tf_op jit(solution)/shard_map/loss_near/ppermute | solution.py:356
  96.5 2.7 %all-to-all-done.4 = f32[320,2,128]{2,1,0:T(2,128)S(1)} async-done(((f32[320,2,128]{2,1,0:T(2,128)}), f32[320,2,128]{2,1,0:T(2,128)S(1)}, u32[]{:S(2)}, u32[]{:S(2)}) %all-to-all-start.4) | async-done | bytes 327712 | tf_op jit(solution)/shard_map/maps_out/all_to_all | solution.py:19
  99.2 1.1 maps_out.1
  100.2 8.5 %all-to-all-start.5 = ((f32[576,2,128]{2,1,0:T(2,128)}), f32[576,2,128]{2,1,0:T(2,128)S(1)}, u32[]{:S(2)}, u32[]{:S(2)}) async-start(f32[576,2,128]{2,1,0:T(2,128)} %bitcast.11), calls=%async_computation.5 | async-start | bytes 1179648 | tf_op jit(solution)/shard_map/maps_back/all_to_all | solution.py:19
  108.8 1.9 %collective-permute-start.3 = (f32[8,128]{1,0:T(8,128)S(1)}, f32[8,128]{1,0:T(8,128)S(1)}, u32[]{:S(2)}, u32[]{:S(2)}) collective-permute-start(f32[8,128]{1,0:T(8,128)S(1)} %add.9), channel_id=1, source_target_pairs={{0,1},{1,0},{2,3},{3,2},{4,5},{5,4},{6,7},{7,6},{8,9},{9,8},{10,11... | collective-permute-start | bytes 12296 | tf_op jit(solution)/shard_map/loss_far/ppermute | solution.py:356
  110.7 1.1 collective-permute-done.3
  111.8 8.8 %collective-permute-start.4 = (f32[8,128]{1,0:T(8,128)S(1)}, f32[8,128]{1,0:T(8,128)S(1)}, u32[]{:S(2)}, u32[]{:S(2)}) collective-permute-start(f32[8,128]{1,0:T(8,128)S(1)} %add.10), channel_id=1, source_target_pairs={{0,4},{1,5},{2,6},{3,7},{4,0},{5,1},{6,2},{7,3},{8,12},{9,13},{10,... | collective-permute-start | bytes 12296 | tf_op jit(solution)/shard_map/loss_far/ppermute | solution.py:356
  120.6 1.6 %collective-permute-done.4 = f32[8,128]{1,0:T(8,128)S(1)} collective-permute-done((f32[8,128]{1,0:T(8,128)S(1)}, f32[8,128]{1,0:T(8,128)S(1)}, u32[]{:S(2)}, u32[]{:S(2)}) %collective-permute-start.4) | collective-permute-done | bytes 4128 | tf_op jit(solution)/shard_map/loss_far/ppermute | solution.py:356
  122.2 0.5 slice.7
  122.8 0.0 all-to-all-done.5
  122.8 1.1 maps_back.1
  (5 shorter events, 0.0 us)
Async XLA Ops:
  2.5 12.8 %copy-start.1 = (bf16[128,1,128]{2,0,1:T(8,128)(2,1)S(1)}, bf16[128,1,128]{2,0,1:T(8,128)(2,1)}, u32[]{:S(2)}) copy-start(bf16[128,1,128]{2,0,1:T(8,128)(2,1)} %param.7) | copy-start | bytes 98308
  2.5 12.8 %copy-start.2 = (bf16[128,1,128]{2,0,1:T(8,128)(2,1)S(1)}, bf16[128,1,128]{2,0,1:T(8,128)(2,1)}, u32[]{:S(2)}) copy-start(bf16[128,1,128]{2,0,1:T(8,128)(2,1)} %param.8) | copy-start | bytes 98308
  2.5 21.8 %all-to-all-start = ((f32[64,3,128]{2,1,0:T(4,128)}), f32[64,3,128]{2,1,0:T(4,128)S(1)}, u32[]{:S(2)}, u32[]{:S(2)}) async-start(f32[64,3,128]{2,1,0:T(4,128)} %get-tuple-element.35), calls=%async_computation | async-start | bytes 262144 | tf_op jit(solution)/shard_map/states_out/all_to_all | solution.py:19
  15.3 10.2 %collective-permute-start = (bf16[256,128]{1,0:T(8,128)(2,1)S(1)}, bf16[256,128]{1,0:T(8,128)(2,1)S(1)}, u32[]{:S(2)}, u32[]{:S(2)}) collective-permute-start(bf16[256,128]{1,0:T(8,128)(2,1)S(1)} %pad_maximum_fusion), channel_id=1, source_target_pairs={{0,8},{8,16},{16,24},{24,32},{32,40},{40,48},{48,56},{56,64},{64,7... | collective-permute-start | bytes 196616 | tf_op jit(solution)/shard_map/ppermute | solution.py:290
  18.7 1.3 %copy-start.3 = (f32[16,128,64]{1,2,0:T(8,128)S(1)}, f32[16,128,64]{1,2,0:T(8,128)}, u32[]{:S(2)}) copy-start(f32[16,128,64]{1,2,0:T(8,128)} %param.10) | copy-start | bytes 1572868
  19.9 14.1 %copy-start = (bf16[16,128,128]{2,1,0:T(8,128)(2,1)}, bf16[16,128,128]{2,1,0:T(8,128)(2,1)S(1)}, u32[]{:S(2)}) copy-start(bf16[16,128,128]{2,1,0:T(8,128)(2,1)S(1)} %copy.9) | copy-start | bytes 1572868
  22.3 11.6 %copy-start.4 = (bf16[128,16,128]{2,1,0:T(8,128)(2,1)S(1)}, bf16[128,16,128]{2,1,0:T(8,128)(2,1)}, u32[]{:S(2)}) copy-start(bf16[128,16,128]{2,1,0:T(8,128)(2,1)} %param.9) | copy-start | bytes 1572868
  25.5 17.2 %all-to-all-start.1 = ((f32[64,3,128]{2,1,0:T(4,128)}), f32[64,3,128]{2,1,0:T(4,128)S(1)}, u32[]{:S(2)}, u32[]{:S(2)}) async-start(f32[64,3,128]{2,1,0:T(4,128)} %prefix.1), calls=%async_computation.1 | async-start | bytes 262144 | tf_op jit(solution)/shard_map/states_back/all_to_all | solution.py:19
  46.8 15.3 %all-to-all-start.2 = ((f32[64,3,128]{2,1,0:T(4,128)}), f32[64,3,128]{2,1,0:T(4,128)S(1)}, u32[]{:S(2)}, u32[]{:S(2)}) async-start(f32[64,3,128]{2,1,0:T(4,128)} %get-tuple-element.50), calls=%async_computation.2 | async-start | bytes 262144 | tf_op jit(solution)/shard_map/grads_out/all_to_all | solution.py:19
  57.3 14.9 %collective-permute-start.1 = (f32[8,64,128]{2,1,0:T(8,128)S(1)}, f32[8,64,128]{2,1,0:T(8,128)S(1)}, u32[]{:S(2)}, u32[]{:S(2)}) collective-permute-start(f32[8,64,128]{2,1,0:T(8,128)S(1)} %slice_bitcast_fusion), channel_id=1, source_target_pairs={{0,8},{8,0},{16,24},{24,16},{32,40},{40,32},{48,56},{56,48},{64,72... | collective-permute-start | bytes 786440 | tf_op jit(solution)/shard_map/grad_q_swap/ppermute | solution.py:345
  63.3 17.8 %all-to-all-start.3 = ((f32[64,3,128]{2,1,0:T(4,128)}), f32[64,3,128]{2,1,0:T(4,128)S(1)}, u32[]{:S(2)}, u32[]{:S(2)}) async-start(f32[64,3,128]{2,1,0:T(4,128)} %get-tuple-element.55), calls=%async_computation.3 | async-start | bytes 262144 | tf_op jit(solution)/shard_map/grads_back/all_to_all | solution.py:19
  82.3 16.9 %all-to-all-start.4 = ((f32[320,2,128]{2,1,0:T(2,128)}), f32[320,2,128]{2,1,0:T(2,128)S(1)}, u32[]{:S(2)}, u32[]{:S(2)}) async-start(f32[320,2,128]{2,1,0:T(2,128)} %bitcast.9), calls=%async_computation.4 | async-start | bytes 655360 | tf_op jit(solution)/shard_map/maps_out/all_to_all | solution.py:19
  88.8 7.7 %collective-permute-start.2 = (f32[8,128]{1,0:T(8,128)S(1)}, f32[8,128]{1,0:T(8,128)S(1)}, u32[]{:S(2)}, u32[]{:S(2)}) collective-permute-start(f32[8,128]{1,0:T(8,128)S(1)} %get-tuple-element.60), channel_id=1, source_target_pairs={{0,2},{1,3},{2,0},{3,1},{4,6},{5,7},{6,4},{7,5},{8,10},{9,11},{10,... | collective-permute-start | bytes 12296 | tf_op jit(solution)/shard_map/loss_near/ppermute | solution.py:356
  100.2 22.5 %all-to-all-start.5 = ((f32[576,2,128]{2,1,0:T(2,128)}), f32[576,2,128]{2,1,0:T(2,128)S(1)}, u32[]{:S(2)}, u32[]{:S(2)}) async-start(f32[576,2,128]{2,1,0:T(2,128)} %bitcast.11), calls=%async_computation.5 | async-start | bytes 1179648 | tf_op jit(solution)/shard_map/maps_back/all_to_all | solution.py:19
  108.8 3.1 %collective-permute-start.3 = (f32[8,128]{1,0:T(8,128)S(1)}, f32[8,128]{1,0:T(8,128)S(1)}, u32[]{:S(2)}, u32[]{:S(2)}) collective-permute-start(f32[8,128]{1,0:T(8,128)S(1)} %add.9), channel_id=1, source_target_pairs={{0,1},{1,0},{2,3},{3,2},{4,5},{5,4},{6,7},{7,6},{8,9},{9,8},{10,11... | collective-permute-start | bytes 12296 | tf_op jit(solution)/shard_map/loss_far/ppermute | solution.py:356
  111.8 10.4 %collective-permute-start.4 = (f32[8,128]{1,0:T(8,128)S(1)}, f32[8,128]{1,0:T(8,128)S(1)}, u32[]{:S(2)}, u32[]{:S(2)}) collective-permute-start(f32[8,128]{1,0:T(8,128)S(1)} %add.10), channel_id=1, source_target_pairs={{0,4},{1,5},{2,6},{3,7},{4,0},{5,1},{6,2},{7,3},{8,12},{9,13},{10,... | collective-permute-start | bytes 12296 | tf_op jit(solution)/shard_map/loss_far/ppermute | solution.py:356

commit v7 on v6

--- a/solution.py
+++ b/solution.py
@@ -328,7 +328,7 @@
             lambda *refs: student_kernel(2.0 / count_all, *refs),
             (parts_shape, grad_shape, grad_shape, far(1, positions)),
             (400 * mega, 4 * mega),
-        )(*keep_far(*pair, *window), returned)
+        )(*pair, *keep_far(*window), returned)
     with jax.named_scope("grads_out"):
         gathered = exchange(packed)
     with jax.named_scope("grad_q"):
@@ -373,7 +373,7 @@
         sums = call(total_kernel, maps_shape, (mega, mega))(parts)
         sums, loss = lax.optimization_barrier((sums, loss))
     with jax.named_scope("loss_far"):
-        loss = over_tp(over_tp(loss, 1), 4)
+        loss = over_tp(over_tp(loss, 1), tp_count - 2)
     with jax.named_scope("maps_back"):
         grad_q, grad_k = call(
             finish_kernel, (shape(heads, half, width), shape(half, width)), (mega, mega)

time: 125 us -> 125 us (level)
  no operation moved by 1% of the time
where the time goes in v7:
time: 125 us; the launch traced here: 124 us
  starting transfers between devices  75 us (60%)
  waiting for transfers between devices  25.7 us (21%)
  Pallas kernels  19.9 us (16%)
  local copies, waits for them, and re-layouts  1.94 us (2%)
    all_to_all x6, starting transfers between devices, exchange(): return lax.all_to_all(parts, axis, 0, 0, tiled=True)  51.5 us
    all_to_all x6, waiting for transfers between devices, exchange(): return lax.all_to_all(parts, axis, 0, 0, tiled=True)  21.3 us
    ppermute x3, starting transfers between devices, over_tp(): lax.ppermute(loss, 'tp', [(i, i ^ bit) for i in range(tp_count)])  16.8 us
    ppermute x3, waiting for transfers between devices, over_tp(): lax.ppermute(loss, 'tp', [(i, i ^ bit) for i in range(tp_count)])  4.4 us
    pallas_call x1, Pallas kernels, on_device(): call(grad_q_kernel, shape(2, heads // 2, half, width), (1000 * mega, 4 *...  4 us
    pallas_call x1, Pallas kernels, on_device(): call(lambda *refs: student_kernel(2.0 / count_all, *refs), (parts_shape,...  3.76 us
    ppermute x1, starting transfers between devices, on_device(): lax.ppermute(grad_q[1], 'section', [(i, i ^ 1) for i in range(count)])  3.38 us
    ppermute x1, starting transfers between devices, on_device(): lax.ppermute(jnp.concatenate([halo_keys, halo_values], axis=0), 'section'...  3.38 us
  transfers between devices with their start and end apart: 11, of which 8 were waited for; matrix products, arithmetic and copies ran while one was open for 2% of the time, Pallas kernels for 9%

profile of v7, /device:TPU:6, one launch (start us, length us, event | category | flops | bytes accessed | tf_op | source)
XLA Modules:
  0.0 123.5 jit_solution(8732427409485772941)
XLA Ops:
  0.6 1.9 %own_state.1 = (f32[64,3,128]{2,1,0:T(4,128)}, f32[128,128]{1,0:T(8,128)S(1)}) custom-call(bf16[128,128]{1,0:T(8,128)(2,1)} %bitcast.25, bf16[128,128]{1,0:T(8,128)(2,1)} %bitcast.29, f32[1,64,128]{2,1,0:T(8,128)} %bitcast.37), custom_call_target="tpu_custom_call" | custom-call | flops 31457280 | bytes 524288 | tf_op jit(solution)/shard_map/own_state/pallas_call | solution.py:284
  2.5 0.0 copy-start.3
  2.5 0.0 copy-start.4
  2.5 12.7 %all-to-all-start = ((f32[64,3,128]{2,1,0:T(4,128)}), f32[64,3,128]{2,1,0:T(4,128)S(1)}, u32[]{:S(2)}, u32[]{:S(2)}) async-start(f32[64,3,128]{2,1,0:T(4,128)} %get-tuple-element.35), calls=%async_computation | async-start | bytes 262144 | tf_op jit(solution)/shard_map/states_out/all_to_all | solution.py:19
  15.2 0.0 copy-done.3
  15.3 0.0 copy-done.4
  15.3 3.4 %collective-permute-start = (bf16[256,128]{1,0:T(8,128)(2,1)S(1)}, bf16[256,128]{1,0:T(8,128)(2,1)S(1)}, u32[]{:S(2)}, u32[]{:S(2)}) collective-permute-start(bf16[256,128]{1,0:T(8,128)(2,1)S(1)} %pad_maximum_fusion), channel_id=1, source_target_pairs={{0,8},{8,16},{16,24},{24,32},{32,40},{40,48},{48,56},{56,64},{64,7... | collective-permute-start | bytes 196616 | tf_op jit(solution)/shard_map/ppermute | solution.py:290
  18.7 0.0 copy-start.5
  18.7 1.2 %copy.9 = bf16[16,128,128]{2,1,0:T(8,128)(2,1)S(1)} copy(bf16[16,128,128]{2,0,1:T(8,128)(2,1)} %bitcast.34) | data formatting | bytes 1048576 | tf_op jit(solution)/shard_map/query_feats/transpose | solution.py:296
  19.9 0.0 copy-start
  19.9 0.0 copy-done.5
  19.9 2.4 %query_feats.1 = (bf16[128,2048]{1,0:T(8,128)(2,1)}, bf16[128,2048]{1,0:T(8,128)(2,1)}) custom-call(bf16[2048,128]{1,0:T(8,128)(2,1)S(1)} %bitcast.21, f32[16,64,128]{2,1,0:T(8,128)S(1)} %bitcast.33), custom_call_target="tpu_custom_call" | custom-call | flops 629145600 | bytes 3145728 | tf_op jit(solution)/shard_map/query_feats/pallas_call | solution.py:298
  22.3 0.0 copy-start.6
  22.3 2.0 %all-to-all-done.refs_0_ = f32[64,3,128]{2,1,0:T(4,128)S(1)} async-done(((f32[64,3,128]{2,1,0:T(4,128)}), f32[64,3,128]{2,1,0:T(4,128)S(1)}, u32[]{:S(2)}, u32[]{:S(2)}) %all-to-all-start) | async-done | bytes 98336 | tf_op jit(solution)/shard_map/states_out/all_to_all | solution.py:19
  24.3 1.2 prefix.1
  25.5 0.0 collective-permute-done.halo_ref
  25.5 8.4 %all-to-all-start.1 = ((f32[64,3,128]{2,1,0:T(4,128)}), f32[64,3,128]{2,1,0:T(4,128)S(1)}, u32[]{:S(2)}, u32[]{:S(2)}) async-start(f32[64,3,128]{2,1,0:T(4,128)} %prefix.1), calls=%async_computation.1 | async-start | bytes 262144 | tf_op jit(solution)/shard_map/states_back/all_to_all | solution.py:19
  33.9 0.0 copy-done.6
  33.9 0.1 copy.10
  34.0 0.0 copy-done
  34.0 0.0 copy-start.1
  34.1 0.0 copy-start.2
  34.1 2.3 %window.1 = (f32[128,2048]{1,0:T(8,128)}, f32[1,2048]{1,0:T(1,128)}, bf16[128,2048]{1,0:T(8,128)(2,1)}) custom-call(bf16[2048,128]{1,0:T(8,128)(2,1)S(1)} %bitcast.22, bf16[128,128]{1,0:T(8,128)(2,1)S(1)} %bitcast.27, bf16[128,128]{1,0:T(8,128)(2,1)S(1)} %bitcast.31, bf16[256,128]{1,0:T(8,128)(2,1)S(1)} %collective-permute-done.halo_ref, ...), custom_call_target="tpu_custom_call" | custom-call | flops 2097152000 | bytes 8388608 | tf_op jit(solution)/shard_map/window/pallas_call | solution.py:317
  36.3 6.4 %all-to-all-done.1.refs_5_.state_ref = f32[64,3,128]{2,1,0:T(4,128)S(1)} async-done(((f32[64,3,128]{2,1,0:T(4,128)}), f32[64,3,128]{2,1,0:T(4,128)S(1)}, u32[]{:S(2)}, u32[]{:S(2)}) %all-to-all-start.1) | async-done | bytes 98336 | tf_op jit(solution)/shard_map/states_back/all_to_all | solution.py:19
  42.7 0.0 copy-done.1
  42.7 0.0 copy-done.2
  42.7 3.8 %student.1 = (f32[64,3,128]{2,1,0:T(4,128)}, bf16[128,2048]{1,0:T(8,128)(2,1)}, bf16[128,2048]{1,0:T(8,128)(2,1)}, f32[1,2048]{1,0:T(1,128)}) custom-call(bf16[128,2048]{1,0:T(8,128)(2,1)S(1)} %copy-done.1, bf16[128,2048]{1,0:T(8,128)(2,1)S(1)} %copy-done.2, f32[128,2048]{1,0:T(8,128)} %get-tuple-element.46.refs_2_, f32[1,2048]{1,0:T(1,128)} %get-tuple-element.47.refs_3_, ...), custom_call_target="tpu_custom_call" | custom-call | flops 419430400 | bytes 4194304 | tf_op jit(solution)/shard_map/student/pallas_call | solution.py:327
  46.5 6.4 %all-to-all-start.2 = ((f32[64,3,128]{2,1,0:T(4,128)}), f32[64,3,128]{2,1,0:T(4,128)S(1)}, u32[]{:S(2)}, u32[]{:S(2)}) async-start(f32[64,3,128]{2,1,0:T(4,128)} %get-tuple-element.50), calls=%async_computation.2 | async-start | bytes 262144 | tf_op jit(solution)/shard_map/grads_out/all_to_all | solution.py:19
  52.9 4.0 %grad_q.1.query_ref = f32[2,8,64,128]{3,2,1,0:T(8,128)S(1)} custom-call(bf16[128,2048]{1,0:T(8,128)(2,1)} %get-tuple-element.41.refs_0_.high_ref, bf16[128,2048]{1,0:T(8,128)(2,1)} %get-tuple-element.42.refs_1_.low_ref, bf16[128,2048]{1,0:T(8,128)(2,1)} %get-tuple-element.51.grad_high_ref, bf16[128,2048]{1,0:T(8,128)(2,1)} %get-tuple-element.52.grad_low_ref, ...), custom_call_target="tpu_custom_call" | custom-call | flops 1048576000 | bytes 4194304 | tf_op jit(solution)/shard_map/grad_q/pallas_call | solution.py:335
  57.0 3.4 %collective-permute-start.1 = (f32[8,64,128]{2,1,0:T(8,128)S(1)}, f32[8,64,128]{2,1,0:T(8,128)S(1)}, u32[]{:S(2)}, u32[]{:S(2)}) collective-permute-start(f32[8,64,128]{2,1,0:T(8,128)S(1)} %slice_bitcast_fusion), channel_id=1, source_target_pairs={{0,8},{8,0},{16,24},{24,16},{32,40},{40,32},{48,56},{56,48},{64,72... | collective-permute-start | bytes 786440 | tf_op jit(solution)/shard_map/grad_q_swap/ppermute | solution.py:345
  60.4 1.4 %all-to-all-done.2.refs_0_ = f32[64,3,128]{2,1,0:T(4,128)S(1)} async-done(((f32[64,3,128]{2,1,0:T(4,128)}), f32[64,3,128]{2,1,0:T(4,128)S(1)}, u32[]{:S(2)}, u32[]{:S(2)}) %all-to-all-start.2) | async-done | bytes 98336 | tf_op jit(solution)/shard_map/grads_out/all_to_all | solution.py:19
  61.7 1.2 suffix.1
  62.9 9.0 %all-to-all-start.3 = ((f32[64,3,128]{2,1,0:T(4,128)}), f32[64,3,128]{2,1,0:T(4,128)S(1)}, u32[]{:S(2)}, u32[]{:S(2)}) async-start(f32[64,3,128]{2,1,0:T(4,128)} %get-tuple-element.55), calls=%async_computation.3 | async-start | bytes 262144 | tf_op jit(solution)/shard_map/grads_back/all_to_all | solution.py:19
  71.9 0.0 collective-permute-done.1.other_ref
  71.9 8.8 %all-to-all-done.3.state_ref = f32[64,3,128]{2,1,0:T(4,128)S(1)} async-done(((f32[64,3,128]{2,1,0:T(4,128)}), f32[64,3,128]{2,1,0:T(4,128)S(1)}, u32[]{:S(2)}, u32[]{:S(2)}) %all-to-all-start.3) | async-done | bytes 98336 | tf_op jit(solution)/shard_map/grads_back/all_to_all | solution.py:19
  80.7 1.2 grad_k.1
  81.9 6.5 %all-to-all-start.4 = ((f32[320,2,128]{2,1,0:T(2,128)}), f32[320,2,128]{2,1,0:T(2,128)S(1)}, u32[]{:S(2)}, u32[]{:S(2)}) async-start(f32[320,2,128]{2,1,0:T(2,128)} %bitcast.9), calls=%async_computation.4 | async-start | bytes 655360 | tf_op jit(solution)/shard_map/maps_out/all_to_all | solution.py:19
  88.4 6.1 %collective-permute-start.2 = (f32[8,128]{1,0:T(8,128)S(1)}, f32[8,128]{1,0:T(8,128)S(1)}, u32[]{:S(2)}, u32[]{:S(2)}) collective-permute-start(f32[8,128]{1,0:T(8,128)S(1)} %get-tuple-element.60), channel_id=1, source_target_pairs={{0,2},{1,3},{2,0},{3,1},{4,6},{5,7},{6,4},{7,5},{8,10},{9,11},{10,... | collective-permute-start | bytes 12296 | tf_op jit(solution)/shard_map/loss_near/ppermute | solution.py:356
  94.5 1.6 %collective-permute-done.2 = f32[8,128]{1,0:T(8,128)S(1)} collective-permute-done((f32[8,128]{1,0:T(8,128)S(1)}, f32[8,128]{1,0:T(8,128)S(1)}, u32[]{:S(2)}, u32[]{:S(2)}) %collective-permute-start.2) | collective-permute-done | bytes 4128 | tf_op jit(solution)/shard_map/loss_near/ppermute | solution.py:356
  96.1 2.8 %all-to-all-done.4 = f32[320,2,128]{2,1,0:T(2,128)S(1)} async-done(((f32[320,2,128]{2,1,0:T(2,128)}), f32[320,2,128]{2,1,0:T(2,128)S(1)}, u32[]{:S(2)}, u32[]{:S(2)}) %all-to-all-start.4) | async-done | bytes 327712 | tf_op jit(solution)/shard_map/maps_out/all_to_all | solution.py:19
  98.9 1.1 maps_out.1
  99.9 8.4 %all-to-all-start.5 = ((f32[576,2,128]{2,1,0:T(2,128)}), f32[576,2,128]{2,1,0:T(2,128)S(1)}, u32[]{:S(2)}, u32[]{:S(2)}) async-start(f32[576,2,128]{2,1,0:T(2,128)} %bitcast.11), calls=%async_computation.5 | async-start | bytes 1179648 | tf_op jit(solution)/shard_map/maps_back/all_to_all | solution.py:19
  108.4 1.9 %collective-permute-start.3 = (f32[8,128]{1,0:T(8,128)S(1)}, f32[8,128]{1,0:T(8,128)S(1)}, u32[]{:S(2)}, u32[]{:S(2)}) collective-permute-start(f32[8,128]{1,0:T(8,128)S(1)} %add.9), channel_id=1, source_target_pairs={{0,1},{1,0},{2,3},{3,2},{4,5},{5,4},{6,7},{7,6},{8,9},{9,8},{10,11... | collective-permute-start | bytes 12296 | tf_op jit(solution)/shard_map/loss_far/ppermute | solution.py:356
  110.3 1.1 collective-permute-done.3
  111.4 8.8 %collective-permute-start.4 = (f32[8,128]{1,0:T(8,128)S(1)}, f32[8,128]{1,0:T(8,128)S(1)}, u32[]{:S(2)}, u32[]{:S(2)}) collective-permute-start(f32[8,128]{1,0:T(8,128)S(1)} %add.10), channel_id=1, source_target_pairs={{0,6},{1,7},{2,4},{3,5},{4,2},{5,3},{6,0},{7,1},{8,14},{9,15},{10,... | collective-permute-start | bytes 12296 | tf_op jit(solution)/shard_map/loss_far/ppermute | solution.py:356
  120.2 1.7 %collective-permute-done.4 = f32[8,128]{1,0:T(8,128)S(1)} collective-permute-done((f32[8,128]{1,0:T(8,128)S(1)}, f32[8,128]{1,0:T(8,128)S(1)}, u32[]{:S(2)}, u32[]{:S(2)}) %collective-permute-start.4) | collective-permute-done | bytes 4128 | tf_op jit(solution)/shard_map/loss_far/ppermute | solution.py:356
  121.9 0.5 slice.7
  122.4 0.0 all-to-all-done.5
  122.4 1.1 maps_back.1
  (5 shorter events, 0.0 us)
Async XLA Ops:
  2.5 12.8 %copy-start.3 = (bf16[128,1,128]{2,0,1:T(8,128)(2,1)S(1)}, bf16[128,1,128]{2,0,1:T(8,128)(2,1)}, u32[]{:S(2)}) copy-start(bf16[128,1,128]{2,0,1:T(8,128)(2,1)} %param.7) | copy-start | bytes 98308
  2.5 12.8 %copy-start.4 = (bf16[128,1,128]{2,0,1:T(8,128)(2,1)S(1)}, bf16[128,1,128]{2,0,1:T(8,128)(2,1)}, u32[]{:S(2)}) copy-start(bf16[128,1,128]{2,0,1:T(8,128)(2,1)} %param.8) | copy-start | bytes 98308
  2.5 21.8 %all-to-all-start = ((f32[64,3,128]{2,1,0:T(4,128)}), f32[64,3,128]{2,1,0:T(4,128)S(1)}, u32[]{:S(2)}, u32[]{:S(2)}) async-start(f32[64,3,128]{2,1,0:T(4,128)} %get-tuple-element.35), calls=%async_computation | async-start | bytes 262144 | tf_op jit(solution)/shard_map/states_out/all_to_all | solution.py:19
  15.3 10.2 %collective-permute-start = (bf16[256,128]{1,0:T(8,128)(2,1)S(1)}, bf16[256,128]{1,0:T(8,128)(2,1)S(1)}, u32[]{:S(2)}, u32[]{:S(2)}) collective-permute-start(bf16[256,128]{1,0:T(8,128)(2,1)S(1)} %pad_maximum_fusion), channel_id=1, source_target_pairs={{0,8},{8,16},{16,24},{24,32},{32,40},{40,48},{48,56},{56,64},{64,7... | collective-permute-start | bytes 196616 | tf_op jit(solution)/shard_map/ppermute | solution.py:290
  18.7 1.3 %copy-start.5 = (f32[16,128,64]{1,2,0:T(8,128)S(1)}, f32[16,128,64]{1,2,0:T(8,128)}, u32[]{:S(2)}) copy-start(f32[16,128,64]{1,2,0:T(8,128)} %param.10) | copy-start | bytes 1572868
  19.9 14.1 %copy-start = (bf16[16,128,128]{2,1,0:T(8,128)(2,1)}, bf16[16,128,128]{2,1,0:T(8,128)(2,1)S(1)}, u32[]{:S(2)}) copy-start(bf16[16,128,128]{2,1,0:T(8,128)(2,1)S(1)} %copy.9) | copy-start | bytes 1572868
  22.3 11.6 %copy-start.6 = (bf16[128,16,128]{2,1,0:T(8,128)(2,1)S(1)}, bf16[128,16,128]{2,1,0:T(8,128)(2,1)}, u32[]{:S(2)}) copy-start(bf16[128,16,128]{2,1,0:T(8,128)(2,1)} %param.9) | copy-start | bytes 1572868
  25.5 17.2 %all-to-all-start.1 = ((f32[64,3,128]{2,1,0:T(4,128)}), f32[64,3,128]{2,1,0:T(4,128)S(1)}, u32[]{:S(2)}, u32[]{:S(2)}) async-start(f32[64,3,128]{2,1,0:T(4,128)} %prefix.1), calls=%async_computation.1 | async-start | bytes 262144 | tf_op jit(solution)/shard_map/states_back/all_to_all | solution.py:19
  34.0 8.7 %copy-start.1 = (bf16[128,2048]{1,0:T(8,128)(2,1)S(1)}, bf16[128,2048]{1,0:T(8,128)(2,1)}, u32[]{:S(2)}) copy-start(bf16[128,2048]{1,0:T(8,128)(2,1)} %get-tuple-element.41.refs_0_.high_ref) | copy-start | bytes 1572868
  34.1 8.7 %copy-start.2 = (bf16[128,2048]{1,0:T(8,128)(2,1)S(1)}, bf16[128,2048]{1,0:T(8,128)(2,1)}, u32[]{:S(2)}) copy-start(bf16[128,2048]{1,0:T(8,128)(2,1)} %get-tuple-element.42.refs_1_.low_ref) | copy-start | bytes 1572868
  46.5 15.2 %all-to-all-start.2 = ((f32[64,3,128]{2,1,0:T(4,128)}), f32[64,3,128]{2,1,0:T(4,128)S(1)}, u32[]{:S(2)}, u32[]{:S(2)}) async-start(f32[64,3,128]{2,1,0:T(4,128)} %get-tuple-element.50), calls=%async_computation.2 | async-start | bytes 262144 | tf_op jit(solution)/shard_map/grads_out/all_to_all | solution.py:19
  57.0 14.9 %collective-permute-start.1 = (f32[8,64,128]{2,1,0:T(8,128)S(1)}, f32[8,64,128]{2,1,0:T(8,128)S(1)}, u32[]{:S(2)}, u32[]{:S(2)}) collective-permute-start(f32[8,64,128]{2,1,0:T(8,128)S(1)} %slice_bitcast_fusion), channel_id=1, source_target_pairs={{0,8},{8,0},{16,24},{24,16},{32,40},{40,32},{48,56},{56,48},{64,72... | collective-permute-start | bytes 786440 | tf_op jit(solution)/shard_map/grad_q_swap/ppermute | solution.py:345
  62.9 17.8 %all-to-all-start.3 = ((f32[64,3,128]{2,1,0:T(4,128)}), f32[64,3,128]{2,1,0:T(4,128)S(1)}, u32[]{:S(2)}, u32[]{:S(2)}) async-start(f32[64,3,128]{2,1,0:T(4,128)} %get-tuple-element.55), calls=%async_computation.3 | async-start | bytes 262144 | tf_op jit(solution)/shard_map/grads_back/all_to_all | solution.py:19
  81.9 17.0 %all-to-all-start.4 = ((f32[320,2,128]{2,1,0:T(2,128)}), f32[320,2,128]{2,1,0:T(2,128)S(1)}, u32[]{:S(2)}, u32[]{:S(2)}) async-start(f32[320,2,128]{2,1,0:T(2,128)} %bitcast.9), calls=%async_computation.4 | async-start | bytes 655360 | tf_op jit(solution)/shard_map/maps_out/all_to_all | solution.py:19
  88.4 7.7 %collective-permute-start.2 = (f32[8,128]{1,0:T(8,128)S(1)}, f32[8,128]{1,0:T(8,128)S(1)}, u32[]{:S(2)}, u32[]{:S(2)}) collective-permute-start(f32[8,128]{1,0:T(8,128)S(1)} %get-tuple-element.60), channel_id=1, source_target_pairs={{0,2},{1,3},{2,0},{3,1},{4,6},{5,7},{6,4},{7,5},{8,10},{9,11},{10,... | collective-permute-start | bytes 12296 | tf_op jit(solution)/shard_map/loss_near/ppermute | solution.py:356
  99.9 22.5 %all-to-all-start.5 = ((f32[576,2,128]{2,1,0:T(2,128)}), f32[576,2,128]{2,1,0:T(2,128)S(1)}, u32[]{:S(2)}, u32[]{:S(2)}) async-start(f32[576,2,128]{2,1,0:T(2,128)} %bitcast.11), calls=%async_computation.5 | async-start | bytes 1179648 | tf_op jit(solution)/shard_map/maps_back/all_to_all | solution.py:19
  108.4 3.1 %collective-permute-start.3 = (f32[8,128]{1,0:T(8,128)S(1)}, f32[8,128]{1,0:T(8,128)S(1)}, u32[]{:S(2)}, u32[]{:S(2)}) collective-permute-start(f32[8,128]{1,0:T(8,128)S(1)} %add.9), channel_id=1, source_target_pairs={{0,1},{1,0},{2,3},{3,2},{4,5},{5,4},{6,7},{7,6},{8,9},{9,8},{10,11... | collective-permute-start | bytes 12296 | tf_op jit(solution)/shard_map/loss_far/ppermute | solution.py:356
  111.4 10.5 %collective-permute-start.4 = (f32[8,128]{1,0:T(8,128)S(1)}, f32[8,128]{1,0:T(8,128)S(1)}, u32[]{:S(2)}, u32[]{:S(2)}) collective-permute-start(f32[8,128]{1,0:T(8,128)S(1)} %add.10), channel_id=1, source_target_pairs={{0,6},{1,7},{2,4},{3,5},{4,2},{5,3},{6,0},{7,1},{8,14},{9,15},{10,... | collective-permute-start | bytes 12296 | tf_op jit(solution)/shard_map/loss_far/ppermute | solution.py:356

commit v8 on v7

--- a/solution.py
+++ b/solution.py
@@ -175,14 +175,13 @@
 
 
 def grad_q_kernel(
-    high_ref, low_ref, grad_high_ref, grad_low_ref, grad_total_ref, query_ref, state_ref, out_ref
+    _, high_ref, low_ref, grad_high_ref, grad_low_ref, grad_total_ref, query_ref, state_ref, out_ref
 ):
     state, total = get_state(state_ref)
     total = jnp.concatenate([total] * (PAIR // total.shape[1]), axis=1)
     state = split(state)
-    _, kept, half, _ = out_ref.shape
+    kept, half, _ = out_ref.shape
     tokens = query_ref.shape[0] // kept
-    slot = (pl.program_id(0) + lax.axis_index("section")) % 2
     for k in range(query_ref.shape[0] // PAIR):
         here = slice(k * PAIR, (k + 1) * PAIR)
         grad = mxu3(state, (grad_high_ref[:, here], grad_low_ref[:, here]))
@@ -193,7 +192,7 @@
             cut = slice(n * tokens, (n + 1) * tokens)
             query = query_ref[k * PAIR + n * tokens : k * PAIR + (n + 1) * tokens, :]
             out = mxu(inner[1][:, cut], query) + mxu(inner[0][:, cut], query)
-            out_ref[slot, k * (PAIR // tokens) + n] = out[:half] - out[half:]
+            out_ref[k * (PAIR // tokens) + n] = out[:half] - out[half:]
 
 
 def grad_k_kernel(state_ref, feats_ref, key_ref, value_ref, query_ref, other_ref, out_ref):
@@ -202,9 +201,9 @@
     inner = split(features_back_t(feats_ref[...], grad))
     out = mxu(inner[1], key_ref[...]) + mxu(inner[0], key_ref[...])
     half = out.shape[0] // 2
-    kept = query_ref.shape[1]
+    kept = query_ref.shape[0]
     for h in range(kept):
-        out_ref[:, h // 2, h % 2, :] = query_ref[0, h] + other_ref[h]
+        out_ref[:, h // 2, h % 2, :] = query_ref[h] + other_ref[h]
     out_ref[:, kept // 2, 0, :] = out[:half] - out[half:]
     out_ref[:, kept // 2, 1, :] = jnp.zeros((half, out.shape[1]), jnp.float32)
 
@@ -332,24 +331,47 @@
     with jax.named_scope("grads_out"):
         gathered = exchange(packed)
     with jax.named_scope("grad_q"):
-        grad_q = call(
-            grad_q_kernel,
-            shape(2, heads // 2, half, width),
-            (1000 * mega, 4 * mega),
-            (STEPS,),
-            [by_lane(feats), by_lane(feats), by_lane(width), by_lane(width), by_lane(1)]
-            + [by_row, whole(count, 3, width)],
-            whole(2, heads // 2, half, width),
-        )(*keep_far(*pair, *grads, query_rows), returned)
+        cut = positions // 2
+
+        def lane_half(rows):
+            return pl.BlockSpec((rows, cut), lambda i, which: (0, which[0]))
+
+        def grad_q_half(which):
+            return pl.pallas_call(
+                grad_q_kernel,
+                out_shape=shape(heads // 2, half, width),
+                grid_spec=pltpu.PrefetchScalarGridSpec(
+                    num_scalar_prefetch=1,
+                    grid=(1,),
+                    in_specs=[lane_half(feats)] * 2
+                    + [lane_half(width)] * 2
+                    + [
+                        lane_half(1),
+                        pl.BlockSpec((cut, width), lambda i, which: (which[0], 0)),
+                        pl.BlockSpec((count, 3, width), lambda i, which: (0, 0, 0)),
+                    ],
+                    out_specs=pl.BlockSpec((heads // 2, half, width), lambda i, which: (0, 0, 0)),
+                ),
+                compiler_params=pltpu.CompilerParams(vmem_limit_bytes=LIMIT),
+                cost_estimate=pl.CostEstimate(
+                    flops=500 * mega, bytes_accessed=2 * mega, transcendentals=0
+                ),
+            )(which[None], *keep_far(*pair, *grads, query_rows), returned)
+
+        mine = lax.axis_index("section") % 2
+        sent = grad_q_half(1 - mine)
     with jax.named_scope("grad_q_swap"):
-        other = lax.ppermute(grad_q[1], "section", [(i, i ^ 1) for i in range(count)])
+        other = lax.ppermute(sent, "section", [(i, i ^ 1) for i in range(count)])
     with jax.named_scope("suffix"):
-        gathered, grad_q = lax.optimization_barrier((gathered, grad_q))
+        gathered, sent = lax.optimization_barrier((gathered, sent))
         suffix, loss = call(
             lambda *refs: running_kernel(True, *refs),
             (parts_shape, shape(SUBLANES, width)),
             (mega, mega // 4),
         )(gathered)
+        suffix, mine = lax.optimization_barrier((suffix, mine))
+    with jax.named_scope("grad_q_kept"):
+        grad_q = grad_q_half(mine)
     with jax.named_scope("grads_back"):
         later = exchange(suffix)
     def over_tp(loss, bit):

time: 125 us -> 123 us (0.984)
  starting transfers between devices: 75 us -> 73.6 us
    all_to_all x6, starting transfers between devices: 51.5 us -> 50 us  [exchange(): return lax.all_to_all(parts, axis, 0, 0, tiled=True)]
    pallas_call x1 -> x2, Pallas kernels: 4 us -> 5.19 us  [grad_q_half(): pl.pallas_call(grad_q_kernel, out_shape=shape(heads // 2, half, width), g...]
  transfers between devices with their start and end apart: 11 -> 11, of which waited for: 8 -> 8; matrix products, arithmetic and copies ran while one was open for 2% -> 1% of each run, Pallas kernels for 9% -> 10%
where the time goes in v8:
time: 123 us; the launch traced here: 122 us
  starting transfers between devices  73.6 us (60%)
  waiting for transfers between devices  24.6 us (20%)
  Pallas kernels  21.1 us (17%)
  local copies, waits for them, and re-layouts  1.92 us (2%)
    all_to_all x6, starting transfers between devices, exchange(): return lax.all_to_all(parts, axis, 0, 0, tiled=True)  50 us
    all_to_all x6, waiting for transfers between devices, exchange(): return lax.all_to_all(parts, axis, 0, 0, tiled=True)  20.3 us
    ppermute x3, starting transfers between devices, over_tp(): lax.ppermute(loss, 'tp', [(i, i ^ bit) for i in range(tp_count)])  16.8 us
    pallas_call x2, Pallas kernels, grad_q_half(): pl.pallas_call(grad_q_kernel, out_shape=shape(heads // 2, half, width), g...  5.19 us
    ppermute x3, waiting for transfers between devices, over_tp(): lax.ppermute(loss, 'tp', [(i, i ^ bit) for i in range(tp_count)])  4.31 us
    pallas_call x1, Pallas kernels, on_device(): call(lambda *refs: student_kernel(2.0 / count_all, *refs), (parts_shape,...  3.76 us
    ppermute x1, starting transfers between devices, on_device(): lax.ppermute(jnp.concatenate([halo_keys, halo_values], axis=0), 'section'...  3.38 us
    ppermute x1, starting transfers between devices, on_device(): other = lax.ppermute(sent, 'section', [(i, i ^ 1) for i in range(count)])  3.38 us
  transfers between devices with their start and end apart: 11, of which 8 were waited for; matrix products, arithmetic and copies ran while one was open for 1% of the time, Pallas kernels for 10%

profile of v8, /device:TPU:6, one launch (start us, length us, event | category | flops | bytes accessed | tf_op | source)
XLA Modules:
  0.0 122.2 jit_solution(6280739768874227480)
XLA Ops:
  0.6 1.9 %own_state.1 = (f32[64,3,128]{2,1,0:T(4,128)}, f32[128,128]{1,0:T(8,128)S(1)}) custom-call(bf16[128,128]{1,0:T(8,128)(2,1)} %bitcast.26, bf16[128,128]{1,0:T(8,128)(2,1)} %bitcast.30, f32[1,64,128]{2,1,0:T(8,128)} %bitcast.38), custom_call_target="tpu_custom_call" | custom-call | flops 31457280 | bytes 524288 | tf_op jit(solution)/shard_map/own_state/pallas_call | solution.py:283
  2.5 0.0 copy-start.3
  2.5 0.0 copy-start.4
  2.5 12.7 %all-to-all-start = ((f32[64,3,128]{2,1,0:T(4,128)}), f32[64,3,128]{2,1,0:T(4,128)S(1)}, u32[]{:S(2)}, u32[]{:S(2)}) async-start(f32[64,3,128]{2,1,0:T(4,128)} %get-tuple-element.36), calls=%async_computation | async-start | bytes 262144 | tf_op jit(solution)/shard_map/states_out/all_to_all | solution.py:19
  15.2 0.0 copy-done.3
  15.3 0.0 copy-done.4
  15.3 3.4 %collective-permute-start = (bf16[256,128]{1,0:T(8,128)(2,1)S(1)}, bf16[256,128]{1,0:T(8,128)(2,1)S(1)}, u32[]{:S(2)}, u32[]{:S(2)}) collective-permute-start(bf16[256,128]{1,0:T(8,128)(2,1)S(1)} %pad_maximum_fusion), channel_id=1, source_target_pairs={{0,8},{8,16},{16,24},{24,32},{32,40},{40,48},{48,56},{56,64},{64,7... | collective-permute-start | bytes 196616 | tf_op jit(solution)/shard_map/ppermute | solution.py:289
  18.7 0.0 copy-start.5
  18.7 1.2 %copy.9 = bf16[16,128,128]{2,1,0:T(8,128)(2,1)S(1)} copy(bf16[16,128,128]{2,0,1:T(8,128)(2,1)} %bitcast.35) | data formatting | bytes 1048576 | tf_op jit(solution)/shard_map/query_feats/transpose | solution.py:295
  19.9 0.0 copy-start
  19.9 0.0 copy-done.5
  19.9 0.0 copy-start.6
  19.9 2.4 %query_feats.1 = (bf16[128,2048]{1,0:T(8,128)(2,1)}, bf16[128,2048]{1,0:T(8,128)(2,1)}) custom-call(bf16[2048,128]{1,0:T(8,128)(2,1)S(1)} %bitcast.19, f32[16,64,128]{2,1,0:T(8,128)S(1)} %bitcast.34), custom_call_target="tpu_custom_call" | custom-call | flops 629145600 | bytes 3145728 | tf_op jit(solution)/shard_map/query_feats/pallas_call | solution.py:297
  22.3 2.0 %all-to-all-done.refs_0_ = f32[64,3,128]{2,1,0:T(4,128)S(1)} async-done(((f32[64,3,128]{2,1,0:T(4,128)}), f32[64,3,128]{2,1,0:T(4,128)S(1)}, u32[]{:S(2)}, u32[]{:S(2)}) %all-to-all-start) | async-done | bytes 98336 | tf_op jit(solution)/shard_map/states_out/all_to_all | solution.py:19
  24.3 1.2 prefix.1
  25.5 0.0 collective-permute-done.halo_ref
  25.5 0.0 copy-done.6
  25.5 0.1 copy.10
  25.6 8.4 %all-to-all-start.1 = ((f32[64,3,128]{2,1,0:T(4,128)}), f32[64,3,128]{2,1,0:T(4,128)S(1)}, u32[]{:S(2)}, u32[]{:S(2)}) async-start(f32[64,3,128]{2,1,0:T(4,128)} %prefix.1), calls=%async_computation.1 | async-start | bytes 262144 | tf_op jit(solution)/shard_map/states_back/all_to_all | solution.py:19
  34.0 0.0 copy-done
  34.0 0.0 copy-start.1
  34.1 0.0 copy-start.2
  34.1 2.3 %window.1 = (f32[128,2048]{1,0:T(8,128)}, f32[1,2048]{1,0:T(1,128)}, bf16[128,2048]{1,0:T(8,128)(2,1)}) custom-call(bf16[2048,128]{1,0:T(8,128)(2,1)S(1)} %bitcast.20, bf16[128,128]{1,0:T(8,128)(2,1)S(1)} %bitcast.28, bf16[128,128]{1,0:T(8,128)(2,1)S(1)} %bitcast.32, bf16[256,128]{1,0:T(8,128)(2,1)S(1)} %collective-permute-done.halo_ref, ...), custom_call_target="tpu_custom_call" | custom-call | flops 2097152000 | bytes 8388608 | tf_op jit(solution)/shard_map/window/pallas_call | solution.py:316
  36.3 6.5 %all-to-all-done.1.refs_5_.state_ref = f32[64,3,128]{2,1,0:T(4,128)S(1)} async-done(((f32[64,3,128]{2,1,0:T(4,128)}), f32[64,3,128]{2,1,0:T(4,128)S(1)}, u32[]{:S(2)}, u32[]{:S(2)}) %all-to-all-start.1) | async-done | bytes 98336 | tf_op jit(solution)/shard_map/states_back/all_to_all | solution.py:19
  42.8 0.0 copy-done.1
  42.8 0.0 copy-done.2
  42.8 3.8 %student.1 = (f32[64,3,128]{2,1,0:T(4,128)}, bf16[128,2048]{1,0:T(8,128)(2,1)}, bf16[128,2048]{1,0:T(8,128)(2,1)}, f32[1,2048]{1,0:T(1,128)}) custom-call(bf16[128,2048]{1,0:T(8,128)(2,1)S(1)} %copy-done.1, bf16[128,2048]{1,0:T(8,128)(2,1)S(1)} %copy-done.2, f32[128,2048]{1,0:T(8,128)} %get-tuple-element.47.refs_2_, f32[1,2048]{1,0:T(1,128)} %get-tuple-element.48.refs_3_, ...), custom_call_target="tpu_custom_call" | custom-call | flops 419430400 | bytes 4194304 | tf_op jit(solution)/shard_map/student/pallas_call | solution.py:326
  46.6 6.5 %all-to-all-start.2 = ((f32[64,3,128]{2,1,0:T(4,128)}), f32[64,3,128]{2,1,0:T(4,128)S(1)}, u32[]{:S(2)}, u32[]{:S(2)}) async-start(f32[64,3,128]{2,1,0:T(4,128)} %get-tuple-element.51), calls=%async_computation.2 | async-start | bytes 262144 | tf_op jit(solution)/shard_map/grads_out/all_to_all | solution.py:19
  53.1 2.6 %grad_q.1 = f32[8,64,128]{2,1,0:T(8,128)S(1)} custom-call(s32[1]{0:T(128)} %bitcast.8._, bf16[128,2048]{1,0:T(8,128)(2,1)} %get-tuple-element.42.refs_0_.high_ref, bf16[128,2048]{1,0:T(8,128)(2,1)} %get-tuple-element.43.refs_1_.low_ref, bf16[128,2048]{1,0:T(8,128)(2,1)} %get-tuple-element.52.grad_high_ref, bf16[128,2048]{1,0:T(8,128)(2,1)} %get-tuple-element.53.grad_low_ref, ...), custom_call_target="tpu_custom_call" | custom-call | flops 524288000 | bytes 2097152 | tf_op jit(solution)/shard_map/grad_q/pallas_call | solution.py:340
  55.7 3.4 %collective-permute-start.1 = (f32[8,64,128]{2,1,0:T(8,128)S(1)}, f32[8,64,128]{2,1,0:T(8,128)S(1)}, u32[]{:S(2)}, u32[]{:S(2)}) collective-permute-start(f32[8,64,128]{2,1,0:T(8,128)S(1)} %grad_q.1), channel_id=1, source_target_pairs={{0,8},{8,0},{16,24},{24,16},{32,40},{40,32},{48,56},{56,48},{64,72... | collective-permute-start | bytes 786440 | tf_op jit(solution)/shard_map/grad_q_swap/ppermute | solution.py:364
  59.1 2.8 %all-to-all-done.2.refs_0_ = f32[64,3,128]{2,1,0:T(4,128)S(1)} async-done(((f32[64,3,128]{2,1,0:T(4,128)}), f32[64,3,128]{2,1,0:T(4,128)S(1)}, u32[]{:S(2)}, u32[]{:S(2)}) %all-to-all-start.2) | async-done | bytes 98336 | tf_op jit(solution)/shard_map/grads_out/all_to_all | solution.py:19
  61.9 1.2 suffix.1
  63.1 7.5 %all-to-all-start.3 = ((f32[64,3,128]{2,1,0:T(4,128)}), f32[64,3,128]{2,1,0:T(4,128)S(1)}, u32[]{:S(2)}, u32[]{:S(2)}) async-start(f32[64,3,128]{2,1,0:T(4,128)} %get-tuple-element.57), calls=%async_computation.3 | async-start | bytes 262144 | tf_op jit(solution)/shard_map/grads_back/all_to_all | solution.py:19
  70.6 2.6 %grad_q_kept.1.query_ref = f32[8,64,128]{2,1,0:T(8,128)S(1)} custom-call(s32[1]{0:T(128)} %bitcast.9._, bf16[128,2048]{1,0:T(8,128)(2,1)} %get-tuple-element.42.refs_0_.high_ref, bf16[128,2048]{1,0:T(8,128)(2,1)} %get-tuple-element.43.refs_1_.low_ref, bf16[128,2048]{1,0:T(8,128)(2,1)} %get-tuple-element.52.grad_high_ref, ...), custom_call_target="tpu_custom_call" | custom-call | flops 524288000 | bytes 2097152 | tf_op jit(solution)/shard_map/grad_q_kept/pallas_call | solution.py:340
  73.2 0.0 collective-permute-done.1.other_ref
  73.2 6.2 %all-to-all-done.3.state_ref = f32[64,3,128]{2,1,0:T(4,128)S(1)} async-done(((f32[64,3,128]{2,1,0:T(4,128)}), f32[64,3,128]{2,1,0:T(4,128)S(1)}, u32[]{:S(2)}, u32[]{:S(2)}) %all-to-all-start.3) | async-done | bytes 98336 | tf_op jit(solution)/shard_map/grads_back/all_to_all | solution.py:19
  79.4 1.2 grad_k.1
  80.6 6.5 %all-to-all-start.4 = ((f32[320,2,128]{2,1,0:T(2,128)}), f32[320,2,128]{2,1,0:T(2,128)S(1)}, u32[]{:S(2)}, u32[]{:S(2)}) async-start(f32[320,2,128]{2,1,0:T(2,128)} %bitcast.10), calls=%async_computation.4 | async-start | bytes 655360 | tf_op jit(solution)/shard_map/maps_out/all_to_all | solution.py:19
  87.1 6.1 %collective-permute-start.2 = (f32[8,128]{1,0:T(8,128)S(1)}, f32[8,128]{1,0:T(8,128)S(1)}, u32[]{:S(2)}, u32[]{:S(2)}) collective-permute-start(f32[8,128]{1,0:T(8,128)S(1)} %get-tuple-element.62), channel_id=1, source_target_pairs={{0,2},{1,3},{2,0},{3,1},{4,6},{5,7},{6,4},{7,5},{8,10},{9,11},{10,... | collective-permute-start | bytes 12296 | tf_op jit(solution)/shard_map/loss_near/ppermute | solution.py:378
  93.2 1.6 %collective-permute-done.2 = f32[8,128]{1,0:T(8,128)S(1)} collective-permute-done((f32[8,128]{1,0:T(8,128)S(1)}, f32[8,128]{1,0:T(8,128)S(1)}, u32[]{:S(2)}, u32[]{:S(2)}) %collective-permute-start.2) | collective-permute-done | bytes 4128 | tf_op jit(solution)/shard_map/loss_near/ppermute | solution.py:378
  94.8 2.8 %all-to-all-done.4 = f32[320,2,128]{2,1,0:T(2,128)S(1)} async-done(((f32[320,2,128]{2,1,0:T(2,128)}), f32[320,2,128]{2,1,0:T(2,128)S(1)}, u32[]{:S(2)}, u32[]{:S(2)}) %all-to-all-start.4) | async-done | bytes 327712 | tf_op jit(solution)/shard_map/maps_out/all_to_all | solution.py:19
  97.7 1.1 maps_out.1
  98.7 8.4 %all-to-all-start.5 = ((f32[576,2,128]{2,1,0:T(2,128)}), f32[576,2,128]{2,1,0:T(2,128)S(1)}, u32[]{:S(2)}, u32[]{:S(2)}) async-start(f32[576,2,128]{2,1,0:T(2,128)} %bitcast.12), calls=%async_computation.5 | async-start | bytes 1179648 | tf_op jit(solution)/shard_map/maps_back/all_to_all | solution.py:19
  107.1 1.9 %collective-permute-start.3 = (f32[8,128]{1,0:T(8,128)S(1)}, f32[8,128]{1,0:T(8,128)S(1)}, u32[]{:S(2)}, u32[]{:S(2)}) collective-permute-start(f32[8,128]{1,0:T(8,128)S(1)} %add.14), channel_id=1, source_target_pairs={{0,1},{1,0},{2,3},{3,2},{4,5},{5,4},{6,7},{7,6},{8,9},{9,8},{10,11... | collective-permute-start | bytes 12296 | tf_op jit(solution)/shard_map/loss_far/ppermute | solution.py:378
  109.0 1.1 collective-permute-done.3
  110.2 8.8 %collective-permute-start.4 = (f32[8,128]{1,0:T(8,128)S(1)}, f32[8,128]{1,0:T(8,128)S(1)}, u32[]{:S(2)}, u32[]{:S(2)}) collective-permute-start(f32[8,128]{1,0:T(8,128)S(1)} %add.15), channel_id=1, source_target_pairs={{0,6},{1,7},{2,4},{3,5},{4,2},{5,3},{6,0},{7,1},{8,14},{9,15},{10,... | collective-permute-start | bytes 12296 | tf_op jit(solution)/shard_map/loss_far/ppermute | solution.py:378
  119.0 1.6 %collective-permute-done.4 = f32[8,128]{1,0:T(8,128)S(1)} collective-permute-done((f32[8,128]{1,0:T(8,128)S(1)}, f32[8,128]{1,0:T(8,128)S(1)}, u32[]{:S(2)}, u32[]{:S(2)}) %collective-permute-start.4) | collective-permute-done | bytes 4128 | tf_op jit(solution)/shard_map/loss_far/ppermute | solution.py:378
  120.6 0.5 slice.3
  121.1 0.0 all-to-all-done.5
  121.1 1.1 maps_back.1
  (4 shorter events, 0.0 us)
Async XLA Ops:
  2.5 12.8 %copy-start.3 = (bf16[128,1,128]{2,0,1:T(8,128)(2,1)S(1)}, bf16[128,1,128]{2,0,1:T(8,128)(2,1)}, u32[]{:S(2)}) copy-start(bf16[128,1,128]{2,0,1:T(8,128)(2,1)} %param.7) | copy-start | bytes 98308
  2.5 12.8 %copy-start.4 = (bf16[128,1,128]{2,0,1:T(8,128)(2,1)S(1)}, bf16[128,1,128]{2,0,1:T(8,128)(2,1)}, u32[]{:S(2)}) copy-start(bf16[128,1,128]{2,0,1:T(8,128)(2,1)} %param.8) | copy-start | bytes 98308
  2.5 21.8 %all-to-all-start = ((f32[64,3,128]{2,1,0:T(4,128)}), f32[64,3,128]{2,1,0:T(4,128)S(1)}, u32[]{:S(2)}, u32[]{:S(2)}) async-start(f32[64,3,128]{2,1,0:T(4,128)} %get-tuple-element.36), calls=%async_computation | async-start | bytes 262144 | tf_op jit(solution)/shard_map/states_out/all_to_all | solution.py:19
  15.3 10.2 %collective-permute-start = (bf16[256,128]{1,0:T(8,128)(2,1)S(1)}, bf16[256,128]{1,0:T(8,128)(2,1)S(1)}, u32[]{:S(2)}, u32[]{:S(2)}) collective-permute-start(bf16[256,128]{1,0:T(8,128)(2,1)S(1)} %pad_maximum_fusion), channel_id=1, source_target_pairs={{0,8},{8,16},{16,24},{24,32},{32,40},{40,48},{48,56},{56,64},{64,7... | collective-permute-start | bytes 196616 | tf_op jit(solution)/shard_map/ppermute | solution.py:289
  18.7 1.3 %copy-start.5 = (f32[16,128,64]{1,2,0:T(8,128)S(1)}, f32[16,128,64]{1,2,0:T(8,128)}, u32[]{:S(2)}) copy-start(f32[16,128,64]{1,2,0:T(8,128)} %param.10) | copy-start | bytes 1572868
  19.9 14.1 %copy-start = (bf16[16,128,128]{2,1,0:T(8,128)(2,1)}, bf16[16,128,128]{2,1,0:T(8,128)(2,1)S(1)}, u32[]{:S(2)}) copy-start(bf16[16,128,128]{2,1,0:T(8,128)(2,1)S(1)} %copy.9) | copy-start | bytes 1572868
  19.9 5.6 %copy-start.6 = (bf16[128,16,128]{2,1,0:T(8,128)(2,1)S(1)}, bf16[128,16,128]{2,1,0:T(8,128)(2,1)}, u32[]{:S(2)}) copy-start(bf16[128,16,128]{2,1,0:T(8,128)(2,1)} %param.9) | copy-start | bytes 1572868
  25.6 17.2 %all-to-all-start.1 = ((f32[64,3,128]{2,1,0:T(4,128)}), f32[64,3,128]{2,1,0:T(4,128)S(1)}, u32[]{:S(2)}, u32[]{:S(2)}) async-start(f32[64,3,128]{2,1,0:T(4,128)} %prefix.1), calls=%async_computation.1 | async-start | bytes 262144 | tf_op jit(solution)/shard_map/states_back/all_to_all | solution.py:19
  34.0 8.8 %copy-start.1 = (bf16[128,2048]{1,0:T(8,128)(2,1)S(1)}, bf16[128,2048]{1,0:T(8,128)(2,1)}, u32[]{:S(2)}) copy-start(bf16[128,2048]{1,0:T(8,128)(2,1)} %get-tuple-element.42.refs_0_.high_ref) | copy-start | bytes 1572868
  34.1 8.8 %copy-start.2 = (bf16[128,2048]{1,0:T(8,128)(2,1)S(1)}, bf16[128,2048]{1,0:T(8,128)(2,1)}, u32[]{:S(2)}) copy-start(bf16[128,2048]{1,0:T(8,128)(2,1)} %get-tuple-element.43.refs_1_.low_ref) | copy-start | bytes 1572868
  46.6 15.3 %all-to-all-start.2 = ((f32[64,3,128]{2,1,0:T(4,128)}), f32[64,3,128]{2,1,0:T(4,128)S(1)}, u32[]{:S(2)}, u32[]{:S(2)}) async-start(f32[64,3,128]{2,1,0:T(4,128)} %get-tuple-element.51), calls=%async_computation.2 | async-start | bytes 262144 | tf_op jit(solution)/shard_map/grads_out/all_to_all | solution.py:19
  55.7 17.5 %collective-permute-start.1 = (f32[8,64,128]{2,1,0:T(8,128)S(1)}, f32[8,64,128]{2,1,0:T(8,128)S(1)}, u32[]{:S(2)}, u32[]{:S(2)}) collective-permute-start(f32[8,64,128]{2,1,0:T(8,128)S(1)} %grad_q.1), channel_id=1, source_target_pairs={{0,8},{8,0},{16,24},{24,16},{32,40},{40,32},{48,56},{56,48},{64,72... | collective-permute-start | bytes 786440 | tf_op jit(solution)/shard_map/grad_q_swap/ppermute | solution.py:364
  63.1 16.3 %all-to-all-start.3 = ((f32[64,3,128]{2,1,0:T(4,128)}), f32[64,3,128]{2,1,0:T(4,128)S(1)}, u32[]{:S(2)}, u32[]{:S(2)}) async-start(f32[64,3,128]{2,1,0:T(4,128)} %get-tuple-element.57), calls=%async_computation.3 | async-start | bytes 262144 | tf_op jit(solution)/shard_map/grads_back/all_to_all | solution.py:19
  80.6 17.1 %all-to-all-start.4 = ((f32[320,2,128]{2,1,0:T(2,128)}), f32[320,2,128]{2,1,0:T(2,128)S(1)}, u32[]{:S(2)}, u32[]{:S(2)}) async-start(f32[320,2,128]{2,1,0:T(2,128)} %bitcast.10), calls=%async_computation.4 | async-start | bytes 655360 | tf_op jit(solution)/shard_map/maps_out/all_to_all | solution.py:19
  87.1 7.7 %collective-permute-start.2 = (f32[8,128]{1,0:T(8,128)S(1)}, f32[8,128]{1,0:T(8,128)S(1)}, u32[]{:S(2)}, u32[]{:S(2)}) collective-permute-start(f32[8,128]{1,0:T(8,128)S(1)} %get-tuple-element.62), channel_id=1, source_target_pairs={{0,2},{1,3},{2,0},{3,1},{4,6},{5,7},{6,4},{7,5},{8,10},{9,11},{10,... | collective-permute-start | bytes 12296 | tf_op jit(solution)/shard_map/loss_near/ppermute | solution.py:378
  98.7 22.3 %all-to-all-start.5 = ((f32[576,2,128]{2,1,0:T(2,128)}), f32[576,2,128]{2,1,0:T(2,128)S(1)}, u32[]{:S(2)}, u32[]{:S(2)}) async-start(f32[576,2,128]{2,1,0:T(2,128)} %bitcast.12), calls=%async_computation.5 | async-start | bytes 1179648 | tf_op jit(solution)/shard_map/maps_back/all_to_all | solution.py:19
  107.1 3.1 %collective-permute-start.3 = (f32[8,128]{1,0:T(8,128)S(1)}, f32[8,128]{1,0:T(8,128)S(1)}, u32[]{:S(2)}, u32[]{:S(2)}) collective-permute-start(f32[8,128]{1,0:T(8,128)S(1)} %add.14), channel_id=1, source_target_pairs={{0,1},{1,0},{2,3},{3,2},{4,5},{5,4},{6,7},{7,6},{8,9},{9,8},{10,11... | collective-permute-start | bytes 12296 | tf_op jit(solution)/shard_map/loss_far/ppermute | solution.py:378
  110.2 10.4 %collective-permute-start.4 = (f32[8,128]{1,0:T(8,128)S(1)}, f32[8,128]{1,0:T(8,128)S(1)}, u32[]{:S(2)}, u32[]{:S(2)}) collective-permute-start(f32[8,128]{1,0:T(8,128)S(1)} %add.15), channel_id=1, source_target_pairs={{0,6},{1,7},{2,4},{3,5},{4,2},{5,3},{6,0},{7,1},{8,14},{9,15},{10,... | collective-permute-start | bytes 12296 | tf_op jit(solution)/shard_map/loss_far/ppermute | solution.py:378

commit v9 on v8

--- a/solution.py
+++ b/solution.py
@@ -223,9 +223,10 @@
 
 def finish_kernel(parts_ref, query_ref, key_ref):
     heads = query_ref.shape[0]
+    first = pl.program_id(0) * (heads // 2)
     for h in range(heads):
-        query_ref[h] = parts_ref[:, h // 2, h % 2, :]
-    key_ref[...] = parts_ref[:, heads // 2, 0, :]
+        query_ref[h] = parts_ref[:, first + h // 2, h % 2, :]
+    key_ref[...] = parts_ref[:, parts_ref.shape[1] - 1, 0, :]
 
 
 def call(kernel, out_shape, cost, grid=None, in_specs=None, out_specs=None, scratch=()):
@@ -398,7 +399,12 @@
         loss = over_tp(over_tp(loss, 1), tp_count - 2)
     with jax.named_scope("maps_back"):
         grad_q, grad_k = call(
-            finish_kernel, (shape(heads, half, width), shape(half, width)), (mega, mega)
+            finish_kernel,
+            (shape(heads, half, width), shape(half, width)),
+            (mega, mega),
+            (STEPS,),
+            [whole(*maps_shape.shape)],
+            [by_head, whole(half, width)],
         )(exchange_maps(sums))
         grad_q = grad_q.transpose(0, 2, 1)
         grad_k = grad_k.T

time: 123 us -> 123 us (level)
  no operation moved by 1% of the time
where the time goes in v9:
time: 123 us; the launch traced here: 122 us
  starting transfers between devices  73.6 us (60%)
  waiting for transfers between devices  24.6 us (20%)
  Pallas kernels  21.1 us (17%)
  local copies, waits for them, and re-layouts  1.92 us (2%)
    all_to_all x6, starting transfers between devices, exchange(): return lax.all_to_all(parts, axis, 0, 0, tiled=True)  50 us
    all_to_all x6, waiting for transfers between devices, exchange(): return lax.all_to_all(parts, axis, 0, 0, tiled=True)  20.3 us
    ppermute x3, starting transfers between devices, over_tp(): lax.ppermute(loss, 'tp', [(i, i ^ bit) for i in range(tp_count)])  16.8 us
    pallas_call x2, Pallas kernels, grad_q_half(): pl.pallas_call(grad_q_kernel, out_shape=shape(heads // 2, half, width), g...  5.19 us
    ppermute x3, waiting for transfers between devices, over_tp(): lax.ppermute(loss, 'tp', [(i, i ^ bit) for i in range(tp_count)])  4.31 us
    pallas_call x1, Pallas kernels, on_device(): call(lambda *refs: student_kernel(2.0 / count_all, *refs), (parts_shape,...  3.76 us
    ppermute x1, starting transfers between devices, on_device(): lax.ppermute(jnp.concatenate([halo_keys, halo_values], axis=0), 'section'...  3.38 us
    ppermute x1, starting transfers between devices, on_device(): other = lax.ppermute(sent, 'section', [(i, i ^ 1) for i in range(count)])  3.38 us
  transfers between devices with their start and end apart: 11, of which 8 were waited for; matrix products, arithmetic and copies ran while one was open for 1% of the time, Pallas kernels for 10%

profile of v9, /device:TPU:6, one launch (start us, length us, event | category | flops | bytes accessed | tf_op | source)
XLA Modules:
  0.0 122.1 jit_solution(13924368698382872780)
XLA Ops:
  0.6 1.9 %own_state.1 = (f32[64,3,128]{2,1,0:T(4,128)}, f32[128,128]{1,0:T(8,128)S(1)}) custom-call(bf16[128,128]{1,0:T(8,128)(2,1)} %bitcast.26, bf16[128,128]{1,0:T(8,128)(2,1)} %bitcast.30, f32[1,64,128]{2,1,0:T(8,128)} %bitcast.38), custom_call_target="tpu_custom_call" | custom-call | flops 31457280 | bytes 524288 | tf_op jit(solution)/shard_map/own_state/pallas_call | solution.py:284
  2.5 0.0 copy-start.3
  2.5 0.0 copy-start.4
  2.5 12.7 %all-to-all-start = ((f32[64,3,128]{2,1,0:T(4,128)}), f32[64,3,128]{2,1,0:T(4,128)S(1)}, u32[]{:S(2)}, u32[]{:S(2)}) async-start(f32[64,3,128]{2,1,0:T(4,128)} %get-tuple-element.36), calls=%async_computation | async-start | bytes 262144 | tf_op jit(solution)/shard_map/states_out/all_to_all | solution.py:19
  15.2 0.0 copy-done.3
  15.3 0.0 copy-done.4
  15.3 3.4 %collective-permute-start = (bf16[256,128]{1,0:T(8,128)(2,1)S(1)}, bf16[256,128]{1,0:T(8,128)(2,1)S(1)}, u32[]{:S(2)}, u32[]{:S(2)}) collective-permute-start(bf16[256,128]{1,0:T(8,128)(2,1)S(1)} %pad_maximum_fusion), channel_id=1, source_target_pairs={{0,8},{8,16},{16,24},{24,32},{32,40},{40,48},{48,56},{56,64},{64,7... | collective-permute-start | bytes 196616 | tf_op jit(solution)/shard_map/ppermute | solution.py:290
  18.7 0.0 copy-start.5
  18.7 1.2 %copy.9 = bf16[16,128,128]{2,1,0:T(8,128)(2,1)S(1)} copy(bf16[16,128,128]{2,0,1:T(8,128)(2,1)} %bitcast.35) | data formatting | bytes 1048576 | tf_op jit(solution)/shard_map/query_feats/transpose | solution.py:296
  19.9 0.0 copy-start
  19.9 0.0 copy-done.5
  19.9 0.0 copy-start.6
  19.9 2.4 %query_feats.1 = (bf16[128,2048]{1,0:T(8,128)(2,1)}, bf16[128,2048]{1,0:T(8,128)(2,1)}) custom-call(bf16[2048,128]{1,0:T(8,128)(2,1)S(1)} %bitcast.19, f32[16,64,128]{2,1,0:T(8,128)S(1)} %bitcast.34), custom_call_target="tpu_custom_call" | custom-call | flops 629145600 | bytes 3145728 | tf_op jit(solution)/shard_map/query_feats/pallas_call | solution.py:298
  22.3 2.0 %all-to-all-done.refs_0_ = f32[64,3,128]{2,1,0:T(4,128)S(1)} async-done(((f32[64,3,128]{2,1,0:T(4,128)}), f32[64,3,128]{2,1,0:T(4,128)S(1)}, u32[]{:S(2)}, u32[]{:S(2)}) %all-to-all-start) | async-done | bytes 98336 | tf_op jit(solution)/shard_map/states_out/all_to_all | solution.py:19
  24.3 1.2 prefix.1
  25.5 0.0 collective-permute-done.halo_ref
  25.5 0.0 copy-done.6
  25.5 0.1 copy.10
  25.6 8.4 %all-to-all-start.1 = ((f32[64,3,128]{2,1,0:T(4,128)}), f32[64,3,128]{2,1,0:T(4,128)S(1)}, u32[]{:S(2)}, u32[]{:S(2)}) async-start(f32[64,3,128]{2,1,0:T(4,128)} %prefix.1), calls=%async_computation.1 | async-start | bytes 262144 | tf_op jit(solution)/shard_map/states_back/all_to_all | solution.py:19
  34.0 0.0 copy-done
  34.0 0.0 copy-start.1
  34.1 0.0 copy-start.2
  34.1 2.3 %window.1 = (f32[128,2048]{1,0:T(8,128)}, f32[1,2048]{1,0:T(1,128)}, bf16[128,2048]{1,0:T(8,128)(2,1)}) custom-call(bf16[2048,128]{1,0:T(8,128)(2,1)S(1)} %bitcast.20, bf16[128,128]{1,0:T(8,128)(2,1)S(1)} %bitcast.28, bf16[128,128]{1,0:T(8,128)(2,1)S(1)} %bitcast.32, bf16[256,128]{1,0:T(8,128)(2,1)S(1)} %collective-permute-done.halo_ref, ...), custom_call_target="tpu_custom_call" | custom-call | flops 2097152000 | bytes 8388608 | tf_op jit(solution)/shard_map/window/pallas_call | solution.py:317
  36.3 6.5 %all-to-all-done.1.refs_5_.state_ref = f32[64,3,128]{2,1,0:T(4,128)S(1)} async-done(((f32[64,3,128]{2,1,0:T(4,128)}), f32[64,3,128]{2,1,0:T(4,128)S(1)}, u32[]{:S(2)}, u32[]{:S(2)}) %all-to-all-start.1) | async-done | bytes 98336 | tf_op jit(solution)/shard_map/states_back/all_to_all | solution.py:19
  42.8 0.0 copy-done.1
  42.8 0.0 copy-done.2
  42.8 3.8 %student.1 = (f32[64,3,128]{2,1,0:T(4,128)}, bf16[128,2048]{1,0:T(8,128)(2,1)}, bf16[128,2048]{1,0:T(8,128)(2,1)}, f32[1,2048]{1,0:T(1,128)}) custom-call(bf16[128,2048]{1,0:T(8,128)(2,1)S(1)} %copy-done.1, bf16[128,2048]{1,0:T(8,128)(2,1)S(1)} %copy-done.2, f32[128,2048]{1,0:T(8,128)} %get-tuple-element.47.refs_2_, f32[1,2048]{1,0:T(1,128)} %get-tuple-element.48.refs_3_, ...), custom_call_target="tpu_custom_call" | custom-call | flops 419430400 | bytes 4194304 | tf_op jit(solution)/shard_map/student/pallas_call | solution.py:327
  46.6 6.5 %all-to-all-start.2 = ((f32[64,3,128]{2,1,0:T(4,128)}), f32[64,3,128]{2,1,0:T(4,128)S(1)}, u32[]{:S(2)}, u32[]{:S(2)}) async-start(f32[64,3,128]{2,1,0:T(4,128)} %get-tuple-element.51), calls=%async_computation.2 | async-start | bytes 262144 | tf_op jit(solution)/shard_map/grads_out/all_to_all | solution.py:19
  53.1 2.6 %grad_q.1 = f32[8,64,128]{2,1,0:T(8,128)S(1)} custom-call(s32[1]{0:T(128)} %bitcast.8._, bf16[128,2048]{1,0:T(8,128)(2,1)} %get-tuple-element.42.refs_0_.high_ref, bf16[128,2048]{1,0:T(8,128)(2,1)} %get-tuple-element.43.refs_1_.low_ref, bf16[128,2048]{1,0:T(8,128)(2,1)} %get-tuple-element.52.grad_high_ref, bf16[128,2048]{1,0:T(8,128)(2,1)} %get-tuple-element.53.grad_low_ref, ...), custom_call_target="tpu_custom_call" | custom-call | flops 524288000 | bytes 2097152 | tf_op jit(solution)/shard_map/grad_q/pallas_call | solution.py:341
  55.7 3.4 %collective-permute-start.1 = (f32[8,64,128]{2,1,0:T(8,128)S(1)}, f32[8,64,128]{2,1,0:T(8,128)S(1)}, u32[]{:S(2)}, u32[]{:S(2)}) collective-permute-start(f32[8,64,128]{2,1,0:T(8,128)S(1)} %grad_q.1), channel_id=1, source_target_pairs={{0,8},{8,0},{16,24},{24,16},{32,40},{40,32},{48,56},{56,48},{64,72... | collective-permute-start | bytes 786440 | tf_op jit(solution)/shard_map/grad_q_swap/ppermute | solution.py:365
  59.1 2.8 %all-to-all-done.2.refs_0_ = f32[64,3,128]{2,1,0:T(4,128)S(1)} async-done(((f32[64,3,128]{2,1,0:T(4,128)}), f32[64,3,128]{2,1,0:T(4,128)S(1)}, u32[]{:S(2)}, u32[]{:S(2)}) %all-to-all-start.2) | async-done | bytes 98336 | tf_op jit(solution)/shard_map/grads_out/all_to_all | solution.py:19
  61.9 1.2 suffix.1
  63.1 7.5 %all-to-all-start.3 = ((f32[64,3,128]{2,1,0:T(4,128)}), f32[64,3,128]{2,1,0:T(4,128)S(1)}, u32[]{:S(2)}, u32[]{:S(2)}) async-start(f32[64,3,128]{2,1,0:T(4,128)} %get-tuple-element.57), calls=%async_computation.3 | async-start | bytes 262144 | tf_op jit(solution)/shard_map/grads_back/all_to_all | solution.py:19
  70.6 2.6 %grad_q_kept.1.query_ref = f32[8,64,128]{2,1,0:T(8,128)S(1)} custom-call(s32[1]{0:T(128)} %bitcast.9._, bf16[128,2048]{1,0:T(8,128)(2,1)} %get-tuple-element.42.refs_0_.high_ref, bf16[128,2048]{1,0:T(8,128)(2,1)} %get-tuple-element.43.refs_1_.low_ref, bf16[128,2048]{1,0:T(8,128)(2,1)} %get-tuple-element.52.grad_high_ref, ...), custom_call_target="tpu_custom_call" | custom-call | flops 524288000 | bytes 2097152 | tf_op jit(solution)/shard_map/grad_q_kept/pallas_call | solution.py:341
  73.2 0.0 collective-permute-done.1.other_ref
  73.2 6.2 %all-to-all-done.3.state_ref = f32[64,3,128]{2,1,0:T(4,128)S(1)} async-done(((f32[64,3,128]{2,1,0:T(4,128)}), f32[64,3,128]{2,1,0:T(4,128)S(1)}, u32[]{:S(2)}, u32[]{:S(2)}) %all-to-all-start.3) | async-done | bytes 98336 | tf_op jit(solution)/shard_map/grads_back/all_to_all | solution.py:19
  79.4 1.2 grad_k.1
  80.6 6.5 %all-to-all-start.4 = ((f32[320,2,128]{2,1,0:T(2,128)}), f32[320,2,128]{2,1,0:T(2,128)S(1)}, u32[]{:S(2)}, u32[]{:S(2)}) async-start(f32[320,2,128]{2,1,0:T(2,128)} %bitcast.10), calls=%async_computation.4 | async-start | bytes 655360 | tf_op jit(solution)/shard_map/maps_out/all_to_all | solution.py:19
  87.1 6.1 %collective-permute-start.2 = (f32[8,128]{1,0:T(8,128)S(1)}, f32[8,128]{1,0:T(8,128)S(1)}, u32[]{:S(2)}, u32[]{:S(2)}) collective-permute-start(f32[8,128]{1,0:T(8,128)S(1)} %get-tuple-element.62), channel_id=1, source_target_pairs={{0,2},{1,3},{2,0},{3,1},{4,6},{5,7},{6,4},{7,5},{8,10},{9,11},{10,... | collective-permute-start | bytes 12296 | tf_op jit(solution)/shard_map/loss_near/ppermute | solution.py:379
  93.2 1.6 %collective-permute-done.2 = f32[8,128]{1,0:T(8,128)S(1)} collective-permute-done((f32[8,128]{1,0:T(8,128)S(1)}, f32[8,128]{1,0:T(8,128)S(1)}, u32[]{:S(2)}, u32[]{:S(2)}) %collective-permute-start.2) | collective-permute-done | bytes 4128 | tf_op jit(solution)/shard_map/loss_near/ppermute | solution.py:379
  94.8 2.8 %all-to-all-done.4 = f32[320,2,128]{2,1,0:T(2,128)S(1)} async-done(((f32[320,2,128]{2,1,0:T(2,128)}), f32[320,2,128]{2,1,0:T(2,128)S(1)}, u32[]{:S(2)}, u32[]{:S(2)}) %all-to-all-start.4) | async-done | bytes 327712 | tf_op jit(solution)/shard_map/maps_out/all_to_all | solution.py:19
  97.7 1.1 maps_out.1
  98.7 8.4 %all-to-all-start.5 = ((f32[576,2,128]{2,1,0:T(2,128)}), f32[576,2,128]{2,1,0:T(2,128)S(1)}, u32[]{:S(2)}, u32[]{:S(2)}) async-start(f32[576,2,128]{2,1,0:T(2,128)} %bitcast.12), calls=%async_computation.5 | async-start | bytes 1179648 | tf_op jit(solution)/shard_map/maps_back/all_to_all | solution.py:19
  107.1 1.9 %collective-permute-start.3 = (f32[8,128]{1,0:T(8,128)S(1)}, f32[8,128]{1,0:T(8,128)S(1)}, u32[]{:S(2)}, u32[]{:S(2)}) collective-permute-start(f32[8,128]{1,0:T(8,128)S(1)} %add.14), channel_id=1, source_target_pairs={{0,1},{1,0},{2,3},{3,2},{4,5},{5,4},{6,7},{7,6},{8,9},{9,8},{10,11... | collective-permute-start | bytes 12296 | tf_op jit(solution)/shard_map/loss_far/ppermute | solution.py:379
  109.0 1.1 collective-permute-done.3
  110.2 8.8 %collective-permute-start.4 = (f32[8,128]{1,0:T(8,128)S(1)}, f32[8,128]{1,0:T(8,128)S(1)}, u32[]{:S(2)}, u32[]{:S(2)}) collective-permute-start(f32[8,128]{1,0:T(8,128)S(1)} %add.15), channel_id=1, source_target_pairs={{0,6},{1,7},{2,4},{3,5},{4,2},{5,3},{6,0},{7,1},{8,14},{9,15},{10,... | collective-permute-start | bytes 12296 | tf_op jit(solution)/shard_map/loss_far/ppermute | solution.py:379
  119.0 1.6 %collective-permute-done.4 = f32[8,128]{1,0:T(8,128)S(1)} collective-permute-done((f32[8,128]{1,0:T(8,128)S(1)}, f32[8,128]{1,0:T(8,128)S(1)}, u32[]{:S(2)}, u32[]{:S(2)}) %collective-permute-start.4) | collective-permute-done | bytes 4128 | tf_op jit(solution)/shard_map/loss_far/ppermute | solution.py:379
  120.6 0.5 slice.3
  121.1 0.0 all-to-all-done.5
  121.1 1.0 maps_back.1
  (4 shorter events, 0.0 us)
Async XLA Ops:
  2.5 12.8 %copy-start.3 = (bf16[128,1,128]{2,0,1:T(8,128)(2,1)S(1)}, bf16[128,1,128]{2,0,1:T(8,128)(2,1)}, u32[]{:S(2)}) copy-start(bf16[128,1,128]{2,0,1:T(8,128)(2,1)} %param.7) | copy-start | bytes 98308
  2.5 12.8 %copy-start.4 = (bf16[128,1,128]{2,0,1:T(8,128)(2,1)S(1)}, bf16[128,1,128]{2,0,1:T(8,128)(2,1)}, u32[]{:S(2)}) copy-start(bf16[128,1,128]{2,0,1:T(8,128)(2,1)} %param.8) | copy-start | bytes 98308
  2.5 21.8 %all-to-all-start = ((f32[64,3,128]{2,1,0:T(4,128)}), f32[64,3,128]{2,1,0:T(4,128)S(1)}, u32[]{:S(2)}, u32[]{:S(2)}) async-start(f32[64,3,128]{2,1,0:T(4,128)} %get-tuple-element.36), calls=%async_computation | async-start | bytes 262144 | tf_op jit(solution)/shard_map/states_out/all_to_all | solution.py:19
  15.3 10.2 %collective-permute-start = (bf16[256,128]{1,0:T(8,128)(2,1)S(1)}, bf16[256,128]{1,0:T(8,128)(2,1)S(1)}, u32[]{:S(2)}, u32[]{:S(2)}) collective-permute-start(bf16[256,128]{1,0:T(8,128)(2,1)S(1)} %pad_maximum_fusion), channel_id=1, source_target_pairs={{0,8},{8,16},{16,24},{24,32},{32,40},{40,48},{48,56},{56,64},{64,7... | collective-permute-start | bytes 196616 | tf_op jit(solution)/shard_map/ppermute | solution.py:290
  18.7 1.3 %copy-start.5 = (f32[16,128,64]{1,2,0:T(8,128)S(1)}, f32[16,128,64]{1,2,0:T(8,128)}, u32[]{:S(2)}) copy-start(f32[16,128,64]{1,2,0:T(8,128)} %param.10) | copy-start | bytes 1572868
  19.9 14.1 %copy-start = (bf16[16,128,128]{2,1,0:T(8,128)(2,1)}, bf16[16,128,128]{2,1,0:T(8,128)(2,1)S(1)}, u32[]{:S(2)}) copy-start(bf16[16,128,128]{2,1,0:T(8,128)(2,1)S(1)} %copy.9) | copy-start | bytes 1572868
  19.9 5.6 %copy-start.6 = (bf16[128,16,128]{2,1,0:T(8,128)(2,1)S(1)}, bf16[128,16,128]{2,1,0:T(8,128)(2,1)}, u32[]{:S(2)}) copy-start(bf16[128,16,128]{2,1,0:T(8,128)(2,1)} %param.9) | copy-start | bytes 1572868
  25.6 17.2 %all-to-all-start.1 = ((f32[64,3,128]{2,1,0:T(4,128)}), f32[64,3,128]{2,1,0:T(4,128)S(1)}, u32[]{:S(2)}, u32[]{:S(2)}) async-start(f32[64,3,128]{2,1,0:T(4,128)} %prefix.1), calls=%async_computation.1 | async-start | bytes 262144 | tf_op jit(solution)/shard_map/states_back/all_to_all | solution.py:19
  34.0 8.8 %copy-start.1 = (bf16[128,2048]{1,0:T(8,128)(2,1)S(1)}, bf16[128,2048]{1,0:T(8,128)(2,1)}, u32[]{:S(2)}) copy-start(bf16[128,2048]{1,0:T(8,128)(2,1)} %get-tuple-element.42.refs_0_.high_ref) | copy-start | bytes 1572868
  34.1 8.8 %copy-start.2 = (bf16[128,2048]{1,0:T(8,128)(2,1)S(1)}, bf16[128,2048]{1,0:T(8,128)(2,1)}, u32[]{:S(2)}) copy-start(bf16[128,2048]{1,0:T(8,128)(2,1)} %get-tuple-element.43.refs_1_.low_ref) | copy-start | bytes 1572868
  46.6 15.3 %all-to-all-start.2 = ((f32[64,3,128]{2,1,0:T(4,128)}), f32[64,3,128]{2,1,0:T(4,128)S(1)}, u32[]{:S(2)}, u32[]{:S(2)}) async-start(f32[64,3,128]{2,1,0:T(4,128)} %get-tuple-element.51), calls=%async_computation.2 | async-start | bytes 262144 | tf_op jit(solution)/shard_map/grads_out/all_to_all | solution.py:19
  55.7 17.5 %collective-permute-start.1 = (f32[8,64,128]{2,1,0:T(8,128)S(1)}, f32[8,64,128]{2,1,0:T(8,128)S(1)}, u32[]{:S(2)}, u32[]{:S(2)}) collective-permute-start(f32[8,64,128]{2,1,0:T(8,128)S(1)} %grad_q.1), channel_id=1, source_target_pairs={{0,8},{8,0},{16,24},{24,16},{32,40},{40,32},{48,56},{56,48},{64,72... | collective-permute-start | bytes 786440 | tf_op jit(solution)/shard_map/grad_q_swap/ppermute | solution.py:365
  63.1 16.3 %all-to-all-start.3 = ((f32[64,3,128]{2,1,0:T(4,128)}), f32[64,3,128]{2,1,0:T(4,128)S(1)}, u32[]{:S(2)}, u32[]{:S(2)}) async-start(f32[64,3,128]{2,1,0:T(4,128)} %get-tuple-element.57), calls=%async_computation.3 | async-start | bytes 262144 | tf_op jit(solution)/shard_map/grads_back/all_to_all | solution.py:19
  80.6 17.1 %all-to-all-start.4 = ((f32[320,2,128]{2,1,0:T(2,128)}), f32[320,2,128]{2,1,0:T(2,128)S(1)}, u32[]{:S(2)}, u32[]{:S(2)}) async-start(f32[320,2,128]{2,1,0:T(2,128)} %bitcast.10), calls=%async_computation.4 | async-start | bytes 655360 | tf_op jit(solution)/shard_map/maps_out/all_to_all | solution.py:19
  87.1 7.7 %collective-permute-start.2 = (f32[8,128]{1,0:T(8,128)S(1)}, f32[8,128]{1,0:T(8,128)S(1)}, u32[]{:S(2)}, u32[]{:S(2)}) collective-permute-start(f32[8,128]{1,0:T(8,128)S(1)} %get-tuple-element.62), channel_id=1, source_target_pairs={{0,2},{1,3},{2,0},{3,1},{4,6},{5,7},{6,4},{7,5},{8,10},{9,11},{10,... | collective-permute-start | bytes 12296 | tf_op jit(solution)/shard_map/loss_near/ppermute | solution.py:379
  98.7 22.3 %all-to-all-start.5 = ((f32[576,2,128]{2,1,0:T(2,128)}), f32[576,2,128]{2,1,0:T(2,128)S(1)}, u32[]{:S(2)}, u32[]{:S(2)}) async-start(f32[576,2,128]{2,1,0:T(2,128)} %bitcast.12), calls=%async_computation.5 | async-start | bytes 1179648 | tf_op jit(solution)/shard_map/maps_back/all_to_all | solution.py:19
  107.1 3.1 %collective-permute-start.3 = (f32[8,128]{1,0:T(8,128)S(1)}, f32[8,128]{1,0:T(8,128)S(1)}, u32[]{:S(2)}, u32[]{:S(2)}) collective-permute-start(f32[8,128]{1,0:T(8,128)S(1)} %add.14), channel_id=1, source_target_pairs={{0,1},{1,0},{2,3},{3,2},{4,5},{5,4},{6,7},{7,6},{8,9},{9,8},{10,11... | collective-permute-start | bytes 12296 | tf_op jit(solution)/shard_map/loss_far/ppermute | solution.py:379
  110.2 10.4 %collective-permute-start.4 = (f32[8,128]{1,0:T(8,128)S(1)}, f32[8,128]{1,0:T(8,128)S(1)}, u32[]{:S(2)}, u32[]{:S(2)}) collective-permute-start(f32[8,128]{1,0:T(8,128)S(1)} %add.15), channel_id=1, source_target_pairs={{0,6},{1,7},{2,4},{3,5},{4,2},{5,3},{6,0},{7,1},{8,14},{9,15},{10,... | collective-permute-start | bytes 12296 | tf_op jit(solution)/shard_map/loss_far/ppermute | solution.py:379
